TPU v7x, 128 devices: a whole 4x4x4 slice. The times are simulated.
128 devices in a mesh: section: 2 (over y_lo), dp: 16 (over z, x), tensor: 4 (over y_hi, core).
Axes of the slice: x: 4, y: 4 (y_hi: 2, y_lo: 2; y = y_hi * 2 + y_lo), z: 4, core: 2. Of those that a mesh axis runs over, the one named last changes fastest.
Arguments:
- inputs: bfloat16 [2, 16, 128, 1024], P(None, 'dp'), may hold values from -6 to 6
- cotangent: bfloat16 [2, 16, 128, 1024], P(None, 'dp'), may hold values from -6 to 6
- norm_gain1: bfloat16 [2, 1024], P('section'), may hold values from 0.099609375 to 1.8984375
- w_query: bfloat16 [2, 1024, 1024], P('section', None, 'tensor'), may hold values from -0.1875 to 0.1875
- w_key: bfloat16 [2, 1024, 1024], P('section', None, 'tensor'), may hold values from -0.1875 to 0.1875
- w_value: bfloat16 [2, 1024, 2048], P('section', None, 'tensor'), may hold values from -0.1875 to 0.1875
- conv_query: bfloat16 [2, 4, 1024], P('section', None, 'tensor'), may hold values from -3 to 3
- conv_key: bfloat16 [2, 4, 1024], P('section', None, 'tensor'), may hold values from -3 to 3
- conv_value: bfloat16 [2, 4, 2048], P('section', None, 'tensor'), may hold values from -3 to 3
- w_beta: bfloat16 [2, 1024, 8], P('section', None, 'tensor'), may hold values from -0.1875 to 0.1875
- w_decay: bfloat16 [2, 1024, 8], P('section', None, 'tensor'), may hold values from -0.1875 to 0.1875
- log_rate: float32 [2, 8], P('section', 'tensor'), may hold values from -4.5 to -1
- step_bias: float32 [2, 8], P('section', 'tensor'), may hold values from -1 to 1
- out_gain: bfloat16 [2, 2048], P('section', 'tensor'), may hold values from 0.099609375 to 1.8984375
- w_gate_out: bfloat16 [2, 1024, 2048], P('section', None, 'tensor'), may hold values from -0.1875 to 0.1875
- w_out: bfloat16 [2, 2048, 1024], P('section', 'tensor'), may hold values from -0.1875 to 0.1875
- norm_gain2: bfloat16 [2, 1024], P('section'), may hold values from 0.099609375 to 1.8984375
- w_ffn_gate: bfloat16 [2, 1024, 2816], P('section', None, 'tensor'), may hold values from -0.1875 to 0.1875
- w_ffn_up: bfloat16 [2, 1024, 2816], P('section', None, 'tensor'), may hold values from -0.1875 to 0.1875
- w_ffn_down: bfloat16 [2, 2816, 1024], P('section', 'tensor'), may hold values from -0.15625 to 0.15625
Outputs:
- hidden_out: bfloat16 [2, 2, 16, 128, 1024], P('section', None, 'dp')
- input_grad: bfloat16 [2, 2, 16, 128, 1024], P('section', None, 'dp')
- grad_norm_gain1: float32 [2, 1024], P('section')
- grad_query: float32 [2, 1024, 1024], P('section', 'dp', 'tensor')
- grad_key: float32 [2, 1024, 1024], P('section', 'dp', 'tensor')
- grad_value: float32 [2, 1024, 2048], P('section', 'dp', 'tensor')
- grad_conv_query: float32 [2, 4, 1024], P('section', None, 'tensor')
- grad_conv_key: float32 [2, 4, 1024], P('section', None, 'tensor')
- grad_conv_value: float32 [2, 4, 2048], P('section', None, 'tensor')
- grad_beta: float32 [2, 1024, 8], P('section', 'dp', 'tensor')
- grad_decay: float32 [2, 1024, 8], P('section', 'dp', 'tensor')
- grad_log_rate: float32 [2, 8], P('section', 'tensor')
- grad_step_bias: float32 [2, 8], P('section', 'tensor')
- grad_out_gain: float32 [2, 2048], P('section', 'tensor')
- grad_gate_out: float32 [2, 1024, 2048], P('section', 'dp', 'tensor')
- grad_out: float32 [2, 2048, 1024], P('section', 'tensor', 'dp')
- grad_norm_gain2: float32 [2, 1024], P('section')
- grad_ffn_gate: float32 [2, 1024, 2816], P('section', 'dp', 'tensor')
- grad_ffn_up: float32 [2, 1024, 2816], P('section', 'dp', 'tensor')
- grad_ffn_down: float32 [2, 2816, 1024], P('section', 'tensor', 'dp')
All inputs are finite; a program needn't handle non-finite values.
Results may differ from a plain program's by a relative error of at most 0.033.
Values may be sent and summed in bfloat16 or wider, within the bound.
A program may use at most 128 MiB of HBM per device.

v0:
```python
import jax
import jax.numpy as jnp
from jax import lax
from jax.sharding import PartitionSpec as P

GROUP = 64


def from_behind(value, axis, steps):
    count = lax.axis_size(axis)
    initial, last = (max(0, -steps), min(count, count - steps))
    return lax.ppermute(value, axis, [(source, source + steps) for source in range(initial, last)])


def rms_norm(activations, gain_vec):
    return (
        activations
        * lax.rsqrt(jnp.mean(activations * activations, axis=-1, keepdims=True) + 1e-06)
        * gain_vec
    )


def short_conv(signal, kernel):
    kernel_len = kernel.shape[0]
    seq_len = signal.shape[1]
    padded = jnp.pad(signal, ((0, 0), (kernel_len - 1, 0), (0, 0)))
    summed = padded[:, 0:seq_len, :] * kernel[0]
    for offset in range(1, kernel_len):
        summed = summed + padded[:, offset : offset + seq_len, :] * kernel[offset]
    return jax.nn.silu(summed)


def unit_rows(vectors):
    return vectors * lax.rsqrt(jnp.sum(vectors * vectors, axis=-1, keepdims=True) + 1e-06)


def block_step(state, block):
    queries, key_vecs, values, beta_gates, log_decay = block
    block_len = log_decay.shape[-1]
    cumulative = jnp.cumsum(log_decay, axis=-1)
    row_ids = lax.broadcasted_iota(jnp.int32, (block_len, block_len), 0)
    col_ids = lax.broadcasted_iota(jnp.int32, (block_len, block_len), 1)
    strict = row_ids > col_ids
    within = row_ids >= col_ids
    log_gaps = cumulative[..., :, None] - cumulative[..., None, :]
    lower_decay = jnp.where(strict, jnp.exp(jnp.where(strict, log_gaps, 0.0)), 0.0)
    full_decay = jnp.where(within, jnp.exp(jnp.where(within, log_gaps, 0.0)), 0.0)
    key_key = jnp.einsum("bhid,bhjd->bhij", key_vecs, key_vecs, precision=lax.Precision.HIGHEST)
    system = (
        jnp.eye(block_len, dtype=jnp.float32) + beta_gates[..., :, None] * key_key * lower_decay
    )
    stacked_rhs = jnp.concatenate(
        [beta_gates[..., None] * values, (beta_gates * jnp.exp(cumulative))[..., None] * key_vecs],
        axis=-1,
    )
    solved = lax.linalg.triangular_solve(system, stacked_rhs, left_side=True, lower=True)
    value_width = values.shape[-1]
    fresh = solved[..., :value_width] - jnp.einsum(
        "bhcd,bhde->bhce", solved[..., value_width:], state, precision=lax.Precision.HIGHEST
    )
    scores = (
        jnp.einsum("bhid,bhjd->bhij", queries, key_vecs, precision=lax.Precision.HIGHEST)
        * full_decay
    )
    output = jnp.exp(cumulative)[..., None] * jnp.einsum(
        "bhcd,bhde->bhce", queries, state, precision=lax.Precision.HIGHEST
    )
    output = output + jnp.einsum("bhij,bhje->bhie", scores, fresh, precision=lax.Precision.HIGHEST)
    final_log = cumulative[..., -1:]
    carried = jnp.exp(final_log)[..., None] * state
    carried = carried + jnp.einsum(
        "bhcd,bhce->bhde",
        key_vecs * jnp.exp(final_log - cumulative)[..., None],
        fresh,
        precision=lax.Precision.HIGHEST,
    )
    return (carried, output)


def delta_rule(queries, key_vecs, values, beta_gates, log_decay):
    batch_size, seq_len, head_count, key_width = queries.shape
    value_width = values.shape[-1]
    block_count = seq_len // GROUP

    def blocks(array_in):
        array_in = array_in.reshape(
            (batch_size, block_count, GROUP, head_count) + array_in.shape[3:]
        )
        return jnp.moveaxis(array_in, (1, 3), (0, 2))

    start_state = jnp.zeros((batch_size, head_count, key_width, value_width), jnp.float32)
    pieces = (
        blocks(queries),
        blocks(key_vecs),
        blocks(values),
        blocks(beta_gates),
        blocks(log_decay),
    )
    unused, outputs = lax.scan(jax.checkpoint(block_step), start_state, pieces)
    outputs = jnp.moveaxis(outputs, (0, 2), (1, 3))
    return outputs.reshape(batch_size, seq_len, head_count, value_width)


def mixer_core(
    proj_query,
    proj_key,
    proj_value,
    proj_beta,
    proj_decay,
    proj_gate,
    conv_query,
    conv_key,
    conv_value,
    log_rate,
    step_bias,
    out_gain,
):
    head_count = log_rate.shape[0]
    batch_size, seq_len, unused = proj_query.shape
    queries = short_conv(proj_query, conv_query).reshape(batch_size, seq_len, head_count, -1)
    key_vecs = short_conv(proj_key, conv_key).reshape(batch_size, seq_len, head_count, -1)
    values = short_conv(proj_value, conv_value).reshape(batch_size, seq_len, head_count, -1)
    queries = unit_rows(queries) * queries.shape[-1] ** (-0.5)
    key_vecs = unit_rows(key_vecs)
    beta_gates = jax.nn.sigmoid(proj_beta)
    log_decay = -jnp.exp(log_rate) * jax.nn.softplus(proj_decay + step_bias)
    mixed = delta_rule(queries, key_vecs, values, beta_gates, log_decay)
    mixed = (
        mixed
        * lax.rsqrt(jnp.mean(mixed * mixed, axis=-1, keepdims=True) + 1e-05)
        * out_gain.reshape(head_count, -1)
    )
    gate_pre = proj_gate.reshape(batch_size, seq_len, head_count, -1)
    return (mixed * jax.nn.silu(gate_pre)).reshape(batch_size, seq_len, -1)


def matmul_low(left, right):
    return jnp.einsum("btd,df->btf", left, right, preferred_element_type=jnp.float32)


def matmul_back(grad_low, weight):
    return jnp.einsum("btf,df->btd", grad_low, weight, preferred_element_type=jnp.float32)


def split_parts(grad_full):
    upper = grad_full.astype(jnp.bfloat16)
    lower = (grad_full - upper.astype(jnp.float32)).astype(jnp.bfloat16)
    return (upper, lower)


def matmul_back_split(grad_full, weight):
    upper, lower = split_parts(grad_full)
    return matmul_back(upper, weight) + matmul_back(lower, weight)


def token_sum(left, right):
    return jnp.einsum("btd,btf->df", left, right, preferred_element_type=jnp.float32)


def token_sum_split(left, grad_full):
    upper, lower = split_parts(grad_full)
    return token_sum(left, upper) + token_sum(left, lower)


def mixer_inputs(normed, weights):
    source = normed.astype(jnp.bfloat16)
    projections = tuple((matmul_low(source, weights[i]) for i in (1, 2, 3, 7, 8, 12)))
    return (source, projections)


def core_params(weights):
    return tuple((weights[i].astype(jnp.float32) for i in (4, 5, 6, 9, 10, 11)))


def forward_layer(current, weights):
    normed = rms_norm(current, weights[0].astype(jnp.float32))
    source, projections = mixer_inputs(normed, weights)
    mixed = mixer_core(*projections, *core_params(weights)).astype(jnp.bfloat16)
    middle = current + lax.psum(matmul_low(mixed, weights[13]), "tensor")
    second = rms_norm(middle, weights[14].astype(jnp.float32)).astype(jnp.bfloat16)
    gate_pre = matmul_low(second, weights[15])
    up_pre = matmul_low(second, weights[16])
    hidden = (jax.nn.silu(gate_pre) * up_pre).astype(jnp.bfloat16)
    result = middle + lax.psum(matmul_low(hidden, weights[17]), "tensor")
    return (middle, result)


def backward_inputs(current, middle, upstream, weights):
    gain_one = weights[0].astype(jnp.float32)
    gain_two = weights[14].astype(jnp.float32)
    normed_mid, pull_mid = jax.vjp(rms_norm, middle, gain_two)
    second = normed_mid.astype(jnp.bfloat16)
    gate_pre = matmul_low(second, weights[15])
    up_pre = matmul_low(second, weights[16])
    sigma = jax.nn.sigmoid(gate_pre)
    silu_gate = gate_pre * sigma
    hidden = (silu_gate * up_pre).astype(jnp.bfloat16)
    d_hidden = matmul_back_split(upstream, weights[17])
    d_gate = (d_hidden * up_pre * (sigma * (1.0 + gate_pre * (1.0 - sigma)))).astype(jnp.bfloat16)
    d_up = (d_hidden * silu_gate).astype(jnp.bfloat16)
    d_second = matmul_back(d_gate, weights[15]) + matmul_back(d_up, weights[16])
    d_normed_mid = lax.psum(d_second.astype(jnp.bfloat16), "tensor").astype(jnp.float32)
    d_mid, d_gain_two = pull_mid(d_normed_mid)
    d_middle = upstream + d_mid
    normed, pull_in = jax.vjp(rms_norm, current, gain_one)
    source, projections = mixer_inputs(normed, weights)
    mixed, pull_core = jax.vjp(mixer_core, *projections, *core_params(weights))
    mixed_low = mixed.astype(jnp.bfloat16)
    d_mixed = matmul_back_split(d_middle, weights[13])
    core_grads = pull_core(d_mixed)
    d_projs = tuple((g.astype(jnp.bfloat16) for g in core_grads[:6]))
    proj_weights = (weights[1], weights[2], weights[3], weights[7], weights[8], weights[12])
    d_first = matmul_back(d_projs[0], proj_weights[0])
    for index in range(1, 6):
        d_first = d_first + matmul_back(d_projs[index], proj_weights[index])
    d_normed = lax.psum(d_first.astype(jnp.bfloat16), "tensor").astype(jnp.float32)
    d_cur, d_gain_one = pull_in(d_normed)
    d_current = d_middle + d_cur
    small = (
        d_gain_one,
        core_grads[6],
        core_grads[7],
        core_grads[8],
        core_grads[9],
        core_grads[10],
        core_grads[11],
        d_gain_two,
    )
    record = (source, d_projs, mixed_low, d_middle, second, d_gate, d_up, hidden, upstream)
    return (d_current, small, record)


def weight_grads(record):
    source, d_projs, mixed_low, d_middle, second, d_gate, d_up, hidden, upstream = record
    projected = tuple((token_sum(source, d_proj) for d_proj in d_projs))
    grad_out = token_sum_split(mixed_low, d_middle)
    grad_gate = token_sum(second, d_gate)
    grad_up = token_sum(second, d_up)
    grad_down = token_sum_split(hidden, upstream)
    return projected + (grad_out, grad_gate, grad_up, grad_down)


def pass_forward(signal):
    return from_behind(signal, "section", 1)


def pass_backward(signal):
    return from_behind(signal, "section", -1)


def arrange(spread, common):
    return (
        common[0],
        spread[0],
        spread[1],
        spread[2],
        common[1],
        common[2],
        common[3],
        spread[3],
        spread[4],
        common[4],
        common[5],
        common[6],
        spread[5],
        spread[6],
        common[7],
        spread[7],
        spread[8],
        spread[9],
    )


def share_at_end(totals):
    parts = totals[0]
    extra = totals[1]
    spread = (
        lax.psum_scatter(
            parts[0].astype(jnp.bfloat16), "dp", scatter_dimension=0, tiled=True
        ).astype(jnp.float32),
        lax.psum_scatter(
            parts[1].astype(jnp.bfloat16), "dp", scatter_dimension=0, tiled=True
        ).astype(jnp.float32),
        lax.psum_scatter(
            parts[2].astype(jnp.bfloat16), "dp", scatter_dimension=0, tiled=True
        ).astype(jnp.float32),
        lax.psum_scatter(
            parts[3].astype(jnp.bfloat16), "dp", scatter_dimension=0, tiled=True
        ).astype(jnp.float32),
        lax.psum_scatter(
            parts[4].astype(jnp.bfloat16), "dp", scatter_dimension=0, tiled=True
        ).astype(jnp.float32),
        lax.psum_scatter(
            parts[5].astype(jnp.bfloat16), "dp", scatter_dimension=0, tiled=True
        ).astype(jnp.float32),
        lax.psum_scatter(
            parts[6].astype(jnp.bfloat16), "dp", scatter_dimension=1, tiled=True
        ).astype(jnp.float32),
        lax.psum_scatter(
            parts[7].astype(jnp.bfloat16), "dp", scatter_dimension=0, tiled=True
        ).astype(jnp.float32),
        lax.psum_scatter(
            parts[8].astype(jnp.bfloat16), "dp", scatter_dimension=0, tiled=True
        ).astype(jnp.float32),
        lax.psum_scatter(
            parts[9].astype(jnp.bfloat16), "dp", scatter_dimension=1, tiled=True
        ).astype(jnp.float32),
    )
    common = lax.psum(
        (extra[0], extra[1], extra[2], extra[3], extra[4], extra[5], extra[6], extra[7]), "dp"
    )
    return arrange(spread, common)


def accumulate(totals, spread_in, common_in):
    if totals is None:
        return (tuple(spread_in), tuple(common_in))
    return (
        tuple((a + b for a, b in zip(totals[0], spread_in))),
        tuple((a + b for a, b in zip(totals[1], common_in))),
    )


def per_device(
    inputs,
    cotangent,
    norm_gain1,
    w_query,
    w_key,
    w_value,
    conv_query,
    conv_key,
    conv_value,
    w_beta,
    w_decay,
    log_rate,
    step_bias,
    out_gain,
    w_gate_out,
    w_out,
    norm_gain2,
    w_ffn_gate,
    w_ffn_up,
    w_ffn_down,
):
    weights_all = (
        norm_gain1,
        w_query,
        w_key,
        w_value,
        conv_query,
        conv_key,
        conv_value,
        w_beta,
        w_decay,
        log_rate,
        step_bias,
        out_gain,
        w_gate_out,
        w_out,
        norm_gain2,
        w_ffn_gate,
        w_ffn_up,
        w_ffn_down,
    )
    weights = tuple((w[0] for w in weights_all))
    rounds = inputs.shape[0]
    is_first = lax.axis_index("section") == 0
    sources = inputs.astype(jnp.float32)
    targets = cotangent.astype(jnp.float32)
    received = jnp.zeros_like(sources[0])
    kept_inputs = []
    kept_mids = []
    results = []
    for step_index in range(rounds + 1):
        current = jnp.where(is_first, sources[min(step_index, rounds - 1)], received)
        middle, result = forward_layer(current, weights)
        leaving = result.astype(jnp.bfloat16)
        kept_inputs.append(current)
        kept_mids.append(middle)
        results.append(leaving)
        if step_index < rounds:
            received = pass_forward(leaving).astype(jnp.float32)
    hidden_out = jnp.stack(
        [jnp.where(is_first, results[m], results[m + 1]) for m in range(rounds)]
    )[None]
    returned = jnp.zeros_like(sources[0])
    sent_grads = []
    totals = None
    for step_index in range(rounds + 1):
        late_index = min(step_index, rounds - 1)
        early_index = max(step_index - 1, 0)
        current = jnp.where(is_first, kept_inputs[early_index], kept_inputs[late_index + 1])
        middle = jnp.where(is_first, kept_mids[early_index], kept_mids[late_index + 1])
        upstream = jnp.where(is_first, returned, targets[late_index])
        usable = jnp.where(
            is_first, 1.0 if step_index >= 1 else 0.0, 1.0 if step_index < rounds else 0.0
        )
        d_current, small, record = backward_inputs(current, middle, upstream, weights)
        small = tuple((g * usable for g in small))
        leaving = d_current.astype(jnp.bfloat16)
        sent_grads.append(leaving)
        if step_index < rounds:
            returned = pass_backward(leaving).astype(jnp.float32)
        spread = tuple((g * usable for g in weight_grads(record)))
        totals = accumulate(totals, spread, small)
    final_grads = share_at_end(totals)
    input_grad = jnp.stack(
        [jnp.where(is_first, sent_grads[m + 1], sent_grads[m]) for m in range(rounds)]
    )[None]
    return (hidden_out, input_grad) + tuple((g[None] for g in final_grads))


def solution(mesh):
    in_specs = (
        P(None, "dp", None, None),
        P(None, "dp", None, None),
        P("section", None),
        P("section", None, "tensor"),
        P("section", None, "tensor"),
        P("section", None, "tensor"),
        P("section", None, "tensor"),
        P("section", None, "tensor"),
        P("section", None, "tensor"),
        P("section", None, "tensor"),
        P("section", None, "tensor"),
        P("section", "tensor"),
        P("section", "tensor"),
        P("section", "tensor"),
        P("section", None, "tensor"),
        P("section", "tensor", None),
        P("section", None),
        P("section", None, "tensor"),
        P("section", None, "tensor"),
        P("section", "tensor", None),
    )
    out_specs = (
        P("section", None, "dp", None, None),
        P("section", None, "dp", None, None),
        P("section", None),
        P("section", "dp", "tensor"),
        P("section", "dp", "tensor"),
        P("section", "dp", "tensor"),
        P("section", None, "tensor"),
        P("section", None, "tensor"),
        P("section", None, "tensor"),
        P("section", "dp", "tensor"),
        P("section", "dp", "tensor"),
        P("section", "tensor"),
        P("section", "tensor"),
        P("section", "tensor"),
        P("section", "dp", "tensor"),
        P("section", "tensor", "dp"),
        P("section", None),
        P("section", "dp", "tensor"),
        P("section", "dp", "tensor"),
        P("section", "tensor", "dp"),
    )
    return jax.shard_map(
        per_device, mesh=mesh, in_specs=in_specs, out_specs=out_specs, check_vma=False
    )
```

profile of v0, /device:TPU:0, one launch (start us, length us, event | category | flops | bytes accessed | tf_op | source)
XLA Modules:
  0.0 1992.2 jit_solution(3273768379251194801)
XLA Ops:
  29.4 28.4 %while.168 = (s32[]{:T(128)}, f32[1,2,128,256]{3,2,1,0:T(8,128)S(1)}, f32[2,1,2,64,256]{4,3,2,1,0:T(8,128)S(1)}, f32[2,1,2,64]{3,2,1,0:T(2,128)}, f32[2,1,2,64,1...) while((s32[]{:T(128)}, ...), condition=%wide.region_5.7_spmd.clone, body=%wide.region_3.6_spmd.clone.sunk | while | flops 239730816 | bytes 3406533 | solution.py:99
  32.1 9.8 custom-call.54
  46.2 9.8 custom-call.54
  63.1 44.0 %all-reduce.113.cloned.1.call-done = f32[1,128,1024]{2,1,0:T(8,128)} async-done(((f32[1,128,1024]{2,1,0:T(8,128)}), f32[1,128,1024]{2,1,0:T(8,128)}) %all-reduce.113.cloned.1.call-update) | async-done | bytes 524304 | tf_op jit(solution)/shard_map/psum | solution.py:179
  120.5 34.7 %all-reduce.115.cloned.1.call-done = f32[1,128,1024]{2,1,0:T(8,128)} async-done(((f32[1,128,1024]{2,1,0:T(8,128)}), f32[1,128,1024]{2,1,0:T(8,128)}) %all-reduce.115.cloned.1.call-update) | async-done | bytes 524304 | tf_op jit(solution)/shard_map/psum | solution.py:184
  206.1 54.8 %while.169 = (s32[]{:T(128)}, f32[1,2,128,256]{3,2,1,0:T(8,128)}, f32[2,1,2,64,256]{4,3,2,1,0:T(8,128)}, f32[2,1,2,64]{3,2,1,0:T(2,128)}, f32[2,1,2,64,128]{4,3,...) while((s32[]{:T(128)}, f32[1,2,128,256]{3,2,1,0:T(8,128)}, ...), condition=%wide.region_15.17_spmd.clone, body=%wide.region_13.16_spmd.clone.sunk | while | flops 239730816 | bytes 3346145 | solution.py:99
  215.2 11.2 custom-call.55
  242.1 11.2 custom-call.55
  296.8 14.8 all-reduce.117.cloned.1.call-done
  322.5 51.3 %while.174 = (s32[]{:T(128)}, f32[1,2,128,256]{3,2,1,0:T(8,128)S(1)}, f32[2,1,2,64,256]{4,3,2,1,0:T(8,128)}, f32[2,1,2,128,256]{4,3,2,1,0:T(8,128)}, f32[2,1,2,6...) while((s32[]{:T(128)}, ...), condition=%wide.region_38.41_spmd.clone.clone, body=%wide.region_36.40_spmd.clone.clone.sunk | while | flops 239792256 | bytes 3888874 | solution.py:99
  331.2 11.2 custom-call.60
  356.9 11.2 custom-call.60
  426.8 53.7 %while.170 = (s32[]{:T(128)}, f32[1,2,128,256]{3,2,1,0:T(8,128)S(1)}, f32[2,1,2,64,256]{4,3,2,1,0:T(8,128)}, f32[2,1,2,64]{3,2,1,0:T(2,128)}, f32[2,1,2,64,128]{...) while((s32[]{:T(128)}, ...), condition=%wide.region_25.27_spmd.clone, body=%wide.region_23.26_spmd.clone.sunk | while | flops 239730816 | bytes 3346145 | solution.py:99
  436.5 11.2 custom-call.56
  463.4 11.2 custom-call.56
  496.4 35.3 %all-reduce.121.cloned.1.call-done = f32[1,128,1024]{2,1,0:T(8,128)} async-done(((f32[1,128,1024]{2,1,0:T(8,128)}), f32[1,128,1024]{2,1,0:T(8,128)}) %all-reduce.121.cloned.1.call-update) | async-done | bytes 524304 | tf_op jit(solution)/shard_map/psum | solution.py:179
  549.9 36.2 %all-reduce.125.cloned.1.call-done = bf16[1,128,1024]{2,1,0:T(8,128)(2,1)} async-done(((bf16[1,128,1024]{2,1,0:T(8,128)(2,1)}), bf16[1,128,1024]{2,1,0:T(8,128)(2,1)}) %all-reduce.125.cloned.1.call-update) | async-done | bytes 262160 | tf_op jit(solution)/shard_map/psum | solution.py:202
  600.2 59.7 %while.171 = (s32[]{:T(128)}, f32[1,2,128,256]{2,3,1,0:T(8,128)}, f32[2,1,2,64,128]{4,3,0,2,1:T(8,128)}, f32[2,1,2,64,128]{4,3,0,2,1:T(8,128)}, f32[2,1,2,64,256...) while((s32[]{:T(128)}, f32[1,2,128,256]{2,3,1,0:T(8,128)}, ...), condition=%wide.region_53.58_spmd.clone, body=%wide.region_41.57_spmd.clone.sunk | while | flops 649618688 | bytes 16885160 | solution.py:99
  608.5 9.8 custom-call.57
  638.6 9.8 custom-call.57
  704.2 25.3 %all-reduce.127.cloned.1.call-done = bf16[1,128,1024]{2,1,0:T(8,128)(2,1)} async-done(((bf16[1,128,1024]{2,1,0:T(8,128)(2,1)}), bf16[1,128,1024]{2,1,0:T(8,128)(2,1)}) %all-reduce.127.cloned.1.call-update) | async-done | bytes 262160 | tf_op jit(solution)/shard_map/psum | solution.py:216
  737.0 43.8 %while.175 = (s32[]{:T(128)}, f32[1,2,128,256]{3,2,1,0:T(8,128)S(1)}, f32[2,1,2,64,256]{4,3,2,1,0:T(8,128)}, f32[2,1,2,128,256]{4,3,2,1,0:T(8,128)}, f32[2,1,2,6...) while((s32[]{:T(128)}, ...), condition=%wide.region_66.71_spmd.clone.clone, body=%wide.region_64.70_spmd.clone.clone.sunk | while | flops 239792256 | bytes 3888362 | solution.py:99
  744.5 10.6 custom-call.61
  766.4 10.6 custom-call.61
  788.9 39.0 %all-reduce.129.cloned.1.call-done = bf16[1,128,1024]{2,1,0:T(8,128)(2,1)} async-done(((bf16[1,128,1024]{2,1,0:T(8,128)(2,1)}), bf16[1,128,1024]{2,1,0:T(8,128)(2,1)}) %all-reduce.129.cloned.1.call-update) | async-done | bytes 262160 | tf_op jit(solution)/shard_map/psum | solution.py:202
  844.7 73.1 %while.172 = (s32[]{:T(128)}, f32[1,2,128,256]{2,3,1,0:T(8,128)}, f32[2,1,2,64,128]{4,3,0,2,1:T(8,128)}, f32[2,1,2,64,128]{4,3,0,2,1:T(8,128)}, f32[2,1,2,64,256...) while((s32[]{:T(128)}, f32[1,2,128,256]{2,3,1,0:T(8,128)}, ...), condition=%wide.region_81.86_spmd.clone, body=%wide.region_69.85_spmd.clone.sunk | while | flops 649618688 | bytes 17052692 | solution.py:99
  855.3 11.2 custom-call.58
  892.2 11.2 custom-call.58
  955.5 37.0 %all-reduce.131.cloned.1.call-done = bf16[1,128,1024]{2,1,0:T(8,128)(2,1)} async-done(((bf16[1,128,1024]{2,1,0:T(8,128)(2,1)}), bf16[1,128,1024]{2,1,0:T(8,128)(2,1)}) %all-reduce.131.cloned.1.call-update) | async-done | bytes 262160 | tf_op jit(solution)/shard_map/psum | solution.py:216
  998.5 8.6 collective-permute-done.3
  1010.9 3.8 fusion.724
  1022.1 37.6 %while.176 = (s32[]{:T(128)}, f32[1,2,128,256]{3,2,1,0:T(8,128)}, f32[2,1,2,64,256]{4,3,2,1,0:T(8,128)}, f32[2,1,2,128,256]{4,3,2,1,0:T(8,128)}, f32[2,1,2,64]{3...) while((s32[]{:T(128)}, f32[1,2,128,256]{3,2,1,0:T(8,128)}, ...), condition=%wide.region_94.99_spmd.clone.clone, body=%wide.region_92.98_spmd.clone.clone.sunk | while | flops 239792256 | bytes 4417762 | solution.py:99
  1025.4 9.9 custom-call.62
  1044.2 9.8 custom-call.62
  1084.2 69.5 %while.173 = (s32[]{:T(128)}, f32[1,2,128,256]{2,3,1,0:T(8,128)}, f32[2,1,2,64,128]{4,3,0,2,1:T(8,128)}, f32[2,1,2,64,128]{4,3,0,2,1:T(8,128)}, f32[2,1,2,64,256...) while((s32[]{:T(128)}, f32[1,2,128,256]{2,3,1,0:T(8,128)}, ...), condition=%wide.region_109.114_spmd.clone, body=%wide.region_97.113_spmd.clone.sunk | while | flops 649618688 | bytes 16786368 | solution.py:99
  1094.1 11.2 custom-call.59
  1129.2 11.2 custom-call.59
  1235.2 25.4 %reduce-scatter.31.cloned.1.call-done = bf16[64,2]{1,0:T(8,128)(2,1)} async-done(((bf16[1024,2]{1,0:T(8,128)(2,1)}), bf16[64,2]{1,0:T(8,128)(2,1)}) %reduce-scatter.31.cloned.1.call-update) | async-done | bytes 272
  1262.0 73.2 %reduce-scatter.33.cloned.1.call-done = bf16[64,2]{1,0:T(8,128)(2,1)} async-done(((bf16[1024,2]{1,0:T(8,128)(2,1)}), bf16[64,2]{1,0:T(8,128)(2,1)}) %reduce-scatter.33.cloned.1.call-update) | async-done | bytes 272
  1336.5 40.9 %all-reduce.135.cloned.1.call-done = bf16[1,128,1024]{2,1,0:T(8,128)(2,1)} async-done(((bf16[1,128,1024]{2,1,0:T(8,128)(2,1)}), bf16[1,128,1024]{2,1,0:T(8,128)(2,1)}) %all-reduce.135.cloned.1.call-update) | async-done | bytes 262160 | tf_op jit(solution)/shard_map/psum | solution.py:216
  1378.6 74.5 %all-reduce.99 = (f32[1,1024]{1,0:T(1,128)}, f32[1,4,256]{2,1,0:T(4,128)}, f32[1,4,256]{2,1,0:T(4,128)}, f32[1,4,512]{2,1,0:T(4,128)}, f32[1,2]{1,0:T(1,128)}, /...) all-reduce(f32[1,1024]{1,0:T(1,128)S(1)} %bitcast.3310, ...), channel_id=1, replica_groups=mesh['section'=2,'dp'=16,'tensor'=4] {'dp'}, use_global_device_ids=true, to_apply=%region_117.122 | all-reduce | flops 6660 | bytes 53280 | tf_op jit(solution)/shard_map/psum | solution.py:309
  1456.6 70.8 %reduce-scatter.17.cloned.1.call-done = bf16[64,256]{1,0:T(8,128)(2,1)} async-done(((bf16[1024,256]{1,0:T(8,128)(2,1)}), bf16[64,256]{1,0:T(8,128)(2,1)}) %reduce-scatter.17.cloned.1.call-update) | async-done | bytes 32784 | tf_op jit(solution)/shard_map/reduce_scatter | solution.py:281
  1528.8 74.0 %reduce-scatter.19.cloned.1.call-done = bf16[64,512]{1,0:T(8,128)(2,1)} async-done(((bf16[1024,512]{1,0:T(8,128)(2,1)}), bf16[64,512]{1,0:T(8,128)(2,1)}) %reduce-scatter.19.cloned.1.call-update) | async-done | bytes 65552 | tf_op jit(solution)/shard_map/reduce_scatter | solution.py:284
  1604.3 74.3 %reduce-scatter.21.cloned.1.call-done = bf16[64,512]{1,0:T(8,128)(2,1)} async-done(((bf16[1024,512]{1,0:T(8,128)(2,1)}), bf16[64,512]{1,0:T(8,128)(2,1)}) %reduce-scatter.21.cloned.1.call-update) | async-done | bytes 65552 | tf_op jit(solution)/shard_map/reduce_scatter | solution.py:293
  1680.1 74.1 %reduce-scatter.23.cloned.1.call-done = bf16[512,64]{0,1:T(8,128)(2,1)} async-done(((bf16[512,1024]{0,1:T(8,128)(2,1)}), bf16[512,64]{0,1:T(8,128)(2,1)}) %reduce-scatter.23.cloned.1.call-update) | async-done | bytes 65552 | tf_op jit(solution)/shard_map/reduce_scatter | solution.py:296
  1755.7 74.9 %reduce-scatter.25.cloned.1.call-done = bf16[64,704]{1,0:T(8,128)(2,1)} async-done(((bf16[1024,704]{1,0:T(8,128)(2,1)}), bf16[64,704]{1,0:T(8,128)(2,1)}) %reduce-scatter.25.cloned.1.call-update) | async-done | bytes 90128 | tf_op jit(solution)/shard_map/reduce_scatter | solution.py:299
  1832.1 74.9 %reduce-scatter.27.cloned.1.call-done = bf16[64,704]{1,0:T(8,128)(2,1)} async-done(((bf16[1024,704]{1,0:T(8,128)(2,1)}), bf16[64,704]{1,0:T(8,128)(2,1)}) %reduce-scatter.27.cloned.1.call-update) | async-done | bytes 90128 | tf_op jit(solution)/shard_map/reduce_scatter | solution.py:302
  1908.6 74.9 %reduce-scatter.29.cloned.1.call-done = bf16[704,64]{0,1:T(8,128)(2,1)} async-done(((bf16[704,1024]{0,1:T(8,128)(2,1)}), bf16[704,64]{0,1:T(8,128)(2,1)}) %reduce-scatter.29.cloned.1.call-update) | async-done | bytes 90128 | tf_op jit(solution)/shard_map/reduce_scatter | solution.py:305
  (2011 shorter events, 766.6 us)
Async XLA Ops:
  7.2 102.7 %copy-start = (bf16[1,704,1024]{2,1,0:T(8,128)(2,1)S(1)}, bf16[1,704,1024]{2,1,0:T(8,128)(2,1)}, u32[]{:S(2)}) copy-start(bf16[1,704,1024]{2,1,0:T(8,128)(2,1)} %param.64) | copy-start | bytes 4325380
  7.2 99.8 %all-reduce.113.cloned.1.call-start = ((), (), s32[]{:S(2)}) async-start(), calls=%async_computation.10 | async-start | bytes 1048576 | tf_op jit(solution)/shard_map/psum | solution.py:179
  10.3 155.3 %copy-start.219 = (f32[1,1024]{1,0:T(1,128)}, f32[1,1024]{1,0:T(1,128)S(1)}, u32[]{:S(2)}) copy-start(f32[1,1024]{1,0:T(1,128)S(1)} %convert_element_type.689) | copy-start | bytes 12292
  59.2 50.0 %copy-start.1 = (bf16[1,1024,704]{1,2,0:T(8,128)(2,1)S(1)}, bf16[1,1024,704]{1,2,0:T(8,128)(2,1)}, u32[]{:S(2)}) copy-start(bf16[1,1024,704]{1,2,0:T(8,128)(2,1)} %param.62) | copy-start | bytes 4325380
  62.4 92.9 %all-reduce.115.cloned.1.call-start = ((), (), s32[]{:S(2)}) async-start(), calls=%async_computation.11 | async-start | bytes 1048576 | tf_op jit(solution)/shard_map/psum | solution.py:184
  62.5 51.1 %copy-start.177 = (f32[1,1024]{1,0:T(1,128)}, f32[1,1024]{1,0:T(1,128)S(1)}, u32[]{:S(2)}) copy-start(f32[1,1024]{1,0:T(1,128)S(1)} %convert_element_type.691) | copy-start | bytes 12292
  113.6 198.1 %all-reduce.117.cloned.1.call-start = ((), (), s32[]{:S(2)}) async-start(), calls=%async_computation.12 | async-start | bytes 1048576 | tf_op jit(solution)/shard_map/psum | solution.py:179
  156.6 8.5 collective-permute-start
  268.1 106.8 %all-reduce.119.cloned.1.call-start = ((), (), s32[]{:S(2)}) async-start(), calls=%async_computation.13 | async-start | bytes 1048576 | tf_op jit(solution)/shard_map/psum | solution.py:184
  272.5 41.9 %copy-start.327 = (f32[128,2]{0,1:T(2,128)}, f32[128,2]{0,1:T(2,128)S(1)}, u32[]{:S(2)}) copy-start(f32[128,2]{0,1:T(2,128)S(1)} %copy.817) | copy-start | bytes 3076
  320.3 211.4 %all-reduce.121.cloned.1.call-start = ((), (), s32[]{:S(2)}) async-start(), calls=%async_computation.14 | async-start | bytes 1048576 | tf_op jit(solution)/shard_map/psum | solution.py:179
  377.2 10.9 collective-permute-start.1
  489.2 96.9 %all-reduce.125.cloned.1.call-start = ((), (), s32[]{:S(2)}) async-start(), calls=%async_computation.16 | async-start | bytes 524288 | tf_op jit(solution)/shard_map/psum | solution.py:202
  496.4 37.7 %copy-start.221 = (f32[1,1024]{1,0:T(1,128)S(1)}, f32[1,1024]{1,0:T(1,128)}, u32[]{:S(2)}) copy-start(f32[1,1024]{1,0:T(1,128)} %copy-done.219) | copy-start | bytes 12292
  534.3 302.0 %copy-start.35 = (bf16[128,1024]{1,0:T(8,128)(2,1)}, bf16[128,1024]{1,0:T(8,128)(2,1)S(1)}, u32[]{:S(2)}) copy-start(bf16[128,1024]{1,0:T(8,128)(2,1)S(1)} %fusion.969) | copy-start | bytes 786436
  546.1 41.9 %copy-start.402 = (f32[128]{0:T(128)S(1)}, f32[128]{0:T(128)}, u32[]{:S(2)}) copy-start(f32[128]{0:T(128)} %get-tuple-element.2870) | copy-start | bytes 1540
  546.1 41.9 %copy-start.372 = (f32[128]{0:T(128)S(1)}, f32[128]{0:T(128)}, u32[]{:S(2)}) copy-start(f32[128]{0:T(128)} %fusion.1185) | copy-start | bytes 1540
  546.2 183.3 %all-reduce.127.cloned.1.call-start = ((), (), s32[]{:S(2)}) async-start(), calls=%async_computation.17 | async-start | bytes 524288 | tf_op jit(solution)/shard_map/psum | solution.py:216
  547.6 41.9 %copy-start.12 = (bf16[1,512,1024]{2,1,0:T(8,128)(2,1)S(1)}, bf16[1,512,1024]{2,1,0:T(8,128)(2,1)}, u32[]{:S(2)}) copy-start(bf16[1,512,1024]{2,1,0:T(8,128)(2,1)} %param.60) | copy-start | bytes 3145732
  689.4 138.5 %all-reduce.129.cloned.1.call-start = ((), (), s32[]{:S(2)}) async-start(), calls=%async_computation.18 | async-start | bytes 524288 | tf_op jit(solution)/shard_map/psum | solution.py:202
  734.2 46.6 %collective-permute-start.2 = (bf16[1,128,1024]{2,1,0:T(8,128)(2,1)}, bf16[1,128,1024]{2,1,0:T(8,128)(2,1)}, u32[]{:S(2)}, u32[]{:S(2)}) collective-permute-start(bf16[1,128,1024]{2,1,0:T(8,128)(2,1)} %fusion.877), channel_id=1, source_target_pairs={{64,0},{65,1},{66,2},{67,3},{68,4},{69,5},{70,6},{71,7},{72,8},{73... | collective-permute-start | bytes 786440 | tf_op jit(solution)/shard_map/ppermute | solution.py:12
  785.7 206.8 %all-reduce.131.cloned.1.call-start = ((), (), s32[]{:S(2)}) async-start(), calls=%async_computation.19 | async-start | bytes 524288 | tf_op jit(solution)/shard_map/psum | solution.py:216
  951.1 41.3 %copy-start.222 = (f32[1,1024]{1,0:T(1,128)S(1)}, f32[1,1024]{1,0:T(1,128)}, u32[]{:S(2)}) copy-start(f32[1,1024]{1,0:T(1,128)} %copy-done.219) | copy-start | bytes 12292
  951.1 41.3 %copy-start.368 = (f32[128]{0:T(128)S(1)}, f32[128]{0:T(128)}, u32[]{:S(2)}) copy-start(f32[128]{0:T(128)} %copy-done.367) | copy-start | bytes 1540
  951.2 43.2 %copy-start.401 = (f32[128]{0:T(128)S(1)}, f32[128]{0:T(128)}, u32[]{:S(2)}) copy-start(f32[128]{0:T(128)} %copy-done.400) | copy-start | bytes 1540
  952.4 117.6 %all-reduce.133.cloned.1.call-start = ((), (), s32[]{:S(2)}) async-start(), calls=%async_computation.20 | async-start | bytes 524288 | tf_op jit(solution)/shard_map/psum | solution.py:202
  952.6 45.3 %copy-start.3 = (bf16[1,1024,704]{1,2,0:T(8,128)(2,1)S(1)}, bf16[1,1024,704]{1,2,0:T(8,128)(2,1)}, u32[]{:S(2)}) copy-start(bf16[1,1024,704]{1,2,0:T(8,128)(2,1)} %param.62) | copy-start | bytes 4325380
  996.7 10.4 collective-permute-start.3
  1010.9 212.3 %all-reduce.123.cloned.1.call-start = ((), (), s32[]{:S(2)}) async-start(), calls=%async_computation.15 | async-start | bytes 1048576 | tf_op jit(solution)/shard_map/psum | solution.py:184
  1014.7 245.9 %reduce-scatter.31.cloned.1.call-start = ((), (), s32[]{:S(2)}) async-start(), calls=%async_computation.30 | async-start | bytes 278528
  1189.5 145.7 %reduce-scatter.33.cloned.1.call-start = ((), (), s32[]{:S(2)}) async-start(), calls=%async_computation.31 | async-start | bytes 278528
  1191.5 185.9 %all-reduce.135.cloned.1.call-start = ((), (), s32[]{:S(2)}) async-start(), calls=%async_computation.21 | async-start | bytes 524288 | tf_op jit(solution)/shard_map/psum | solution.py:216
  1196.1 259.0 %reduce-scatter.15.cloned.1.call-start = ((), (), s32[]{:S(2)}) async-start(), calls=%async_computation.22 | async-start | bytes 557056 | tf_op jit(solution)/shard_map/reduce_scatter | solution.py:278
  1198.6 328.8 %reduce-scatter.17.cloned.1.call-start = ((), (), s32[]{:S(2)}) async-start(), calls=%async_computation.23 | async-start | bytes 557056 | tf_op jit(solution)/shard_map/reduce_scatter | solution.py:281
  1200.7 402.1 %reduce-scatter.19.cloned.1.call-start = ((), (), s32[]{:S(2)}) async-start(), calls=%async_computation.24 | async-start | bytes 1114112 | tf_op jit(solution)/shard_map/reduce_scatter | solution.py:284
  1203.2 475.4 %reduce-scatter.21.cloned.1.call-start = ((), (), s32[]{:S(2)}) async-start(), calls=%async_computation.25 | async-start | bytes 1114112 | tf_op jit(solution)/shard_map/reduce_scatter | solution.py:293
  1206.1 548.1 %reduce-scatter.23.cloned.1.call-start = ((), (), s32[]{:S(2)}) async-start(), calls=%async_computation.26 | async-start | bytes 1114112 | tf_op jit(solution)/shard_map/reduce_scatter | solution.py:296
  1210.7 619.9 %reduce-scatter.25.cloned.1.call-start = ((), (), s32[]{:S(2)}) async-start(), calls=%async_computation.27 | async-start | bytes 1671168 | tf_op jit(solution)/shard_map/reduce_scatter | solution.py:299
  1214.6 692.4 %reduce-scatter.27.cloned.1.call-start = ((), (), s32[]{:S(2)}) async-start(), calls=%async_computation.28 | async-start | bytes 1671168 | tf_op jit(solution)/shard_map/reduce_scatter | solution.py:302
  1218.3 765.2 %reduce-scatter.29.cloned.1.call-start = ((), (), s32[]{:S(2)}) async-start(), calls=%async_computation.29 | async-start | bytes 1671168 | tf_op jit(solution)/shard_map/reduce_scatter | solution.py:305
  1229.5 148.0 %copy-start.223 = (f32[1,1024]{1,0:T(1,128)S(1)}, f32[1,1024]{1,0:T(1,128)}, u32[]{:S(2)}) copy-start(f32[1,1024]{1,0:T(1,128)} %copy-done.219) | copy-start | bytes 12292
  1229.5 148.0 %copy-start.370 = (f32[128]{0:T(128)S(1)}, f32[128]{0:T(128)}, u32[]{:S(2)}) copy-start(f32[128]{0:T(128)} %copy-done.369) | copy-start | bytes 1540
  1231.9 145.6 %copy-start.72 = (f32[1,128,1024]{2,1,0:T(8,128)S(1)}, f32[1,128,1024]{2,1,0:T(8,128)}, u32[]{:S(2)}) copy-start(f32[1,128,1024]{2,1,0:T(8,128)} %copy-done.71) | copy-start | bytes 1572868
  1231.9 146.7 %copy-start.317 = (f32[1024]{0:T(1024)S(1)}, f32[1024]{0:T(1024)}, u32[]{:S(2)}) copy-start(f32[1024]{0:T(1024)} %get-tuple-element.2562) | copy-start | bytes 12292
  1231.9 146.7 %copy-start.319 = (f32[1024]{0:T(1024)S(1)}, f32[1024]{0:T(1024)}, u32[]{:S(2)}) copy-start(f32[1024]{0:T(1024)} %get-tuple-element.2564) | copy-start | bytes 12292
  1231.9 221.3 %copy-start.408 = (f32[128]{0:T(128)S(1)}, f32[128]{0:T(128)}, u32[]{:S(2)}) copy-start(f32[128]{0:T(128)} %copy-done.407) | copy-start | bytes 1540
  1231.9 221.3 %copy-start.176 = (bf16[1,128,1024]{2,1,0:T(8,128)(2,1)S(1)}, bf16[1,128,1024]{2,1,0:T(8,128)(2,1)}, u32[]{:S(2)}) copy-start(bf16[1,128,1024]{2,1,0:T(8,128)(2,1)} %copy-done.175) | copy-start | bytes 786436
  1231.9 222.4 %copy-start.165 = (bf16[1,1,128,1024]{3,2,1,0:T(8,128)(2,1)S(1)}, bf16[1,1,128,1024]{3,2,1,0:T(8,128)(2,1)}, u32[]{:S(2)}) copy-start(bf16[1,1,128,1024]{3,2,1,0:T(8,128)(2,1)} %get-tuple-element.2837) | copy-start | bytes 786436
  (454 other events, 2130.7 us)
Sparse Core Ops, SparseCore 0:
  62.5 44.5 all-reduce.112
  113.7 41.4 all-reduce.114
  268.3 43.3 all-reduce.116
  320.4 41.6 all-reduce.118
  489.3 42.3 all-reduce.120
  546.3 39.7 all-reduce.124
  689.5 39.8 all-reduce.126
  785.8 42.0 all-reduce.128
  952.5 39.9 all-reduce.130
  1011.0 40.0 all-reduce.132
  1054.3 41.3 all-reduce.122
  1189.6 70.9 reduce-scatter.30
  1263.8 71.3 reduce-scatter.32
  1337.7 39.7 all-reduce.134
  1380.5 71.8 reduce-scatter.14
  1455.7 71.6 reduce-scatter.16
  1530.5 72.3 reduce-scatter.18
  1606.2 72.3 reduce-scatter.20
  1681.8 72.3 reduce-scatter.22
  1757.6 72.9 reduce-scatter.24
  1834.1 72.8 reduce-scatter.26
  1910.6 72.8 reduce-scatter.28
where the time goes:
time: 2010 us; the launch traced here: 1990 us
  waiting for transfers between devices  936 us (47%)
  other arithmetic  428 us (21%)
  matrix products  300 us (15%)
  local copies, waits for them, and re-layouts  221 us (11%)
  blocking collectives  74.5 us (4%)
    another operation x36, other arithmetic, block_step(): lax.linalg.triangular_solve(system, stacked_rhs, left_side=True, lower=True)  195 us
    psum x3, waiting for transfers between devices, backward_inputs(): lax.psum(d_first.astype(jnp.bfloat16), 'tensor').astype(jnp.float32)  103 us
    unnamed x24, waiting for transfers between devices  98.9 us
    psum x3, waiting for transfers between devices, forward_layer(): middle = current + lax.psum(matmul_low(mixed, weights[13]), 'tensor')  94.1 us
    psum x3, waiting for transfers between devices, backward_inputs(): lax.psum(d_second.astype(jnp.bfloat16), 'tensor').astype(jnp.float32)  75.2 us
    reduce_scatter x1, waiting for transfers between devices, share_at_end(): lax.psum_scatter(parts[8].astype(jnp.bfloat16), 'dp', scatter_dimension=0...  74.9 us
    reduce_scatter x1, waiting for transfers between devices, share_at_end(): lax.psum_scatter(parts[9].astype(jnp.bfloat16), 'dp', scatter_dimension=1...  74.9 us
    reduce_scatter x1, waiting for transfers between devices, share_at_end(): lax.psum_scatter(parts[7].astype(jnp.bfloat16), 'dp', scatter_dimension=0...  74.9 us
  transfers between devices with their start and end apart: 26, of which 20 were waited for; matrix products, arithmetic and copies ran while one was open for 20% of the time, Pallas kernels for 0%

commit v1 on v0

v1 whole, which is shorter than its diff:
```python
import functools

import jax
import jax.numpy as jnp
from jax import lax
from jax.experimental import pallas as pl
from jax.experimental.pallas import tpu as pltpu
from jax.sharding import PartitionSpec as P

F32 = jnp.float32
BF16 = jnp.bfloat16
MESH = pl.DeviceIdType.MESH
LEN = 128
ROWS = 64
HEADS = 2
DK = 128
DV = 256
SCALE = DK**-0.5
PQ, PK, PV, PG, PB, PEND = 0, 256, 512, 1024, 1536, 1664
FPAD = 768
NA = PEND + 512
NB = 3 * FPAD


def dot(left, right):
    return jnp.dot(left.astype(BF16), right.astype(BF16), preferred_element_type=F32)


def dot_nt(left, right):
    return lax.dot_general(
        left.astype(BF16),
        right.astype(BF16),
        (((1,), (1,)), ((), ())),
        preferred_element_type=F32,
    )


def dot_full(left, right):
    return jnp.dot(left, right, precision=lax.Precision.HIGHEST, preferred_element_type=F32)


def sigmoid(v):
    return 1.0 / (1.0 + jnp.exp(-v))


def rows_of(shape):
    return lax.broadcasted_iota(jnp.int32, shape, 0)


def shift_down(v, steps):
    if steps == 0:
        return v
    return jnp.where(rows_of(v.shape) >= steps, pltpu.roll(v, steps, 0), 0.0)


def shift_up(v, steps):
    if steps == 0:
        return v
    count = v.shape[0]
    return jnp.where(rows_of(v.shape) < count - steps, pltpu.roll(v, count - steps, 0), 0.0)


def conv_sum(v, taps):
    total = v * taps[3:4]
    for j in range(3):
        total = total + shift_down(v, 3 - j) * taps[j : j + 1]
    return total


def silu_slope(z):
    s = sigmoid(z)
    return s * (1.0 + z * (1.0 - s))


def unit_inverses(systems):
    row = lax.broadcasted_iota(jnp.int32, (LEN, LEN), 0)
    col = lax.broadcasted_iota(jnp.int32, (LEN, LEN), 1)
    eye = jnp.where(row == col, 1.0, 0.0)

    def band(level):
        same = (row >> (level + 1)) == (col >> (level + 1))
        return same & (((row >> level) & 1) == 1) & (((col >> level) & 1) == 0)

    first = band(0)
    inverses = [eye - jnp.where(first, m, 0.0) for m in systems]
    for level in range(1, 7):
        at = band(level)
        halves = [dot(t, jnp.where(at, m, 0.0)) for t, m in zip(inverses, systems)]
        inverses = [t - dot(x, t) for t, x in zip(inverses, halves)]
    return inverses


def rms_back(z, gain, dn):
    inv = lax.rsqrt(jnp.mean(z * z, axis=-1, keepdims=True) + 1e-06)
    hat = z * inv
    weighted = dn * gain
    dz = (weighted - hat * jnp.mean(weighted * hat, axis=-1, keepdims=True)) * inv
    return dz, jnp.sum(dn * hat, axis=0, keepdims=True)


def layer_kernel(
    inp, cot, g1, wq, wk, wv, cvq, cvk, cvv, wba, lrate, sbias, ogain, wgo, wo, g2, wfg, wfu, wfd,
    hid, ing, a1, dpr, a2, dgu, dho, mix, dyo, act, small,
    xbuf, ybuf, nbuf, hbuf, dbuf, gbuf,
    part, r1, r2, fwd, hrow, drow, acc,
    proj, zsum, qkv, gpre, onorm, dmix, upg, upu,
    tinv, amat, dmat, emat, umat, cols, gains,
    rs_s, rs_r, ag_s, ag_r, hop_s, hop_r, ga_s, ga_r,
):
    section = lax.axis_index("section")
    t = lax.axis_index("tensor")
    hi = t // 2
    core = t % 2
    sib = hi * 2 + (1 - core)
    opp = (1 - hi) * 2 + core
    other = 1 - section

    def remote(src, dst, ssem, rsem, device):
        return pltpu.make_async_remote_copy(
            src_ref=src, dst_ref=dst, send_sem=ssem, recv_sem=rsem,
            device_id=device, device_id_type=MESH,
        )

    barrier = pltpu.get_barrier_semaphore()
    for step in range(1, 4):
        pl.semaphore_signal(
            barrier, inc=1, device_id={"tensor": (t + step) % 4}, device_id_type=MESH
        )
    for step in range(4):
        pl.semaphore_signal(
            barrier, inc=1, device_id={"section": other, "tensor": (t + step) % 4},
            device_id_type=MESH,
        )
    pl.semaphore_wait(barrier, 7)

    def reduce_scatter(ph):
        far = remote(
            part.at[ph, 2 * (1 - hi) + 1 - core], r1.at[ph, 0], rs_s.at[ph, 0], rs_r.at[ph, 0],
            {"tensor": sib},
        )
        near = remote(
            part.at[ph, 2 * hi + 1 - core], r1.at[ph, 1], rs_s.at[ph, 1], rs_r.at[ph, 1],
            {"tensor": sib},
        )
        far.start()
        near.start()
        far.wait_recv()
        fwd[ph] = (part[ph, opp].astype(F32) + r1[ph, 0].astype(F32)).astype(BF16)
        cross = remote(
            fwd.at[ph], r2.at[ph], rs_s.at[ph, 2], rs_r.at[ph, 2], {"tensor": opp}
        )
        cross.start()
        near.wait_recv()
        acc[...] = part[ph, t].astype(F32) + r1[ph, 1].astype(F32)
        cross.wait_recv()
        total = acc[...] + r2[ph].astype(F32)
        far.wait_send()
        near.wait_send()
        cross.wait_send()
        return total

    class Gather:
        def __init__(self, buf, k):
            self.far = remote(buf.at[t], buf.at[t], ag_s.at[k, 0], ag_r.at[k, 0], {"tensor": opp})
            self.near = remote(buf.at[t], buf.at[t], ag_s.at[k, 1], ag_r.at[k, 1], {"tensor": sib})
            self.pass_on = remote(
                buf.at[opp], buf.at[opp], ag_s.at[k, 2], ag_r.at[k, 2], {"tensor": sib}
            )

        def start(self):
            self.far.start()
            self.near.start()

        def middle(self):
            self.far.wait_recv()
            self.pass_on.start()

        def finish(self):
            self.near.wait_recv()
            self.pass_on.wait_recv()
            self.far.wait_send()
            self.near.wait_send()
            self.pass_on.wait_send()

    def hop_send(buf, dst, k):
        copies = [
            remote(
                buf.at[t], dst.at[t], hop_s.at[k, y], hop_r.at[k, hi],
                {"section": other, "tensor": 2 * y + core},
            )
            for y in range(2)
        ]
        for copy in copies:
            copy.start()
        for copy in copies:
            copy.wait_send()

    def hop_receive(dst, k):
        passes = []
        for y in range(2):
            at = 2 * y + core
            remote(
                dst.at[at], dst.at[at], hop_s.at[k, y], hop_r.at[k, y],
                {"section": other, "tensor": t},
            ).wait_recv()
            pass_on = remote(
                dst.at[at], dst.at[at], hop_s.at[k, 2 + y], hop_r.at[k, 2 + y], {"tensor": sib}
            )
            pass_on.start()
            passes.append(pass_on)
        for pass_on in passes:
            pass_on.wait_recv()
        for pass_on in passes:
            pass_on.wait_send()

    def put_part(ph, value):
        for c in range(4):
            part[ph, c] = value[ROWS * c : ROWS * (c + 1)].astype(BF16)

    pairs = [(s, h) for s in range(2) for h in range(HEADS)]
    row = lax.broadcasted_iota(jnp.int32, (LEN, LEN), 0)
    col = lax.broadcasted_iota(jnp.int32, (LEN, LEN), 1)
    within = row >= col
    strict = row > col
    gain1 = g1[...].astype(F32)
    gain2 = g2[...].astype(F32)
    ogains = ogain[...].astype(F32)
    taps_q = cvq[...].astype(F32)
    taps_k = cvk[...].astype(F32)
    taps_v = cvv[...].astype(F32)

    def seq(s):
        return slice(LEN * s, LEN * (s + 1))

    def qc(h):
        return slice(PQ + DK * h, PQ + DK * (h + 1))

    def kc(h):
        return slice(PK + DK * h, PK + DK * (h + 1))

    def vc(h):
        return slice(PV + DV * h, PV + DV * (h + 1))

    def hv(h):
        return slice(DV * h, DV * (h + 1))

    @pl.when(section == 0)
    def _():
        for c in range(4):
            xbuf[c] = inp[ROWS * c : ROWS * (c + 1)]

    @pl.when(section == 1)
    def _():
        hop_receive(xbuf, 0)

    for c in range(4):
        x = xbuf[c].astype(F32)
        inv = lax.rsqrt(jnp.mean(x * x, axis=-1, keepdims=True) + 1e-06)
        a1[ROWS * c : ROWS * (c + 1)] = (x * inv * gain1).astype(BF16)
    source = a1[...]
    proj[:, PQ:PK] = dot(source, wq[...])
    proj[:, PK:PV] = dot(source, wk[...])
    proj[:, PV:PG] = dot(source, wv[...])
    pba = dot(source, wba[...])
    gpre[...] = dot(source, wgo[...])

    lane = lax.broadcasted_iota(jnp.int32, (LEN, LEN), 1)
    ltri = jnp.where(within, 1.0, 0.0)
    utri = jnp.where(row <= col, 1.0, 0.0)
    betas, decays, slopes = [], [], []
    for s, h in pairs:
        betas.append(sigmoid(pba[seq(s), h : h + 1]))
        pre = pba[seq(s), 2 + h : 3 + h] + sbias[0:1, h : h + 1]
        soft = jnp.maximum(pre, 0.0) + jnp.log1p(jnp.exp(-jnp.abs(pre)))
        rate = -jnp.exp(lrate[0:1, h : h + 1])
        decays.append(rate * soft)
        slopes.append(rate * sigmoid(pre))
    packed = jnp.zeros((LEN, LEN), F32)
    for i in range(4):
        packed = jnp.where(lane == i, decays[i], packed)
    cums = dot_full(ltri, packed)

    for s, h in pairs:
        z = conv_sum(proj[seq(s), qc(h)], taps_q[:, DK * h : DK * (h + 1)])
        zsum[seq(s), qc(h)] = z
        c = z * sigmoid(z)
        rq = lax.rsqrt(jnp.sum(c * c, axis=-1, keepdims=True) + 1e-06)
        qkv[seq(s), qc(h)] = c * (rq * SCALE)
        z = conv_sum(proj[seq(s), kc(h)], taps_k[:, DK * h : DK * (h + 1)])
        zsum[seq(s), kc(h)] = z
        c = z * sigmoid(z)
        rk = lax.rsqrt(jnp.sum(c * c, axis=-1, keepdims=True) + 1e-06)
        qkv[seq(s), kc(h)] = c * rk
        z = conv_sum(proj[seq(s), vc(h)], taps_v[:, hv(h)])
        zsum[seq(s), vc(h)] = z
        qkv[seq(s), vc(h)] = z * sigmoid(z)
        i = 2 * s + h
        cols[0, i] = jnp.broadcast_to(betas[i], (LEN, LEN))
        cols[1, i] = jnp.broadcast_to(decays[i], (LEN, LEN))
        cols[2, i] = jnp.broadcast_to(slopes[i], (LEN, LEN))
        cols[3, i] = jnp.broadcast_to(rq, (LEN, LEN))
        cols[4, i] = jnp.broadcast_to(rk, (LEN, LEN))

    systems = []
    for i, (s, h) in enumerate(pairs):
        cum = jnp.broadcast_to(cums[:, i : i + 1], (LEN, LEN))
        gaps = cum - cum.T
        decay = jnp.where(within, jnp.exp(jnp.where(within, gaps, 0.0)), 0.0)
        dmat[i] = decay
        kn = qkv[seq(s), kc(h)]
        e = jnp.where(strict, dot_nt(kn, kn) * decay, 0.0)
        emat[i] = e
        systems.append(cols[0, i] * e)
        amat[i] = dot_nt(qkv[seq(s), qc(h)], kn) * decay
    for i, inverse in enumerate(unit_inverses(systems)):
        tinv[i] = inverse.astype(BF16)
    for i, (s, h) in enumerate(pairs):
        w = qkv[seq(s), vc(h)] * cols[0, i][:, 0:1]
        umat[i] = dot(tinv[i], w).astype(BF16)
    for i, (s, h) in enumerate(pairs):
        o = dot(amat[i], umat[i])
        ro = lax.rsqrt(jnp.mean(o * o, axis=-1, keepdims=True) + 1e-05)
        cols[5, i] = jnp.broadcast_to(ro, (LEN, LEN))
        on = o * ro
        onorm[seq(s), hv(h)] = on
        gp = gpre[seq(s), hv(h)]
        mix[seq(s), hv(h)] = (on * ogains[:, hv(h)] * (gp * sigmoid(gp))).astype(BF16)

    put_part(0, dot(mix[...], wo[...]))
    hrow[...] = xbuf[t].astype(F32) + reduce_scatter(0)
    h_mine = hrow[...]
    inv = lax.rsqrt(jnp.mean(h_mine * h_mine, axis=-1, keepdims=True) + 1e-06)
    nbuf[t] = (h_mine * inv * gain2).astype(BF16)
    gather = Gather(nbuf, 0)
    gather.start()
    gather.middle()
    gather.finish()
    for c in range(4):
        a2[ROWS * c : ROWS * (c + 1)] = nbuf[c]
    source = a2[...]
    upg[...] = dot(source, wfg[...])
    upu[...] = dot(source, wfu[...])
    ug = upg[...]
    s_act = (ug * sigmoid(ug) * upu[...]).astype(BF16)
    act[:, 704:FPAD] = jnp.zeros((2 * LEN, FPAD - 704), BF16)
    act[:, 0:704] = s_act
    put_part(1, dot(s_act, wfd[...]))
    ybuf[t] = (hrow[...] + reduce_scatter(1)).astype(BF16)
    hidden = Gather(ybuf, 1)

    @pl.when(section == 0)
    def _():
        hop_send(ybuf, xbuf, 0)

    hidden.start()

    @pl.when(section == 1)
    def _():
        for c in range(4):
            dbuf[c] = cot[ROWS * c : ROWS * (c + 1)]

    @pl.when(section == 0)
    def _():
        hidden.middle()
        hop_receive(dbuf, 1)

    for c in range(4):
        dyo[ROWS * c : ROWS * (c + 1)] = dbuf[c]
    ds = dot_nt(dyo[...], wfd[...])
    ug = upg[...]
    uu = upu[...]
    sg = sigmoid(ug)
    pad = jnp.zeros((2 * LEN, FPAD - 704), BF16)
    dgu[:, 704:FPAD] = pad
    dgu[:, FPAD + 704 :] = pad
    dgu[:, 0:704] = (ds * uu * (sg * (1.0 + ug * (1.0 - sg)))).astype(BF16)
    dgu[:, FPAD : FPAD + 704] = (ds * (ug * sg)).astype(BF16)
    put_part(2, dot_nt(dgu[:, 0:704], wfg[...]) + dot_nt(dgu[:, FPAD : FPAD + 704], wfu[...]))
    dn = reduce_scatter(2)
    dz, dgain2 = rms_back(hrow[...], gain2, dn)
    drow[...] = dbuf[t].astype(F32) + dz
    hbuf[t] = drow[...].astype(BF16)
    gather = Gather(hbuf, 2)
    gather.start()

    @pl.when(section == 1)
    def _():
        hidden.middle()

    gather.middle()
    gather.finish()
    for c in range(4):
        dho[ROWS * c : ROWS * (c + 1)] = hbuf[c]
    dmix[...] = dot_nt(dho[...], wo[...])

    small[...] = jnp.zeros_like(small)
    douts = [jnp.zeros((1, DV), F32) for _ in range(HEADS)]
    dos = []
    for i, (s, h) in enumerate(pairs):
        dm = dmix[seq(s), hv(h)]
        gp = gpre[seq(s), hv(h)]
        sg = sigmoid(gp)
        on = onorm[seq(s), hv(h)]
        og = ogains[:, hv(h)]
        dgate = dm * on
        dpr[seq(s), PG + DV * h : PG + DV * (h + 1)] = (
            dgate * og * (sg * (1.0 + gp * (1.0 - sg)))
        ).astype(BF16)
        silu_g = gp * sg
        douts[h] = douts[h] + jnp.sum(dgate * silu_g, axis=0, keepdims=True)
        don = dm * silu_g * og
        ro = cols[5, i][:, 0:1]
        do = ro * (don - on * jnp.mean(don * on, axis=-1, keepdims=True))
        dos.append(do.astype(BF16))
    for h in range(HEADS):
        small[6:7, hv(h)] = douts[h]
    das = [dot_nt(dos[i], umat[i]) for i in range(4)]
    dus = [dot(amat[i].T, dos[i]) for i in range(4)]
    dws = [dot(tinv[i].astype(F32).T, dus[i]) for i in range(4)]
    dms = [jnp.where(strict, -dot_nt(dws[i], umat[i]), 0.0) for i in range(4)]
    dbetas, dcs, dqs, dks = [], [], [], []
    for i, (s, h) in enumerate(pairs):
        beta = cols[0, i]
        e = emat[i]
        decay = dmat[i]
        v = qkv[seq(s), vc(h)]
        de = dms[i] * e
        dbetas.append(
            jnp.sum(dws[i] * v, axis=-1, keepdims=True) + jnp.sum(de, axis=-1, keepdims=True)
        )
        dgap = das[i] * amat[i] + de * beta
        dcs.append(jnp.sum(dgap - dgap.T, axis=-1, keepdims=True))
        dqk = das[i] * decay
        dkk = dms[i] * beta * decay
        kn = qkv[seq(s), kc(h)]
        qn = qkv[seq(s), qc(h)]
        dqs.append(dot(dqk, kn))
        dks.append(dot(dqk.T, qn) + dot(dkk + dkk.T, kn))
    packed = jnp.zeros((LEN, LEN), F32)
    for i in range(4):
        packed = jnp.where(lane == i, dcs[i], packed)
    dgs = dot_full(utri, packed)

    dcq = [jnp.zeros((1, DK), F32) for _ in range(4 * HEADS)]
    dck = [jnp.zeros((1, DK), F32) for _ in range(4 * HEADS)]
    dcv = [jnp.zeros((1, DV), F32) for _ in range(4 * HEADS)]

    def conv_back(dz, at_rows, at_cols, taps, sums, h):
        pre = proj[at_rows, at_cols]
        total = dz * taps[3:4]
        for j in range(3):
            total = total + shift_up(dz, 3 - j) * taps[j : j + 1]
        for j in range(4):
            sums[4 * h + j] = sums[4 * h + j] + jnp.sum(
                dz * shift_down(pre, 3 - j), axis=0, keepdims=True
            )
        dpr[at_rows, at_cols] = total.astype(BF16)

    for i, (s, h) in enumerate(pairs):
        qn = qkv[seq(s), qc(h)]
        dq = dqs[i]
        dc = (cols[3, i] * SCALE) * (
            dq - qn * (jnp.sum(qn * dq, axis=-1, keepdims=True) * (1.0 / (SCALE * SCALE)))
        )
        dz = dc * silu_slope(zsum[seq(s), qc(h)])
        conv_back(dz, seq(s), qc(h), taps_q[:, DK * h : DK * (h + 1)], dcq, h)
        kn = qkv[seq(s), kc(h)]
        dk = dks[i]
        dc = cols[4, i] * (dk - kn * jnp.sum(kn * dk, axis=-1, keepdims=True))
        dz = dc * silu_slope(zsum[seq(s), kc(h)])
        conv_back(dz, seq(s), kc(h), taps_k[:, DK * h : DK * (h + 1)], dck, h)
        dv = dws[i] * cols[0, i][:, 0:1]
        dz = dv * silu_slope(zsum[seq(s), vc(h)])
        conv_back(dz, seq(s), vc(h), taps_v[:, hv(h)], dcv, h)
    for h in range(HEADS):
        for j in range(4):
            small[2 + j : 3 + j, DK * h : DK * (h + 1)] = dcq[4 * h + j]
            small[2 + j : 3 + j, 256 + DK * h : 256 + DK * (h + 1)] = dck[4 * h + j]
            small[2 + j : 3 + j, 512 + DV * h : 512 + DV * (h + 1)] = dcv[4 * h + j]
    lane_row = lax.broadcasted_iota(jnp.int32, (1, LEN), 1)
    scal = jnp.zeros((1, LEN), F32)
    for s in range(2):
        block = jnp.zeros((LEN, LEN), F32)
        for h in range(HEADS):
            i = 2 * s + h
            beta = cols[0, i]
            dg = jnp.broadcast_to(dgs[:, i : i + 1], (LEN, LEN))
            dpb = dbetas[i] * beta * (1.0 - beta)
            dpa = dg * cols[2, i]
            block = jnp.where(lane == h, dpb, block)
            block = jnp.where(lane == 2 + h, dpa, block)
            scal = scal + jnp.where(
                lane_row == h, jnp.sum(dg * cols[1, i], axis=0, keepdims=True), 0.0
            )
            scal = scal + jnp.where(lane_row == 2 + h, jnp.sum(dpa, axis=0, keepdims=True), 0.0)
        dpr[seq(s), PB:PEND] = block.astype(BF16)
    small[6:7, 512:640] = scal

    value = dot_nt(dpr[:, PQ:PK], wq[...])
    value = value + dot_nt(dpr[:, PK:PV], wk[...])
    value = value + dot_nt(dpr[:, PV:PG], wv[...])
    value = value + dot_nt(dpr[:, PG:PB], wgo[...])
    value = value + dot_nt(dpr[:, PB:PEND], wba[...])
    put_part(3, value)
    dn = reduce_scatter(3)
    dz, dgain1 = rms_back(xbuf[t].astype(F32), gain1, dn)
    gbuf[t] = (drow[...] + dz).astype(BF16)
    back = Gather(gbuf, 3)

    @pl.when(section == 1)
    def _():
        hop_send(gbuf, dbuf, 1)

    back.start()
    zero = jnp.zeros((6, 1024), F32)
    gains[0] = jnp.concatenate([dgain1, dgain2, zero], axis=0)
    sums = [
        remote(
            gains.at[0], gains.at[step], ga_s.at[step - 1], ga_r.at[step - 1],
            {"tensor": (t + step) % 4},
        )
        for step in range(1, 4)
    ]
    for copy in sums:
        copy.start()
    back.middle()
    hidden.finish()
    for c in range(4):
        hid[ROWS * c : ROWS * (c + 1)] = ybuf[c]
    for copy in sums:
        copy.wait_recv()
    total = gains[0] + gains[1] + gains[2] + gains[3]
    small[0:2] = total[0:2]
    back.finish()
    for c in range(4):
        ing[ROWS * c : ROWS * (c + 1)] = gbuf[c]
    for copy in sums:
        copy.wait_send()


def run_layer(args):
    tokens = 2 * LEN
    results = (
        ((tokens, 1024), BF16), ((tokens, 1024), BF16), ((tokens, 1024), BF16),
        ((tokens, PEND), BF16), ((tokens, 1024), BF16), ((tokens, 2 * FPAD), BF16),
        ((tokens, 1024), BF16), ((tokens, 512), BF16), ((tokens, 1024), BF16),
        ((tokens, FPAD), BF16), ((8, 1024), F32),
    )
    chunk = (4, ROWS, 1024)
    buffers = [pltpu.VMEM(chunk, BF16)] * 6 + [
        pltpu.VMEM((4,) + chunk, BF16),
        pltpu.VMEM((4, 2, ROWS, 1024), BF16),
        pltpu.VMEM((4, ROWS, 1024), BF16),
        pltpu.VMEM((4, ROWS, 1024), BF16),
        pltpu.VMEM((ROWS, 1024), F32),
        pltpu.VMEM((ROWS, 1024), F32),
        pltpu.VMEM((ROWS, 1024), F32),
        pltpu.VMEM((tokens, 1024), F32),
        pltpu.VMEM((tokens, 1024), F32),
        pltpu.VMEM((tokens, 1024), F32),
        pltpu.VMEM((tokens, 512), F32),
        pltpu.VMEM((tokens, 512), F32),
        pltpu.VMEM((tokens, 512), F32),
        pltpu.VMEM((tokens, 704), F32),
        pltpu.VMEM((tokens, 704), F32),
        pltpu.VMEM((4, LEN, LEN), BF16),
        pltpu.VMEM((4, LEN, LEN), F32),
        pltpu.VMEM((4, LEN, LEN), F32),
        pltpu.VMEM((4, LEN, LEN), F32),
        pltpu.VMEM((4, LEN, DV), BF16),
        pltpu.VMEM((6, 4, LEN, LEN), F32),
        pltpu.VMEM((4, 8, 1024), F32),
    ]
    sems = [
        pltpu.SemaphoreType.DMA((4, 3)), pltpu.SemaphoreType.DMA((4, 3)),
        pltpu.SemaphoreType.DMA((4, 3)), pltpu.SemaphoreType.DMA((4, 3)),
        pltpu.SemaphoreType.DMA((2, 4)), pltpu.SemaphoreType.DMA((2, 4)),
        pltpu.SemaphoreType.DMA((3,)), pltpu.SemaphoreType.DMA((3,)),
    ]
    return pl.pallas_call(
        layer_kernel,
        out_shape=[jax.ShapeDtypeStruct(s, d) for s, d in results],
        in_specs=[pl.BlockSpec(memory_space=pltpu.VMEM)] * len(args),
        out_specs=[pl.BlockSpec(memory_space=pltpu.VMEM)] * len(results),
        scratch_shapes=buffers + sems,
        compiler_params=pltpu.CompilerParams(
            collective_id=0, has_side_effects=True, vmem_limit_bytes=58 * 1024 * 1024
        ),
        name="layer",
    )(*args)


def grad_kernel(
    a1, dpr, a2, dgu, dho, mix, dyo, act, small,
    gq, gk, gv, gb, gd, ggo, gout, gfg, gfu, gfd,
    dg1, dcq, dck, dcv, dlr, dsb, dog, dg2,
    ga, gz, a1p, a1m, a2p, a2m, b1p, b1m, b2p, b2m,
    ha, hb, c1p, c1m, c2p, c2m, d1p, d1m, d2p, d2m,
    sx, sz, send, recv, ssend, srecv,
):
    place = lax.axis_index("dp")
    z = place // 4
    x = place % 4

    def at_x(step):
        return {"dp": z * 4 + (x + step) % 4}

    def at_z(step):
        return {"dp": ((z + step) % 4) * 4 + x}

    def remote(src, dst, ssem, rsem, device):
        return pltpu.make_async_remote_copy(
            src_ref=src, dst_ref=dst, send_sem=ssem, recv_sem=rsem,
            device_id=device, device_id_type=MESH,
        )

    barrier = pltpu.get_barrier_semaphore()
    for step in range(1, 4):
        pl.semaphore_signal(barrier, inc=1, device_id=at_x(step), device_id_type=MESH)
        pl.semaphore_signal(barrier, inc=1, device_id=at_z(step), device_id_type=MESH)

    def outer(left, right, width, store):
        for rows in range(4):
            lt = left[:, 256 * rows : 256 * (rows + 1)].T
            for start in range(0, width, 256):
                size = min(256, width - start)
                value = jnp.dot(
                    lt, right[:, start : start + size], preferred_element_type=F32
                ).astype(BF16)
                for part in range(4):
                    store(rows, part, start, size, value[ROWS * part : ROWS * (part + 1)])

    def into_a(offset):
        def store(zz, xx, start, size, value):
            ga[xx, zz, :, offset + start : offset + start + size] = value
        return store

    def into_b(offset):
        def store(zz, xx, start, size, value):
            gz[zz, xx, :, offset + start : offset + start + size] = value
        return store

    outer(a1, dpr, PEND, into_a(0))
    outer(dho, mix, 512, into_a(PEND))
    outer(a2, dgu, 2 * FPAD, into_b(0))
    outer(dyo, act, FPAD, into_b(2 * FPAD))

    pl.semaphore_wait(barrier, 6)

    class Ring:
        def __init__(self, g, me, where, bufs, k, half):
            one_p, one_m, two_p, two_m = bufs
            self.g, self.me, self.bufs, self.half = g, me, bufs, half
            self.right = right = (me + 1) % 4
            self.left = left = (me + 3) % 4
            far = (me + 2) % 4
            lo, up = pl.ds(0, half), pl.ds(half, half)
            self.lo, self.up = lo, up
            self.p1 = remote(g.at[far, lo], one_p, send.at[k, 0], recv.at[k, 0], where(1))
            self.m1 = remote(g.at[far, up], one_m, send.at[k, 1], recv.at[k, 1], where(3))
            self.p2 = remote(g.at[right, up], two_p.at[up], send.at[k, 2], recv.at[k, 2], where(1))
            self.m2 = remote(g.at[left, lo], two_m.at[lo], send.at[k, 3], recv.at[k, 3], where(3))
            self.p3 = remote(g.at[right, lo], two_p.at[lo], send.at[k, 4], recv.at[k, 4], where(1))
            self.m3 = remote(g.at[left, up], two_m.at[up], send.at[k, 5], recv.at[k, 5], where(3))

        def start(self):
            for copy in (self.p1, self.m1, self.p2, self.m2):
                copy.start()

        def relay(self):
            one_p, one_m, two_p, two_m = self.bufs
            g, lo, up = self.g, self.lo, self.up
            self.p1.wait_recv()
            add_into(g.at[self.right, lo], one_p)
            self.p3.start()
            self.m1.wait_recv()
            add_into(g.at[self.left, up], one_m)
            self.m3.start()

        def arrive(self):
            for copy in (self.p2, self.m2, self.p3, self.m3):
                copy.wait_recv()

        def sent(self):
            for copy in (self.p1, self.m1, self.p2, self.m2, self.p3, self.m3):
                copy.wait_send()

    def add_into(ref, other):
        if len(other.shape) == 3:
            @pl.loop(0, other.shape[0])
            def _(c):
                ref[c] = (ref[c].astype(F32) + other[c].astype(F32)).astype(BF16)
        else:
            ref[...] = (ref[...].astype(F32) + other[...].astype(F32)).astype(BF16)

    sx[0] = small[...]
    small_x = [
        remote(sx.at[0], sx.at[step], ssend.at[step - 1], srecv.at[step - 1], at_x(step))
        for step in range(1, 4)
    ]
    small_z = [
        remote(sz.at[0], sz.at[step], ssend.at[step + 2], srecv.at[step + 2], at_z(step))
        for step in range(1, 4)
    ]
    first_a = Ring(ga, x, at_x, (a1p, a1m, a2p, a2m), 0, 2)
    first_b = Ring(gz, z, at_z, (b1p, b1m, b2p, b2m), 1, 2)
    second_a = Ring(ha, z, at_z, (c1p, c1m, c2p, c2m), 2, 32)
    second_b = Ring(hb, x, at_x, (d1p, d1m, d2p, d2m), 3, 32)
    first_a.start()
    first_b.start()
    for copy in small_x:
        copy.start()
    first_a.relay()
    first_b.relay()
    for copy in small_x:
        copy.wait_recv()
    sz[0] = sx[0] + sx[1] + sx[2] + sx[3]
    for copy in small_z:
        copy.start()

    def merge(ring, out):
        _, _, two_p, two_m = ring.bufs

        @pl.loop(0, 4)
        def _(c):
            out[c] = (
                ring.g[ring.me, c].astype(F32) + two_p[c].astype(F32) + two_m[c].astype(F32)
            ).astype(BF16)

    first_a.arrive()
    merge(first_a, ha)
    second_a.start()
    first_b.arrive()
    merge(first_b, hb)
    second_b.start()
    second_a.relay()
    second_b.relay()
    for copy in small_z:
        copy.wait_recv()
    sums = sz[0] + sz[1] + sz[2] + sz[3]
    dg1[...] = sums[0:1]
    dg2[...] = sums[1:2]
    dcq[...] = sums[2:6, 0:256]
    dck[...] = sums[2:6, 256:512]
    dcv[...] = sums[2:6, 512:1024]
    dog[...] = sums[6:7, 0:512]
    dlr[...] = sums[6:7, 512:514]
    dsb[...] = sums[6:7, 514:516]

    def total(ring, start, size):
        _, _, two_p, two_m = ring.bufs
        at = slice(start, start + size)
        return (
            ring.g[ring.me, :, at].astype(F32)
            + two_p[:, at].astype(F32)
            + two_m[:, at].astype(F32)
        )

    second_a.arrive()
    gq[...] = total(second_a, PQ, 256)
    gk[...] = total(second_a, PK, 256)
    gv[...] = total(second_a, PV, 512)
    ggo[...] = total(second_a, PG, 512)
    pair = total(second_a, PB, 128)
    gb[...] = pair[:, 0:2]
    gd[...] = pair[:, 2:4]
    gout[...] = total(second_a, PEND, 512).T
    second_b.arrive()
    gfg[...] = total(second_b, 0, FPAD)[:, 0:704]
    gfu[...] = total(second_b, FPAD, FPAD)[:, 0:704]
    gfd[...] = total(second_b, 2 * FPAD, FPAD).T[0:704]
    for ring in (first_a, first_b, second_a, second_b):
        ring.sent()
    for copy in small_x + small_z:
        copy.wait_send()


def run_grads(args):
    results = (
        (ROWS, 256), (ROWS, 256), (ROWS, 512), (ROWS, 2), (ROWS, 2), (ROWS, 512),
        (512, ROWS), (ROWS, 704), (ROWS, 704), (704, ROWS),
        (1, 1024), (4, 256), (4, 256), (4, 512), (1, 2), (1, 2), (1, 512), (1, 1024),
    )

    def first(n):
        return [pltpu.VMEM((2, ROWS, n), BF16)] * 2 + [pltpu.VMEM((4, ROWS, n), BF16)] * 2

    def second(n):
        return [pltpu.VMEM((ROWS // 2, n), BF16)] * 2 + [pltpu.VMEM((ROWS, n), BF16)] * 2

    buffers = (
        [pltpu.VMEM((4, 4, ROWS, NA), BF16), pltpu.VMEM((4, 4, ROWS, NB), BF16)]
        + first(NA)
        + first(NB)
        + [pltpu.VMEM((4, ROWS, NA), BF16), pltpu.VMEM((4, ROWS, NB), BF16)]
        + second(NA)
        + second(NB)
        + [pltpu.VMEM((4, 8, 1024), F32)] * 2
    )
    sems = [
        pltpu.SemaphoreType.DMA((4, 6)), pltpu.SemaphoreType.DMA((4, 6)),
        pltpu.SemaphoreType.DMA((6,)), pltpu.SemaphoreType.DMA((6,)),
    ]
    return pl.pallas_call(
        grad_kernel,
        out_shape=[jax.ShapeDtypeStruct(s, F32) for s in results],
        in_specs=[pl.BlockSpec(memory_space=pltpu.VMEM)] * len(args),
        out_specs=[pl.BlockSpec(memory_space=pltpu.VMEM)] * len(results),
        scratch_shapes=buffers + sems,
        compiler_params=pltpu.CompilerParams(
            collective_id=1, has_side_effects=True, vmem_limit_bytes=58 * 1024 * 1024
        ),
        name="grads",
    )(*args)


def per_device(
    inputs, cotangent, norm_gain1, w_query, w_key, w_value, conv_query, conv_key, conv_value,
    w_beta, w_decay, log_rate, step_bias, out_gain, w_gate_out, w_out, norm_gain2,
    w_ffn_gate, w_ffn_up, w_ffn_down,
):
    tokens = 2 * LEN
    width = inputs.shape[-1]
    wba = jnp.concatenate(
        [w_beta[0], w_decay[0], jnp.zeros((width, LEN - 4), BF16)], axis=1
    )
    out = run_layer((
        inputs.reshape(tokens, width), cotangent.reshape(tokens, width),
        norm_gain1, w_query[0], w_key[0], w_value[0],
        conv_query[0], conv_key[0], conv_value[0], wba, log_rate, step_bias, out_gain,
        w_gate_out[0], w_out[0], norm_gain2, w_ffn_gate[0], w_ffn_up[0], w_ffn_down[0],
    ))
    hidden, input_grad = (v.reshape((1,) + inputs.shape) for v in out[:2])
    (gq, gk, gv, gb, gd, ggo, gout, gfg, gfu, gfd, dg1, dcq, dck, dcv, dlr, dsb, dog, dg2) = (
        run_grads(tuple(out[2:]))
    )
    return (
        hidden, input_grad, dg1, gq[None], gk[None], gv[None], dcq[None], dck[None], dcv[None],
        gb[None], gd[None], dlr, dsb, dog, ggo[None], gout[None], dg2,
        gfg[None], gfu[None], gfd[None],
    )


def solution(mesh):
    three = P("section", None, "tensor")
    in_specs = (
        P(None, "dp", None, None), P(None, "dp", None, None), P("section", None),
        three, three, three, three, three, three, three, three,
        P("section", "tensor"), P("section", "tensor"), P("section", "tensor"),
        three, P("section", "tensor", None), P("section", None),
        three, three, P("section", "tensor", None),
    )
    spread = P("section", "dp", "tensor")
    out_specs = (
        P("section", None, "dp", None, None), P("section", None, "dp", None, None),
        P("section", None), spread, spread, spread, three, three, three, spread, spread,
        P("section", "tensor"), P("section", "tensor"), P("section", "tensor"),
        spread, P("section", "tensor", "dp"), P("section", None),
        spread, spread, P("section", "tensor", "dp"),
    )
    return jax.shard_map(
        per_device, mesh=mesh, in_specs=in_specs, out_specs=out_specs, check_vma=False
    )
```

time: 2010 us -> 222 us (0.11)
  waiting for transfers between devices: 936 us -> 0 us
  other arithmetic: 428 us -> 0.87 us
  matrix products: 300 us -> 0 us
  local copies, waits for them, and re-layouts: 221 us -> 22.7 us
  Pallas kernels: 0 us -> 198 us
  blocking collectives: 74.5 us -> 0 us
    reduce_scatter x8 -> x0, waiting for transfers between devices: 518 us -> none  [the longest x1 74.9 us: share_at_end(): lax.psum_scatter(parts[8].astype(jnp.bfloat16), 'dp', scatter_dimension=0...]
    psum x12 -> x0, waiting for transfers between devices: 307 us -> none  [the longest x3 103 us: backward_inputs(): lax.psum(d_first.astype(jnp.bfloat16), 'tensor').astype(jnp.float32)]
    dot_general x294 -> x0, matrix products: 275 us -> none  [the longest x48 68.8 us: matmul_low(): jnp.einsum('btd,df->btf', left, right, preferred_element_type=jnp.float32)]
    another operation x89 -> x0, other arithmetic: 221 us -> none  [the longest x36 195 us: block_step(): lax.linalg.triangular_solve(system, stacked_rhs, left_side=True, lower=True)]
    pallas_call x0 -> x2, Pallas kernels: none -> 198 us  [the longest x1 134 us: run_layer(): pl.pallas_call(layer_kernel, out_shape=[jax.ShapeDtypeStruct(s, d) for s,...]
    unnamed x24 -> x0, waiting for transfers between devices: 98.9 us -> none
    psum x1 -> x0, blocking collectives: 74.5 us -> none  [share_at_end(): lax.psum((extra[0], extra[1], extra[2], extra[3], extra[4], extra[5], ext...]
    reduce_sum x77 -> x0, other arithmetic: 66.5 us -> none  [the longest x9 14 us: short_conv(): summed = summed + padded[:, offset:offset + seq_len, :] * kernel[offset]]
  transfers between devices with their start and end apart: 26 -> 0, of which waited for: 20 -> 0; matrix products, arithmetic and copies ran while one was open for 20% -> 0% of each run, Pallas kernels for 0% -> 0%
where the time goes in v1:
time: 222 us
  Pallas kernels  198 us (89%)
  local copies, waits for them, and re-layouts  22.7 us (10%)
    pallas_call x1, Pallas kernels, run_layer(): pl.pallas_call(layer_kernel, out_shape=[jax.ShapeDtypeStruct(s, d) for s,...  134 us
    pallas_call x1, Pallas kernels, run_grads(): pl.pallas_call(grad_kernel, out_shape=[jax.ShapeDtypeStruct(s, F32) for s...  63.5 us
    unnamed x56, local copies, waits for them, and re-layouts  19.8 us

profile of v1, /device:TPU:0, one launch (start us, length us, event | category | flops | bytes accessed | tf_op | source)
XLA Modules:
  0.0 222.0 jit_solution(18058990130246302282)
XLA Ops:
  0.7 0.1 pad.2.clone
  0.7 0.9 copy.40
  1.6 0.9 copy.41
  2.5 0.9 maximum_maximum_fusion.wba
  3.4 2.7 %copy.42 = bf16[1,1024,704]{2,1,0:T(8,128)(2,1)} copy(bf16[1,1024,704]{1,2,0:T(8,128)(2,1)} %param.37) | data formatting | bytes 2883584 | tf_op args[17]
  6.1 0.0 copy-done
  6.1 1.6 copy.43
  7.7 134.1 %layer.1 = (bf16[256,1024]{1,0:T(8,128)(2,1)}, bf16[256,1024]{1,0:T(8,128)(2,1)}, bf16[256,1024]{1,0:T(8,128)(2,1)}, bf16[256,1664]{1,0:T(8,128)(2,1)}, bf16[256...) custom-call(bf16[256,1024]{1,0:T(8,128)(2,1)} %bitcast.42, ...), custom_call_target="tpu_custom_call" | custom-call | tf_op jit(solution)/shard_map/layer/pallas_call | solution.py:580
  141.7 0.0 copy-start.2
  141.7 63.5 %grads.1 = (f32[64,256]{1,0:T(8,128)}, f32[64,256]{1,0:T(8,128)}, f32[64,512]{1,0:T(8,128)}, f32[64,2]{1,0:T(8,128)}, f32[64,2]{1,0:T(8,128)}, /*index=5*/f32[64...) custom-call(bf16[256,1024]{1,0:T(8,128)(2,1)} %get-tuple-element.51., ...), custom_call_target="tpu_custom_call" | custom-call | tf_op jit(solution)/shard_map/grads/pallas_call | solution.py:804
  205.3 0.0 copy-start.1
  205.3 1.5 copy.44
  206.7 1.4 copy.45
  208.1 1.8 copy.48
  209.9 1.9 copy.49
  211.8 0.0 copy-done.2
  211.8 0.0 copy-start.16
  211.8 0.0 copy-start.15
  211.8 0.0 copy-start.14
  211.8 0.0 copy-start.5
  211.8 0.0 copy-start.10
  211.8 0.0 copy-start.4
  211.8 0.0 copy-start.3
  211.8 0.8 copy.66
  212.6 0.0 copy-done.1
  212.6 0.8 copy.67
  213.4 0.0 copy-done.13
  213.4 0.6 copy.68
  214.0 0.0 copy-done.8
  214.0 0.6 copy.69
  214.7 0.0 copy-done.7
  214.7 0.6 copy.70
  215.3 0.0 copy-done.6
  215.3 0.7 copy.71
  215.9 0.0 copy-done.12
  216.0 0.6 copy.72
  216.5 0.0 copy-done.11
  216.5 0.6 copy.73
  217.1 0.6 copy.74
  217.7 0.5 copy.75
  218.3 0.5 copy.76
  218.8 0.6 copy.77
  219.4 0.7 copy.78
  220.0 0.6 copy.79
  220.6 0.0 copy-done.4
  220.6 0.7 copy.80
  221.3 0.0 copy-done.3
  221.3 0.7 copy.81
  (15 shorter events, 0.0 us)
Async XLA Ops:
  3.4 2.7 %copy-start = (bf16[1,1024,704]{1,2,0:T(8,128)(2,1)S(1)}, bf16[1,1024,704]{1,2,0:T(8,128)(2,1)}, u32[]{:S(2)}) copy-start(bf16[1,1024,704]{1,2,0:T(8,128)(2,1)} %param.38) | copy-start | bytes 4325380
  141.7 70.0 %copy-start.2 = (bf16[256,1024]{1,0:T(8,128)(2,1)S(1)}, bf16[256,1024]{1,0:T(8,128)(2,1)}, u32[]{:S(2)}) copy-start(bf16[256,1024]{1,0:T(8,128)(2,1)} %get-tuple-element.49) | copy-start | bytes 1572868
  205.3 7.3 %copy-start.1 = (bf16[256,1024]{1,0:T(8,128)(2,1)S(1)}, bf16[256,1024]{1,0:T(8,128)(2,1)}, u32[]{:S(2)}) copy-start(bf16[256,1024]{1,0:T(8,128)(2,1)} %get-tuple-element.50) | copy-start | bytes 1572868
  208.1 5.3 %copy-start.13 = (f32[1,1024]{1,0:T(1,128)S(1)}, f32[1,1024]{1,0:T(1,128)}, u32[]{:S(2)}) copy-start(f32[1,1024]{1,0:T(1,128)} %get-tuple-element.120) | copy-start | bytes 12292
  208.1 5.9 %copy-start.8 = (f32[64,256]{1,0:T(8,128)S(1)}, f32[64,256]{1,0:T(8,128)}, u32[]{:S(2)}) copy-start(f32[64,256]{1,0:T(8,128)} %get-tuple-element.61) | copy-start | bytes 196612
  209.9 4.8 %copy-start.7 = (f32[64,256]{1,0:T(8,128)S(1)}, f32[64,256]{1,0:T(8,128)}, u32[]{:S(2)}) copy-start(f32[64,256]{1,0:T(8,128)} %get-tuple-element.62) | copy-start | bytes 196612
  209.9 5.4 %copy-start.6 = (f32[64,512]{1,0:T(8,128)S(1)}, f32[64,512]{1,0:T(8,128)}, u32[]{:S(2)}) copy-start(f32[64,512]{1,0:T(8,128)} %get-tuple-element.63) | copy-start | bytes 393220
  211.8 4.2 %copy-start.12 = (f32[4,256]{1,0:T(4,128)S(1)}, f32[4,256]{1,0:T(4,128)}, u32[]{:S(2)}) copy-start(f32[4,256]{1,0:T(4,128)} %get-tuple-element.64) | copy-start | bytes 12292
  211.8 4.8 %copy-start.11 = (f32[4,256]{1,0:T(4,128)S(1)}, f32[4,256]{1,0:T(4,128)}, u32[]{:S(2)}) copy-start(f32[4,256]{1,0:T(4,128)} %get-tuple-element.65) | copy-start | bytes 12292
  211.8 5.4 %copy-start.9 = (f32[4,512]{1,0:T(4,128)S(1)}, f32[4,512]{1,0:T(4,128)}, u32[]{:S(2)}) copy-start(f32[4,512]{1,0:T(4,128)} %get-tuple-element.66) | copy-start | bytes 24580
  211.8 6.0 %copy-start.16 = (f32[1,2]{1,0:T(1,128)S(1)}, f32[1,2]{1,0:T(1,128)}, u32[]{:S(2)}) copy-start(f32[1,2]{1,0:T(1,128)} %get-tuple-element.129) | copy-start | bytes 28
  211.8 6.5 %copy-start.15 = (f32[1,2]{1,0:T(1,128)S(1)}, f32[1,2]{1,0:T(1,128)}, u32[]{:S(2)}) copy-start(f32[1,2]{1,0:T(1,128)} %get-tuple-element.130) | copy-start | bytes 28
  211.8 7.0 %copy-start.14 = (f32[1,512]{1,0:T(1,128)S(1)}, f32[1,512]{1,0:T(1,128)}, u32[]{:S(2)}) copy-start(f32[1,512]{1,0:T(1,128)} %get-tuple-element.131) | copy-start | bytes 6148
  211.8 7.6 %copy-start.5 = (f32[64,512]{1,0:T(8,128)S(1)}, f32[64,512]{1,0:T(8,128)}, u32[]{:S(2)}) copy-start(f32[64,512]{1,0:T(8,128)} %get-tuple-element.72) | copy-start | bytes 393220
  211.8 8.2 %copy-start.10 = (f32[1,1024]{1,0:T(1,128)S(1)}, f32[1,1024]{1,0:T(1,128)}, u32[]{:S(2)}) copy-start(f32[1,1024]{1,0:T(1,128)} %get-tuple-element.134) | copy-start | bytes 12292
  211.8 8.8 %copy-start.4 = (f32[64,704]{1,0:T(8,128)S(1)}, f32[64,704]{1,0:T(8,128)}, u32[]{:S(2)}) copy-start(f32[64,704]{1,0:T(8,128)} %get-tuple-element.75) | copy-start | bytes 540676
  211.8 9.5 %copy-start.3 = (f32[64,704]{1,0:T(8,128)S(1)}, f32[64,704]{1,0:T(8,128)}, u32[]{:S(2)}) copy-start(f32[64,704]{1,0:T(8,128)} %get-tuple-element.76) | copy-start | bytes 540676

commit v2 on v1

--- a/solution.py
+++ b/solution.py
@@ -99,13 +99,12 @@
 
 
 def layer_kernel(
-    inp, cot, g1, wq, wk, wv, cvq, cvk, cvv, wba, lrate, sbias, ogain, wgo, wo, g2, wfg, wfu, wfd,
+    inp, cot, g1, wq, wk, wv, cvq, cvk, cvv, wb, wd, lrate, sbias, ogain, wgo, wo, g2, wfg, wfu, wfd,
     hid, ing, a1, dpr, a2, dgu, dho, mix, dyo, act, small,
-    xbuf, ybuf, nbuf, hbuf, dbuf, gbuf,
-    part, r1, r2, fwd, hrow, drow, acc,
-    proj, zsum, qkv, gpre, onorm, dmix, upg, upu,
+    part, r1, r2, fwd, hopb, gbuf, xrow, hrow, drow,
+    proj, zsum, qkv, gpre, onorm, dmix, upg, upu, dact,
     tinv, amat, dmat, emat, umat, cols, gains,
-    rs_s, rs_r, ag_s, ag_r, hop_s, hop_r, ga_s, ga_r,
+    rs_s, rs_r, op_s, op_r, ag_s, ag_r, hop_s, hop_r, ga_s, ga_r,
 ):
     section = lax.axis_index("section")
     t = lax.axis_index("tensor")
@@ -114,6 +113,7 @@
     sib = hi * 2 + (1 - core)
     opp = (1 - hi) * 2 + core
     other = 1 - section
+    pieces = range(2)
 
     def remote(src, dst, ssem, rsem, device):
         return pltpu.make_async_remote_copy(
@@ -133,89 +133,98 @@
         )
     pl.semaphore_wait(barrier, 7)
 
-    def reduce_scatter(ph):
-        far = remote(
-            part.at[ph, 2 * (1 - hi) + 1 - core], r1.at[ph, 0], rs_s.at[ph, 0], rs_r.at[ph, 0],
-            {"tensor": sib},
-        )
-        near = remote(
-            part.at[ph, 2 * hi + 1 - core], r1.at[ph, 1], rs_s.at[ph, 1], rs_r.at[ph, 1],
-            {"tensor": sib},
-        )
-        far.start()
-        near.start()
-        far.wait_recv()
-        fwd[ph] = (part[ph, opp].astype(F32) + r1[ph, 0].astype(F32)).astype(BF16)
-        cross = remote(
-            fwd.at[ph], r2.at[ph], rs_s.at[ph, 2], rs_r.at[ph, 2], {"tensor": opp}
-        )
-        cross.start()
-        near.wait_recv()
-        acc[...] = part[ph, t].astype(F32) + r1[ph, 1].astype(F32)
-        cross.wait_recv()
-        total = acc[...] + r2[ph].astype(F32)
-        far.wait_send()
-        near.wait_send()
-        cross.wait_send()
-        return total
-
-    class Gather:
-        def __init__(self, buf, k):
-            self.far = remote(buf.at[t], buf.at[t], ag_s.at[k, 0], ag_r.at[k, 0], {"tensor": opp})
-            self.near = remote(buf.at[t], buf.at[t], ag_s.at[k, 1], ag_r.at[k, 1], {"tensor": sib})
-            self.pass_on = remote(
-                buf.at[opp], buf.at[opp], ag_s.at[k, 2], ag_r.at[k, 2], {"tensor": sib}
-            )
-
-        def start(self):
-            self.far.start()
-            self.near.start()
-
-        def middle(self):
-            self.far.wait_recv()
-            self.pass_on.start()
-
-        def finish(self):
-            self.near.wait_recv()
-            self.pass_on.wait_recv()
-            self.far.wait_send()
-            self.near.wait_send()
-            self.pass_on.wait_send()
-
-    def hop_send(buf, dst, k):
-        copies = [
-            remote(
-                buf.at[t], dst.at[t], hop_s.at[k, y], hop_r.at[k, hi],
-                {"section": other, "tensor": 2 * y + core},
-            )
+    def pair_sum(ph):
+        return [
+            remote(part.at[ph, 1 - core, p], r1.at[ph, p], rs_s.at[ph, p], rs_r.at[ph, p],
+                   {"tensor": sib})
+            for p in pieces
+        ]
+
+    def chip_swap(ph):
+        return [
+            remote(fwd.at[ph, p], r2.at[ph, p], op_s.at[ph, p], op_r.at[ph, p], {"tensor": opp})
+            for p in pieces
+        ]
+
+    def pair_share(k):
+        return [
+            remote(gbuf.at[k, core, p], gbuf.at[k, core, p], ag_s.at[k, p], ag_r.at[k, p],
+                   {"tensor": sib})
+            for p in pieces
+        ]
+
+    def started(copies):
+        for copy in copies:
+            copy.start()
+
+    def received(copies):
+        for copy in copies:
+            copy.wait_recv()
+
+    def sent(copies):
+        for copy in copies:
+            copy.wait_send()
+
+    def pair_total(ph, p):
+        return part[ph, core, p].astype(F32) + r1[ph, p].astype(F32)
+
+    def chip_total(ph, p):
+        return fwd[ph, p].astype(F32) + r2[ph, p].astype(F32)
+
+    def all_sum(ph, k, finish, between=None):
+        firsts, swaps, shares = pair_sum(ph), chip_swap(ph), pair_share(k)
+        started(firsts)
+        for p in pieces:
+            firsts[p].wait_recv()
+            fwd[ph, p] = pair_total(ph, p).astype(BF16)
+            swaps[p].start()
+        if between is not None:
+            between()
+        for p in pieces:
+            swaps[p].wait_recv()
+            gbuf[k, core, p] = finish(p, chip_total(ph, p)).astype(BF16)
+            shares[p].start()
+        received(shares)
+        sent(firsts + swaps + shares)
+
+    def hop_send(ph, k):
+        return [
+            remote(fwd.at[ph, p], hopb.at[k, hi, p], hop_s.at[k, y, p], hop_r.at[k, hi, p],
+                   {"section": other, "tensor": 2 * y + core})
+            for p in pieces
             for y in range(2)
         ]
-        for copy in copies:
-            copy.start()
-        for copy in copies:
-            copy.wait_send()
-
-    def hop_receive(dst, k):
-        passes = []
-        for y in range(2):
-            at = 2 * y + core
-            remote(
-                dst.at[at], dst.at[at], hop_s.at[k, y], hop_r.at[k, y],
-                {"section": other, "tensor": t},
-            ).wait_recv()
-            pass_on = remote(
-                dst.at[at], dst.at[at], hop_s.at[k, 2 + y], hop_r.at[k, 2 + y], {"tensor": sib}
-            )
-            pass_on.start()
-            passes.append(pass_on)
-        for pass_on in passes:
-            pass_on.wait_recv()
-        for pass_on in passes:
-            pass_on.wait_send()
+
+    def hop_receive(k, share, finish):
+        shares = pair_share(share)
+        for p in pieces:
+            for y in range(2):
+                remote(hopb.at[k, y, p], hopb.at[k, y, p], hop_s.at[k, y, p], hop_r.at[k, y, p],
+                       {"section": other, "tensor": t}).wait_recv()
+            value = (hopb[k, 0, p].astype(F32) + hopb[k, 1, p].astype(F32)).astype(BF16)
+            gbuf[share, core, p] = finish(p, value)
+            shares[p].start()
+        received(shares)
+        sent(shares)
 
     def put_part(ph, value):
-        for c in range(4):
-            part[ph, c] = value[ROWS * c : ROWS * (c + 1)].astype(BF16)
+        for s in range(2):
+            for p in pieces:
+                at = LEN * s + ROWS * p
+                part[ph, s, p] = value[at : at + ROWS].astype(BF16)
+
+    def spread(k, out):
+        for s in range(2):
+            for p in pieces:
+                at = LEN * s + ROWS * p
+                out[at : at + ROWS] = gbuf[k, s, p]
+
+    def piece(p):
+        return slice(ROWS * p, ROWS * (p + 1))
+
+    def normed(x, gain):
+        inv = lax.rsqrt(jnp.mean(x * x, axis=-1, keepdims=True) + 1e-06)
+        return (x * inv * gain).astype(BF16)
 
     pairs = [(s, h) for s in range(2) for h in range(HEADS)]
     row = lax.broadcasted_iota(jnp.int32, (LEN, LEN), 0)
@@ -247,21 +256,32 @@
     @pl.when(section == 0)
     def _():
         for c in range(4):
-            xbuf[c] = inp[ROWS * c : ROWS * (c + 1)]
+            at = slice(ROWS * c, ROWS * (c + 1))
+            a1[at] = normed(inp[at].astype(F32), gain1)
+        for p in pieces:
+            at = pl.multiple_of(core * LEN + ROWS * p, ROWS)
+            xrow[piece(p)] = inp[pl.ds(at, ROWS)].astype(F32)
+
+    def take_input(p, value):
+        x = value.astype(F32)
+        xrow[piece(p)] = x
+        return normed(x, gain1)
 
     @pl.when(section == 1)
     def _():
-        hop_receive(xbuf, 0)
-
-    for c in range(4):
-        x = xbuf[c].astype(F32)
-        inv = lax.rsqrt(jnp.mean(x * x, axis=-1, keepdims=True) + 1e-06)
-        a1[ROWS * c : ROWS * (c + 1)] = (x * inv * gain1).astype(BF16)
+        dyo[...] = cot[...]
+        dact[...] = dot_nt(cot[...], wfd[...])
+        hop_receive(0, 0, take_input)
+        spread(0, a1)
+
     source = a1[...]
     proj[:, PQ:PK] = dot(source, wq[...])
     proj[:, PK:PV] = dot(source, wk[...])
     proj[:, PV:PG] = dot(source, wv[...])
-    pba = dot(source, wba[...])
+    wba = jnp.concatenate(
+        [wb[...].astype(F32), wd[...].astype(F32), jnp.zeros((4, 1024), F32)], axis=0
+    ).astype(BF16)
+    pba = dot_nt(source, wba)
     gpre[...] = dot(source, wgo[...])
 
     lane = lax.broadcasted_iota(jnp.int32, (LEN, LEN), 1)
@@ -327,46 +347,51 @@
         mix[seq(s), hv(h)] = (on * ogains[:, hv(h)] * (gp * sigmoid(gp))).astype(BF16)
 
     put_part(0, dot(mix[...], wo[...]))
-    hrow[...] = xbuf[t].astype(F32) + reduce_scatter(0)
-    h_mine = hrow[...]
-    inv = lax.rsqrt(jnp.mean(h_mine * h_mine, axis=-1, keepdims=True) + 1e-06)
-    nbuf[t] = (h_mine * inv * gain2).astype(BF16)
-    gather = Gather(nbuf, 0)
-    gather.start()
-    gather.middle()
-    gather.finish()
-    for c in range(4):
-        a2[ROWS * c : ROWS * (c + 1)] = nbuf[c]
+
+    def take_middle(p, total):
+        h = xrow[piece(p)] + total
+        hrow[piece(p)] = h
+        return normed(h, gain2)
+
+    all_sum(0, 1, take_middle)
+    spread(1, a2)
     source = a2[...]
-    upg[...] = dot(source, wfg[...])
-    upu[...] = dot(source, wfu[...])
-    ug = upg[...]
-    s_act = (ug * sigmoid(ug) * upu[...]).astype(BF16)
-    act[:, 704:FPAD] = jnp.zeros((2 * LEN, FPAD - 704), BF16)
-    act[:, 0:704] = s_act
-    put_part(1, dot(s_act, wfd[...]))
-    ybuf[t] = (hrow[...] + reduce_scatter(1)).astype(BF16)
-    hidden = Gather(ybuf, 1)
+    upg[...] = dot_nt(source, wfg[...])
+    upu[...] = dot_nt(source, wfu[...])
+
+    outs = pair_sum(1)
+    out_swaps = chip_swap(1)
+
+    def output_part():
+        ug = upg[...]
+        s_act = (ug * sigmoid(ug) * upu[...]).astype(BF16)
+        act[:, 704:FPAD] = jnp.zeros((2 * LEN, FPAD - 704), BF16)
+        act[:, 0:704] = s_act
+        put_part(1, dot(s_act, wfd[...]))
+        started(outs)
+
+    def output_sum():
+        for p in pieces:
+            outs[p].wait_recv()
+            h = jnp.where(hi == 0, hrow[piece(p)], 0.0)
+            fwd[1, p] = (pair_total(1, p) + h).astype(BF16)
+
+    def take_cotangent(p, value):
+        return value
 
     @pl.when(section == 0)
     def _():
-        hop_send(ybuf, xbuf, 0)
-
-    hidden.start()
-
-    @pl.when(section == 1)
-    def _():
-        for c in range(4):
-            dbuf[c] = cot[ROWS * c : ROWS * (c + 1)]
-
-    @pl.when(section == 0)
-    def _():
-        hidden.middle()
-        hop_receive(dbuf, 1)
-
-    for c in range(4):
-        dyo[ROWS * c : ROWS * (c + 1)] = dbuf[c]
-    ds = dot_nt(dyo[...], wfd[...])
+        output_part()
+        output_sum()
+        hops = hop_send(1, 0)
+        started(hops)
+        sent(hops)
+        started(out_swaps)
+        hop_receive(1, 2, take_cotangent)
+        spread(2, dyo)
+        dact[...] = dot_nt(dyo[...], wfd[...])
+
+    ds = dact[...]
     ug = upg[...]
     uu = upu[...]
     sg = sigmoid(ug)
@@ -375,22 +400,27 @@
     dgu[:, FPAD + 704 :] = pad
     dgu[:, 0:704] = (ds * uu * (sg * (1.0 + ug * (1.0 - sg)))).astype(BF16)
     dgu[:, FPAD : FPAD + 704] = (ds * (ug * sg)).astype(BF16)
-    put_part(2, dot_nt(dgu[:, 0:704], wfg[...]) + dot_nt(dgu[:, FPAD : FPAD + 704], wfu[...]))
-    dn = reduce_scatter(2)
-    dz, dgain2 = rms_back(hrow[...], gain2, dn)
-    drow[...] = dbuf[t].astype(F32) + dz
-    hbuf[t] = drow[...].astype(BF16)
-    gather = Gather(hbuf, 2)
-    gather.start()
+    put_part(2, dot(dgu[:, 0:704], wfg[...]) + dot(dgu[:, FPAD : FPAD + 704], wfu[...]))
+
+    def take_gradient(p, total):
+        dz, dgain = rms_back(hrow[piece(p)], gain2, total)
+        at = pl.multiple_of(core * LEN + ROWS * p, ROWS)
+        dh = dyo[pl.ds(at, ROWS)].astype(F32) + dz
+        drow[piece(p)] = dh
+        gains[0, p] = dgain
+        return dh
+
+    def second_output():
+        pl.when(section == 1)(output_part)
+
+    all_sum(2, 3, take_gradient, second_output)
 
     @pl.when(section == 1)
     def _():
-        hidden.middle()
-
-    gather.middle()
-    gather.finish()
-    for c in range(4):
-        dho[ROWS * c : ROWS * (c + 1)] = hbuf[c]
+        output_sum()
+        started(out_swaps)
+
+    spread(3, dho)
     dmix[...] = dot_nt(dho[...], wo[...])
 
     small[...] = jnp.zeros_like(small)
@@ -500,20 +530,27 @@
     value = value + dot_nt(dpr[:, PK:PV], wk[...])
     value = value + dot_nt(dpr[:, PV:PG], wv[...])
     value = value + dot_nt(dpr[:, PG:PB], wgo[...])
-    value = value + dot_nt(dpr[:, PB:PEND], wba[...])
+    value = value + dot(dpr[:, PB:PEND][:, 0:8], wba)
     put_part(3, value)
-    dn = reduce_scatter(3)
-    dz, dgain1 = rms_back(xbuf[t].astype(F32), gain1, dn)
-    gbuf[t] = (drow[...] + dz).astype(BF16)
-    back = Gather(gbuf, 3)
+    firsts, swaps = pair_sum(3), chip_swap(3)
+    started(firsts)
+    dgain1 = jnp.zeros((1, 1024), F32)
+    for p in pieces:
+        firsts[p].wait_recv()
+        dz, dgain = rms_back(xrow[piece(p)], gain1, pair_total(3, p))
+        dgain1 = dgain1 + dgain
+        fwd[3, p] = (dz + jnp.where(hi == 0, drow[piece(p)], 0.0)).astype(BF16)
 
     @pl.when(section == 1)
     def _():
-        hop_send(gbuf, dbuf, 1)
-
-    back.start()
-    zero = jnp.zeros((6, 1024), F32)
-    gains[0] = jnp.concatenate([dgain1, dgain2, zero], axis=0)
+        hops = hop_send(3, 1)
+        started(hops)
+        sent(hops)
+
+    started(swaps)
+    dgain2 = jnp.where(hi == 0, gains[0, 0] + gains[0, 1], 0.0)
+    gains[0, 0] = dgain1
+    gains[0, 1] = dgain2
     sums = [
         remote(
             gains.at[0], gains.at[step], ga_s.at[step - 1], ga_r.at[step - 1],
@@ -521,21 +558,24 @@
         )
         for step in range(1, 4)
     ]
-    for copy in sums:
-        copy.start()
-    back.middle()
-    hidden.finish()
-    for c in range(4):
-        hid[ROWS * c : ROWS * (c + 1)] = ybuf[c]
-    for copy in sums:
-        copy.wait_recv()
-    total = gains[0] + gains[1] + gains[2] + gains[3]
-    small[0:2] = total[0:2]
-    back.finish()
-    for c in range(4):
-        ing[ROWS * c : ROWS * (c + 1)] = gbuf[c]
-    for copy in sums:
-        copy.wait_send()
+    started(sums)
+    hidden, back = pair_share(4), pair_share(5)
+    for p in pieces:
+        out_swaps[p].wait_recv()
+        gbuf[4, core, p] = chip_total(1, p).astype(BF16)
+        hidden[p].start()
+    for p in pieces:
+        swaps[p].wait_recv()
+        gbuf[5, core, p] = chip_total(3, p).astype(BF16)
+        back[p].start()
+    received(sums)
+    small[0:1] = (gains[0, 0] + gains[2, 0]) + (gains[1, 0] + gains[3, 0])
+    small[1:2] = (gains[0, 1] + gains[2, 1]) + (gains[1, 1] + gains[3, 1])
+    received(hidden)
+    spread(4, hid)
+    received(back)
+    spread(5, ing)
+    sent(outs + out_swaps + firsts + swaps + sums + hidden + back)
 
 
 def run_layer(args):
@@ -546,15 +586,17 @@
         ((tokens, 1024), BF16), ((tokens, 512), BF16), ((tokens, 1024), BF16),
         ((tokens, FPAD), BF16), ((8, 1024), F32),
     )
-    chunk = (4, ROWS, 1024)
-    buffers = [pltpu.VMEM(chunk, BF16)] * 6 + [
-        pltpu.VMEM((4,) + chunk, BF16),
-        pltpu.VMEM((4, 2, ROWS, 1024), BF16),
-        pltpu.VMEM((4, ROWS, 1024), BF16),
-        pltpu.VMEM((4, ROWS, 1024), BF16),
-        pltpu.VMEM((ROWS, 1024), F32),
-        pltpu.VMEM((ROWS, 1024), F32),
-        pltpu.VMEM((ROWS, 1024), F32),
+    rows = (2, ROWS, 1024)
+    buffers = [
+        pltpu.VMEM((4, 2) + rows, BF16),
+        pltpu.VMEM((4,) + rows, BF16),
+        pltpu.VMEM((4,) + rows, BF16),
+        pltpu.VMEM((4,) + rows, BF16),
+        pltpu.VMEM((2, 2) + rows, BF16),
+        pltpu.VMEM((6, 2) + rows, BF16),
+        pltpu.VMEM((LEN, 1024), F32),
+        pltpu.VMEM((LEN, 1024), F32),
+        pltpu.VMEM((LEN, 1024), F32),
         pltpu.VMEM((tokens, 1024), F32),
         pltpu.VMEM((tokens, 1024), F32),
         pltpu.VMEM((tokens, 1024), F32),
@@ -563,18 +605,20 @@
         pltpu.VMEM((tokens, 512), F32),
         pltpu.VMEM((tokens, 704), F32),
         pltpu.VMEM((tokens, 704), F32),
+        pltpu.VMEM((tokens, 704), F32),
         pltpu.VMEM((4, LEN, LEN), BF16),
         pltpu.VMEM((4, LEN, LEN), F32),
         pltpu.VMEM((4, LEN, LEN), F32),
         pltpu.VMEM((4, LEN, LEN), F32),
         pltpu.VMEM((4, LEN, DV), BF16),
         pltpu.VMEM((6, 4, LEN, LEN), F32),
-        pltpu.VMEM((4, 8, 1024), F32),
+        pltpu.VMEM((4, 2, 1, 1024), F32),
     ]
     sems = [
-        pltpu.SemaphoreType.DMA((4, 3)), pltpu.SemaphoreType.DMA((4, 3)),
-        pltpu.SemaphoreType.DMA((4, 3)), pltpu.SemaphoreType.DMA((4, 3)),
-        pltpu.SemaphoreType.DMA((2, 4)), pltpu.SemaphoreType.DMA((2, 4)),
+        pltpu.SemaphoreType.DMA((4, 2)), pltpu.SemaphoreType.DMA((4, 2)),
+        pltpu.SemaphoreType.DMA((4, 2)), pltpu.SemaphoreType.DMA((4, 2)),
+        pltpu.SemaphoreType.DMA((6, 2)), pltpu.SemaphoreType.DMA((6, 2)),
+        pltpu.SemaphoreType.DMA((2, 2, 2)), pltpu.SemaphoreType.DMA((2, 2, 2)),
         pltpu.SemaphoreType.DMA((3,)), pltpu.SemaphoreType.DMA((3,)),
     ]
     return pl.pallas_call(
@@ -592,11 +636,10 @@
 
 def grad_kernel(
     a1, dpr, a2, dgu, dho, mix, dyo, act, small,
-    gq, gk, gv, gb, gd, ggo, gout, gfg, gfu, gfd,
-    dg1, dcq, dck, dcv, dlr, dsb, dog, dg2,
+    gq, gk, gv, gb, gd, ggo, gout, gfg, gfu, gfd, gsmall,
     ga, gz, a1p, a1m, a2p, a2m, b1p, b1m, b2p, b2m,
     ha, hb, c1p, c1m, c2p, c2m, d1p, d1m, d2p, d2m,
-    sx, sz, send, recv, ssend, srecv,
+    sx, sz, a1t, a2t, dht, dyt, send, recv, ssend, srecv,
 ):
     place = lax.axis_index("dp")
     z = place // 4
@@ -619,32 +662,35 @@
         pl.semaphore_signal(barrier, inc=1, device_id=at_x(step), device_id_type=MESH)
         pl.semaphore_signal(barrier, inc=1, device_id=at_z(step), device_id_type=MESH)
 
-    def outer(left, right, width, store):
+    def turned(source, out):
         for rows in range(4):
-            lt = left[:, 256 * rows : 256 * (rows + 1)].T
-            for start in range(0, width, 256):
-                size = min(256, width - start)
-                value = jnp.dot(
-                    lt, right[:, start : start + size], preferred_element_type=F32
-                ).astype(BF16)
-                for part in range(4):
-                    store(rows, part, start, size, value[ROWS * part : ROWS * (part + 1)])
-
-    def into_a(offset):
-        def store(zz, xx, start, size, value):
-            ga[xx, zz, :, offset + start : offset + start + size] = value
-        return store
-
-    def into_b(offset):
-        def store(zz, xx, start, size, value):
-            gz[zz, xx, :, offset + start : offset + start + size] = value
-        return store
-
-    outer(a1, dpr, PEND, into_a(0))
-    outer(dho, mix, 512, into_a(PEND))
-    outer(a2, dgu, 2 * FPAD, into_b(0))
-    outer(dyo, act, FPAD, into_b(2 * FPAD))
-
+            flat = source[:, 256 * rows : 256 * (rows + 1)].T
+            for c in range(4):
+                out[rows, c] = flat[ROWS * c : ROWS * (c + 1)]
+
+    def outer(left, right, width, out, offset):
+        for start in range(0, width, 256):
+            size = min(256, width - start)
+            value = jnp.dot(
+                left, right[:, start : start + size], preferred_element_type=F32
+            ).astype(BF16)
+            for c in range(4):
+                out[c, :, offset + start : offset + start + size] = value[
+                    ROWS * c : ROWS * (c + 1)
+                ]
+
+    def chunk_a(c):
+        outer(a1t[:, c].reshape(256, 256), dpr, PEND, ga.at[c], 0)
+        outer(dht[:, c].reshape(256, 256), mix, 512, ga.at[c], PEND)
+
+    def chunk_b(c):
+        outer(a2t[c].reshape(256, 256), dgu, 2 * FPAD, gz.at[c], 0)
+        outer(dyt[c].reshape(256, 256), act, FPAD, gz.at[c], 2 * FPAD)
+
+    turned(a1, a1t)
+    turned(dho, dht)
+    turned(a2, a2t)
+    turned(dyo, dyt)
     pl.semaphore_wait(barrier, 6)
 
     class Ring:
@@ -663,9 +709,18 @@
             self.p3 = remote(g.at[right, lo], two_p.at[lo], send.at[k, 4], recv.at[k, 4], where(1))
             self.m3 = remote(g.at[left, up], two_m.at[up], send.at[k, 5], recv.at[k, 5], where(3))
 
-        def start(self):
-            for copy in (self.p1, self.m1, self.p2, self.m2):
-                copy.start()
+        def start(self, chunk=None):
+            for at, copies in (
+                ((self.me + 2) % 4, (self.p1, self.m1)),
+                (self.right, (self.p2,)),
+                (self.left, (self.m2,)),
+            ):
+                if chunk is not None:
+                    chunk(at)
+                for copy in copies:
+                    copy.start()
+            if chunk is not None:
+                chunk(self.me)
 
         def relay(self):
             one_p, one_m, two_p, two_m = self.bufs
@@ -706,15 +761,15 @@
     first_b = Ring(gz, z, at_z, (b1p, b1m, b2p, b2m), 1, 2)
     second_a = Ring(ha, z, at_z, (c1p, c1m, c2p, c2m), 2, 32)
     second_b = Ring(hb, x, at_x, (d1p, d1m, d2p, d2m), 3, 32)
-    first_a.start()
-    first_b.start()
+    first_a.start(chunk_a)
+    first_b.start(chunk_b)
     for copy in small_x:
         copy.start()
     first_a.relay()
     first_b.relay()
     for copy in small_x:
         copy.wait_recv()
-    sz[0] = sx[0] + sx[1] + sx[2] + sx[3]
+    sz[0] = (sx[0] + sx[2]) + (sx[1] + sx[3])
     for copy in small_z:
         copy.start()
 
@@ -737,15 +792,8 @@
     second_b.relay()
     for copy in small_z:
         copy.wait_recv()
-    sums = sz[0] + sz[1] + sz[2] + sz[3]
-    dg1[...] = sums[0:1]
-    dg2[...] = sums[1:2]
-    dcq[...] = sums[2:6, 0:256]
-    dck[...] = sums[2:6, 256:512]
-    dcv[...] = sums[2:6, 512:1024]
-    dog[...] = sums[6:7, 0:512]
-    dlr[...] = sums[6:7, 512:514]
-    dsb[...] = sums[6:7, 514:516]
+    sums = (sz[0] + sz[2]) + (sz[1] + sz[3])
+    gsmall[...] = sums
 
     def total(ring, start, size):
         _, _, two_p, two_m = ring.bufs
@@ -761,14 +809,14 @@
     gk[...] = total(second_a, PK, 256)
     gv[...] = total(second_a, PV, 512)
     ggo[...] = total(second_a, PG, 512)
-    pair = total(second_a, PB, 128)
-    gb[...] = pair[:, 0:2]
-    gd[...] = pair[:, 2:4]
-    gout[...] = total(second_a, PEND, 512).T
+    pair = total(second_a, PB, 128).T
+    gb[...] = pair[0:2]
+    gd[...] = pair[2:4]
+    gout[...] = total(second_a, PEND, 512)
     second_b.arrive()
     gfg[...] = total(second_b, 0, FPAD)[:, 0:704]
     gfu[...] = total(second_b, FPAD, FPAD)[:, 0:704]
-    gfd[...] = total(second_b, 2 * FPAD, FPAD).T[0:704]
+    gfd[...] = total(second_b, 2 * FPAD, FPAD)[:, 0:704]
     for ring in (first_a, first_b, second_a, second_b):
         ring.sent()
     for copy in small_x + small_z:
@@ -777,9 +825,8 @@
 
 def run_grads(args):
     results = (
-        (ROWS, 256), (ROWS, 256), (ROWS, 512), (ROWS, 2), (ROWS, 2), (ROWS, 512),
-        (512, ROWS), (ROWS, 704), (ROWS, 704), (704, ROWS),
-        (1, 1024), (4, 256), (4, 256), (4, 512), (1, 2), (1, 2), (1, 512), (1, 1024),
+        (ROWS, 256), (ROWS, 256), (ROWS, 512), (2, ROWS), (2, ROWS), (ROWS, 512),
+        (ROWS, 512), (ROWS, 704), (ROWS, 704), (ROWS, 704), (8, 1024),
     )
 
     def first(n):
@@ -796,6 +843,7 @@
         + second(NA)
         + second(NB)
         + [pltpu.VMEM((4, 8, 1024), F32)] * 2
+        + [pltpu.VMEM((4, 4, ROWS, 256), BF16)] * 4
     )
     sems = [
         pltpu.SemaphoreType.DMA((4, 6)), pltpu.SemaphoreType.DMA((4, 6)),
@@ -814,6 +862,39 @@
     )(*args)
 
 
+def result_kernel(*refs):
+    hid, ing, gq, gk, gv, gb, gd, ggo, gout, gfg, gfu, gfd, sums = refs[:13]
+    outs = refs[13:]
+    dg1, dcq, dck, dcv, dlr, dsb, dog, dg2 = outs[12:]
+    for source, out in zip((hid, ing, gq, gk, gv, gb, gd, ggo, gout, gfg, gfu, gfd), outs):
+        out[...] = source[...]
+    dg1[...] = sums[0:1]
+    dg2[...] = sums[1:2]
+    dcq[...] = sums[2:6, 0:256]
+    dck[...] = sums[2:6, 256:512]
+    dcv[...] = sums[2:6, 512:1024]
+    dog[...] = sums[6:7, 0:512]
+    dlr[...] = sums[6:7, 512:514]
+    dsb[...] = sums[6:7, 514:516]
+
+
+def run_results(args):
+    results = [(v.shape, v.dtype) for v in args[:12]] + [
+        (shape, F32)
+        for shape in (
+            (1, 1024), (4, 256), (4, 256), (4, 512), (1, 2), (1, 2), (1, 512), (1, 1024)
+        )
+    ]
+    return pl.pallas_call(
+        result_kernel,
+        out_shape=[jax.ShapeDtypeStruct(s, d) for s, d in results],
+        in_specs=[pl.BlockSpec(memory_space=pltpu.VMEM)] * len(args),
+        out_specs=[pl.BlockSpec(memory_space=pltpu.VMEM)] * len(results),
+        compiler_params=pltpu.CompilerParams(vmem_limit_bytes=32 * 1024 * 1024),
+        name="results",
+    )(*args)
+
+
 def per_device(
     inputs, cotangent, norm_gain1, w_query, w_key, w_value, conv_query, conv_key, conv_value,
     w_beta, w_decay, log_rate, step_bias, out_gain, w_gate_out, w_out, norm_gain2,
@@ -821,23 +902,23 @@
 ):
     tokens = 2 * LEN
     width = inputs.shape[-1]
-    wba = jnp.concatenate(
-        [w_beta[0], w_decay[0], jnp.zeros((width, LEN - 4), BF16)], axis=1
-    )
     out = run_layer((
         inputs.reshape(tokens, width), cotangent.reshape(tokens, width),
         norm_gain1, w_query[0], w_key[0], w_value[0],
-        conv_query[0], conv_key[0], conv_value[0], wba, log_rate, step_bias, out_gain,
-        w_gate_out[0], w_out[0], norm_gain2, w_ffn_gate[0], w_ffn_up[0], w_ffn_down[0],
+        conv_query[0], conv_key[0], conv_value[0], w_beta[0].T, w_decay[0].T,
+        log_rate, step_bias, out_gain, w_gate_out[0], w_out[0], norm_gain2,
+        w_ffn_gate[0].T, w_ffn_up[0].T, w_ffn_down[0],
     ))
-    hidden, input_grad = (v.reshape((1,) + inputs.shape) for v in out[:2])
-    (gq, gk, gv, gb, gd, ggo, gout, gfg, gfu, gfd, dg1, dcq, dck, dcv, dlr, dsb, dog, dg2) = (
-        run_grads(tuple(out[2:]))
-    )
+    grads = run_grads(tuple(out[2:]))
+    (
+        hidden, input_grad, gq, gk, gv, gb, gd, ggo, gout, gfg, gfu, gfd,
+        dg1, dcq, dck, dcv, dlr, dsb, dog, dg2,
+    ) = run_results(tuple(out[:2]) + tuple(grads))
+    shape = (1,) + inputs.shape
     return (
-        hidden, input_grad, dg1, gq[None], gk[None], gv[None], dcq[None], dck[None], dcv[None],
-        gb[None], gd[None], dlr, dsb, dog, ggo[None], gout[None], dg2,
-        gfg[None], gfu[None], gfd[None],
+        hidden.reshape(shape), input_grad.reshape(shape), dg1, gq[None], gk[None], gv[None],
+        dcq[None], dck[None], dcv[None], gb.T[None], gd.T[None], dlr, dsb, dog,
+        ggo[None], gout.T[None], dg2, gfg[None], gfu[None], gfd.T[None],
     )
 
 

time: 222 us -> 185 us (0.83)
  Pallas kernels: 198 us -> 175 us
  local copies, waits for them, and re-layouts: 22.7 us -> 9.17 us
    pallas_call x1, Pallas kernels: 134 us -> 109 us  [run_layer(): pl.pallas_call(layer_kernel, out_shape=[jax.ShapeDtypeStruct(s, d) for s,...]
    unnamed x56 -> x26, local copies, waits for them, and re-layouts: 19.8 us -> 9.17 us
    pallas_call x2 -> x0, local copies, waits for them, and re-layouts: 2.84 us -> none  [run_grads(): pl.pallas_call(grad_kernel, out_shape=[jax.ShapeDtypeStruct(s, F32) for s...]
where the time goes in v2:
time: 185 us
  Pallas kernels  175 us (95%)
  local copies, waits for them, and re-layouts  9.17 us (5%)
    pallas_call x1, Pallas kernels, run_layer(): pl.pallas_call(layer_kernel, out_shape=[jax.ShapeDtypeStruct(s, d) for s,...  109 us
    pallas_call x1, Pallas kernels, run_grads(): pl.pallas_call(grad_kernel, out_shape=[jax.ShapeDtypeStruct(s, F32) for s...  63.9 us
    unnamed x26, local copies, waits for them, and re-layouts  9.17 us

profile of v2, /device:TPU:0, one launch (start us, length us, event | category | flops | bytes accessed | tf_op | source)
XLA Modules:
  0.0 184.8 jit_solution(8278883504483588120)
XLA Ops:
  0.7 109.4 %layer.1 = (bf16[256,1024]{1,0:T(8,128)(2,1)}, bf16[256,1024]{1,0:T(8,128)(2,1)}, bf16[256,1024]{1,0:T(8,128)(2,1)}, bf16[256,1664]{1,0:T(8,128)(2,1)}, bf16[256...) custom-call(bf16[256,1024]{1,0:T(8,128)(2,1)} %bitcast.56, ...), custom_call_target="tpu_custom_call" | custom-call | tf_op jit(solution)/shard_map/layer/pallas_call | solution.py:624
  110.1 0.0 copy-start
  110.1 0.0 copy-start.1
  110.1 63.9 %grads.1 = (f32[64,256]{1,0:T(8,128)}, f32[64,256]{1,0:T(8,128)}, f32[64,512]{1,0:T(8,128)}, f32[2,64]{1,0:T(2,128)}, f32[2,64]{1,0:T(2,128)}, /*index=5*/f32[64...) custom-call(bf16[256,1024]{1,0:T(8,128)(2,1)} %get-tuple-element.64., ...), custom_call_target="tpu_custom_call" | custom-call | tf_op jit(solution)/shard_map/grads/pallas_call | solution.py:852
  174.0 0.0 copy-done
  174.0 0.0 copy-done.1
  174.1 0.0 copy-start.2
  174.1 0.9 copy-done.2
  175.0 0.0 copy-start.3
  175.0 0.9 copy-done.3
  175.9 0.0 copy-start.4
  175.9 0.9 copy-done.4
  176.8 0.0 copy-start.5
  176.8 0.9 copy-done.5
  177.7 0.0 copy-start.6
  177.7 0.9 copy-done.6
  178.6 0.0 copy-start.7
  178.6 0.9 copy-done.7
  179.6 0.0 copy-start.8
  179.6 0.8 copy-done.8
  180.4 0.0 copy-start.9
  180.4 0.8 copy-done.9
  181.2 0.0 copy-start.10
  181.2 0.8 copy-done.10
  182.0 0.0 copy-start.11
  182.0 0.6 copy-done.11
  182.6 0.0 copy-start.12
  182.6 0.6 copy-done.12
  183.2 1.4 results.1
Async XLA Ops:
  110.1 63.9 %copy-start = (bf16[256,1024]{1,0:T(8,128)(2,1)S(1)}, bf16[256,1024]{1,0:T(8,128)(2,1)}, u32[]{:S(2)}) copy-start(bf16[256,1024]{1,0:T(8,128)(2,1)} %get-tuple-element.62.refs_0_) | copy-start | bytes 1572868
  110.1 63.9 %copy-start.1 = (bf16[256,1024]{1,0:T(8,128)(2,1)S(1)}, bf16[256,1024]{1,0:T(8,128)(2,1)}, u32[]{:S(2)}) copy-start(bf16[256,1024]{1,0:T(8,128)(2,1)} %get-tuple-element.63.refs_1_) | copy-start | bytes 1572868
  174.1 0.9 copy-start.2
  175.0 0.9 copy-start.3
  175.9 0.9 copy-start.4
  176.8 0.9 copy-start.5
  177.7 0.9 copy-start.6
  178.6 0.9 copy-start.7
  179.6 0.8 copy-start.8
  180.4 0.8 copy-start.9
  181.2 0.8 copy-start.10
  182.0 0.6 copy-start.11
  182.6 0.6 copy-start.12

commit v3 on v2

--- a/solution.py
+++ b/solution.py
@@ -1,5 +1,3 @@
-import functools
-
 import jax
 import jax.numpy as jnp
 from jax import lax
@@ -18,8 +16,9 @@
 SCALE = DK**-0.5
 PQ, PK, PV, PG, PB, PEND = 0, 256, 512, 1024, 1536, 1664
 FPAD = 768
-NA = PEND + 512
-NB = 3 * FPAD
+NF = FPAD + FPAD // 2
+NQ = PV + (PEND - PB) + 512
+NV = PB - PV
 
 
 def dot(left, right):
@@ -98,13 +97,259 @@
     return dz, jnp.sum(dn * hat, axis=0, keepdims=True)
 
 
+def torus_steps(place):
+    z = place // 4
+    x = place % 4
+    along_x = [{"dp": z * 4 + (x + step) % 4} for step in range(1, 4)]
+    along_z = [{"dp": ((z + step) % 4) * 4 + x} for step in range(1, 4)]
+    return along_x + along_z
+
+
+def turned(source, out):
+    for rows in range(4):
+        flat = source[:, 256 * rows : 256 * (rows + 1)].T
+        for c in range(4):
+            out[rows, c] = flat[ROWS * c : ROWS * (c + 1)]
+
+
+def add_into(ref, more):
+    if len(more.shape) == 3:
+        @pl.loop(0, more.shape[0])
+        def _(c):
+            ref[c] = (ref[c].astype(F32) + more[c].astype(F32)).astype(BF16)
+    else:
+        ref[...] = (ref[...].astype(F32) + more[...].astype(F32)).astype(BF16)
+
+
+class Ring:
+    def __init__(self, remote, g, me, devices, bufs, send, recv, half):
+        one_p, one_m, two_p, two_m = bufs
+        after, _, before = devices
+        self.g, self.me, self.bufs = g, me, bufs
+        self.right = right = (me + 1) % 4
+        self.left = left = (me + 3) % 4
+        self.far = far = (me + 2) % 4
+        lo, up = pl.ds(0, half), pl.ds(half, half)
+        self.lo, self.up = lo, up
+        self.p1 = remote(g.at[far, lo], one_p, send.at[0], recv.at[0], after)
+        self.m1 = remote(g.at[far, up], one_m, send.at[1], recv.at[1], before)
+        self.p2 = remote(g.at[right, up], two_p.at[up], send.at[2], recv.at[2], after)
+        self.m2 = remote(g.at[left, lo], two_m.at[lo], send.at[3], recv.at[3], before)
+        self.p3 = remote(g.at[right, lo], two_p.at[lo], send.at[4], recv.at[4], after)
+        self.m3 = remote(g.at[left, up], two_m.at[up], send.at[5], recv.at[5], before)
+        self.steps = ((far, (self.p1, self.m1)), (right, (self.p2,)), (left, (self.m2,)))
+
+    def start(self):
+        for _, copies in self.steps:
+            for copy in copies:
+                copy.start()
+
+    def relay(self):
+        one_p, one_m, _, _ = self.bufs
+        self.p1.wait_recv()
+        add_into(self.g.at[self.right, self.lo], one_p)
+        self.p3.start()
+        self.m1.wait_recv()
+        add_into(self.g.at[self.left, self.up], one_m)
+        self.m3.start()
+
+    def arrive(self):
+        for copy in (self.p2, self.m2, self.p3, self.m3):
+            copy.wait_recv()
+
+    def sent(self):
+        for copy in (self.p1, self.m1, self.p2, self.m2, self.p3, self.m3):
+            copy.wait_send()
+
+    def merge(self, out):
+        _, _, two_p, two_m = self.bufs
+
+        @pl.loop(0, 4)
+        def _(c):
+            out[c] = (
+                self.g[self.me, c].astype(F32) + two_p[c].astype(F32) + two_m[c].astype(F32)
+            ).astype(BF16)
+
+    def total(self, start, size):
+        _, _, two_p, two_m = self.bufs
+        at = slice(start, start + size)
+        return (
+            self.g[self.me, :, at].astype(F32)
+            + two_p[:, at].astype(F32)
+            + two_m[:, at].astype(F32)
+        )
+
+
+WIDTHS = (NF, NF, NQ, NV)
+
+
+def sum_scratch():
+    scratch = []
+    for n in WIDTHS:
+        scratch.append(pltpu.VMEM((4, 4, ROWS, n), BF16))
+        scratch += [pltpu.VMEM((2, ROWS, n), BF16)] * 2 + [pltpu.VMEM((4, ROWS, n), BF16)] * 3
+        scratch += [pltpu.VMEM((ROWS // 2, n), BF16)] * 2 + [pltpu.VMEM((ROWS, n), BF16)] * 2
+    scratch += [pltpu.VMEM((4, 8, 1024), F32)] * 2
+    scratch += [pltpu.SemaphoreType.DMA((8, 6))] * 2 + [pltpu.SemaphoreType.DMA((6,))] * 2
+    return scratch
+
+
+class Sums:
+    def __init__(self, place, remote, data, outs, refs):
+        self.data, self.outs = data, outs
+        z, x = place // 4, place % 4
+        steps = torus_steps(place)
+        ways = ((x, steps[:3]), (z, steps[3:]))
+        self.sx, self.sz, send, recv, ssend, srecv = refs[-6:]
+        self.first, self.second, self.half = [], [], []
+        for k in range(4):
+            g, one_p, one_m, two_p, two_m, h, a, b, c, d = refs[10 * k : 10 * k + 10]
+            me, way = ways[k % 2]
+            self.first.append(
+                Ring(remote, g, me, way, (one_p, one_m, two_p, two_m), send.at[k], recv.at[k], 2)
+            )
+            me, way = ways[1 - k % 2]
+            self.second.append(
+                Ring(remote, h, me, way, (a, b, c, d), send.at[4 + k], recv.at[4 + k], ROWS // 2)
+            )
+        self.small_x = [
+            remote(self.sx.at[0], self.sx.at[i + 1], ssend.at[i], srecv.at[i], steps[i])
+            for i in range(3)
+        ]
+        self.small_z = [
+            remote(self.sz.at[0], self.sz.at[i + 1], ssend.at[3 + i], srecv.at[3 + i], steps[3 + i])
+            for i in range(3)
+        ]
+
+    def chunk(self, k, c):
+        data = self.data
+        out = self.first[k].g.at[c]
+
+        def outer(left, right, first, width, offset):
+            rows = left[:, c] if k % 2 == 0 else left[c]
+            flat = rows.reshape(4 * ROWS, 2 * LEN)
+            for start in range(0, width, 256):
+                size = min(256, width - start)
+                value = jnp.dot(
+                    flat, right[:, first + start : first + start + size],
+                    preferred_element_type=F32,
+                ).astype(BF16)
+                for i in range(4):
+                    out[i, :, offset + start : offset + start + size] = value[
+                        ROWS * i : ROWS * (i + 1)
+                    ]
+
+        if k < 2:
+            outer(data["a2"], data["pair"], FPAD * k, FPAD, 0)
+            outer(data["dy"], data["act"], FPAD // 2 * k, FPAD // 2, FPAD)
+        elif k == 2:
+            outer(data["a1"], data["proj"], PQ, PV, 0)
+            outer(data["a1"], data["proj"], PB, PEND - PB, PV)
+            outer(data["dh"], data["mix"], 0, 512, PV + PEND - PB)
+        else:
+            outer(data["a1"], data["proj"], PV, PB - PV, 0)
+
+    def begin(self, groups):
+        for step in range(3):
+            for k in groups:
+                at, copies = self.first[k].steps[step]
+                self.chunk(k, at)
+                for copy in copies:
+                    copy.start()
+        for k in groups:
+            self.chunk(k, self.first[k].me)
+
+    def merge(self, groups):
+        for k in groups:
+            self.first[k].arrive()
+            self.first[k].merge(self.second[k].g)
+            self.second[k].start()
+
+    def ffn_start(self):
+        self.begin((0, 1))
+
+    def ffn_relay(self):
+        self.first[0].relay()
+        self.first[1].relay()
+
+    def ffn_merge(self):
+        self.merge((0, 1))
+
+    def ffn_relay_second(self):
+        self.second[0].relay()
+        self.second[1].relay()
+
+    def ffn_finish(self):
+        one, two, outs = self.second[0], self.second[1], self.outs
+        one.arrive()
+        outs["fg"][...] = one.total(0, FPAD)[:, 0:704]
+        outs["fd"][:, 0:384] = one.total(FPAD, 384)
+        two.arrive()
+        outs["fu"][...] = two.total(0, FPAD)[:, 0:704]
+        outs["fd"][:, 384:704] = two.total(FPAD, 384)[:, 0:320]
+
+    def mix_start(self):
+        self.begin((2, 3))
+
+    def mix_relay(self):
+        self.first[2].relay()
+        self.first[3].relay()
+
+    def mix_merge(self):
+        self.merge((2, 3))
+
+    def mix_relay_second(self):
+        self.second[2].relay()
+        self.second[3].relay()
+
+    def mix_finish(self):
+        one, two, outs = self.second[2], self.second[3], self.outs
+        one.arrive()
+        outs["q"][...] = one.total(0, 256)
+        outs["k"][...] = one.total(256, 256)
+        both = one.total(PV, PEND - PB).T
+        outs["b"][...] = both[0:2]
+        outs["d"][...] = both[2:4]
+        outs["out"][...] = one.total(PV + PEND - PB, 512)
+        two.arrive()
+        outs["v"][...] = two.total(0, 512)
+        outs["go"][...] = two.total(512, 512)
+
+    def small_start(self, small):
+        self.sx[0] = small[...]
+        for copy in self.small_x:
+            copy.start()
+
+    def small_relay(self):
+        sx = self.sx
+        for copy in self.small_x:
+            copy.wait_recv()
+        self.sz[0] = (sx[0] + sx[2]) + (sx[1] + sx[3])
+        for copy in self.small_z:
+            copy.start()
+
+    def small_finish(self):
+        sz = self.sz
+        for copy in self.small_z:
+            copy.wait_recv()
+        self.outs["small"][...] = (sz[0] + sz[2]) + (sz[1] + sz[3])
+
+    def sent(self):
+        for ring in self.first + self.second:
+            ring.sent()
+        for copy in self.small_x + self.small_z:
+            copy.wait_send()
+
+
 def layer_kernel(
     inp, cot, g1, wq, wk, wv, cvq, cvk, cvv, wb, wd, lrate, sbias, ogain, wgo, wo, g2, wfg, wfu, wfd,
-    hid, ing, a1, dpr, a2, dgu, dho, mix, dyo, act, small,
+    hid, ing, gq, gk, gv, gb, gd, ggo, gout, gfg, gfu, gfd, gsmall,
+    a1, dpr, a2, dgu, dho, mix, dyo, act, small, a1t, a2t, dht, dyt,
     part, r1, r2, fwd, hopb, gbuf, xrow, hrow, drow,
-    proj, zsum, qkv, gpre, onorm, dmix, upg, upu, dact,
-    tinv, amat, dmat, emat, umat, cols, gains,
+    proj, zsum, qkv, gpre, onorm, upg, upu, dact,
+    tinv, amat, dmat, emat, umat, cols, gains, dg2s,
     rs_s, rs_r, op_s, op_r, ag_s, ag_r, hop_s, hop_r, ga_s, ga_r,
+    *sum_refs,
 ):
     section = lax.axis_index("section")
     t = lax.axis_index("tensor")
@@ -131,7 +376,18 @@
             barrier, inc=1, device_id={"section": other, "tensor": (t + step) % 4},
             device_id_type=MESH,
         )
-    pl.semaphore_wait(barrier, 7)
+    place = lax.axis_index("dp")
+    links = torus_steps(place)
+    for device in links:
+        pl.semaphore_signal(barrier, inc=1, device_id=device, device_id_type=MESH)
+    pl.semaphore_wait(barrier, 7 + len(links))
+
+    grads = Sums(
+        place, remote,
+        dict(a1=a1t, a2=a2t, dh=dht, dy=dyt, proj=dpr, pair=dgu, mix=mix, act=act),
+        dict(q=gq, k=gk, v=gv, b=gb, d=gd, go=ggo, out=gout, fg=gfg, fu=gfu, fd=gfd, small=gsmall),
+        sum_refs,
+    )
 
     def pair_sum(ph):
         return [
@@ -271,6 +527,7 @@
     def _():
         dyo[...] = cot[...]
         dact[...] = dot_nt(cot[...], wfd[...])
+        turned(dyo, dyt)
         hop_receive(0, 0, take_input)
         spread(0, a1)
 
@@ -387,6 +644,8 @@
         started(hops)
         sent(hops)
         started(out_swaps)
+        turned(a1, a1t)
+        turned(a2, a2t)
         hop_receive(1, 2, take_cotangent)
         spread(2, dyo)
         dact[...] = dot_nt(dyo[...], wfd[...])
@@ -407,11 +666,21 @@
         at = pl.multiple_of(core * LEN + ROWS * p, ROWS)
         dh = dyo[pl.ds(at, ROWS)].astype(F32) + dz
         drow[piece(p)] = dh
-        gains[0, p] = dgain
+        dg2s[p] = dgain
         return dh
 
     def second_output():
-        pl.when(section == 1)(output_part)
+        @pl.when(section == 1)
+        def _():
+            output_part()
+            turned(a1, a1t)
+            turned(a2, a2t)
+
+        @pl.when(section == 0)
+        def _():
+            turned(dyo, dyt)
+
+        grads.ffn_start()
 
     all_sum(2, 3, take_gradient, second_output)
 
@@ -421,13 +690,14 @@
         started(out_swaps)
 
     spread(3, dho)
-    dmix[...] = dot_nt(dho[...], wo[...])
+    dact[:, 0:512] = dot_nt(dho[...], wo[...])
+    grads.ffn_relay()
 
     small[...] = jnp.zeros_like(small)
     douts = [jnp.zeros((1, DV), F32) for _ in range(HEADS)]
     dos = []
     for i, (s, h) in enumerate(pairs):
-        dm = dmix[seq(s), hv(h)]
+        dm = dact[seq(s), hv(h)]
         gp = gpre[seq(s), hv(h)]
         sg = sigmoid(gp)
         on = onorm[seq(s), hv(h)]
@@ -526,6 +796,11 @@
         dpr[seq(s), PB:PEND] = block.astype(BF16)
     small[6:7, 512:640] = scal
 
+    def mixer_grads():
+        turned(dho, dht)
+        grads.mix_start()
+
+    pl.when(section == 0)(mixer_grads)
     value = dot_nt(dpr[:, PQ:PK], wq[...])
     value = value + dot_nt(dpr[:, PK:PV], wk[...])
     value = value + dot_nt(dpr[:, PV:PG], wv[...])
@@ -540,17 +815,17 @@
         dz, dgain = rms_back(xrow[piece(p)], gain1, pair_total(3, p))
         dgain1 = dgain1 + dgain
         fwd[3, p] = (dz + jnp.where(hi == 0, drow[piece(p)], 0.0)).astype(BF16)
+    gains[0, 0] = dgain1
+    gains[0, 1] = jnp.where(hi == 0, dg2s[0] + dg2s[1], 0.0)
 
     @pl.when(section == 1)
     def _():
         hops = hop_send(3, 1)
         started(hops)
+        mixer_grads()
         sent(hops)
 
     started(swaps)
-    dgain2 = jnp.where(hi == 0, gains[0, 0] + gains[0, 1], 0.0)
-    gains[0, 0] = dgain1
-    gains[0, 1] = dgain2
     sums = [
         remote(
             gains.at[0], gains.at[step], ga_s.at[step - 1], ga_r.at[step - 1],
@@ -564,6 +839,8 @@
         out_swaps[p].wait_recv()
         gbuf[4, core, p] = chip_total(1, p).astype(BF16)
         hidden[p].start()
+    grads.ffn_merge()
+    grads.mix_relay()
     for p in pieces:
         swaps[p].wait_recv()
         gbuf[5, core, p] = chip_total(3, p).astype(BF16)
@@ -571,23 +848,35 @@
     received(sums)
     small[0:1] = (gains[0, 0] + gains[2, 0]) + (gains[1, 0] + gains[3, 0])
     small[1:2] = (gains[0, 1] + gains[2, 1]) + (gains[1, 1] + gains[3, 1])
+    grads.small_start(small)
+    grads.ffn_relay_second()
     received(hidden)
     spread(4, hid)
     received(back)
     spread(5, ing)
+    grads.mix_merge()
+    grads.small_relay()
+    grads.ffn_finish()
+    grads.mix_relay_second()
+    grads.small_finish()
+    grads.mix_finish()
     sent(outs + out_swaps + firsts + swaps + sums + hidden + back)
+    grads.sent()
 
 
 def run_layer(args):
     tokens = 2 * LEN
-    results = (
-        ((tokens, 1024), BF16), ((tokens, 1024), BF16), ((tokens, 1024), BF16),
-        ((tokens, PEND), BF16), ((tokens, 1024), BF16), ((tokens, 2 * FPAD), BF16),
-        ((tokens, 1024), BF16), ((tokens, 512), BF16), ((tokens, 1024), BF16),
-        ((tokens, FPAD), BF16), ((8, 1024), F32),
-    )
+    results = [((tokens, 1024), BF16)] * 2 + [
+        (shape, F32)
+        for shape in (
+            (ROWS, 256), (ROWS, 256), (ROWS, 512), (2, ROWS), (2, ROWS), (ROWS, 512),
+            (ROWS, 512), (ROWS, 704), (ROWS, 704), (ROWS, 704), (8, 1024),
+        )
+    ]
     rows = (2, ROWS, 1024)
     buffers = [
+        pltpu.VMEM((tokens, n), BF16) for n in (1024, PEND, 1024, 2 * FPAD, 1024, 512, 1024, FPAD)
+    ] + [pltpu.VMEM((8, 1024), F32)] + [pltpu.VMEM((4, 4, ROWS, 256), BF16)] * 4 + [
         pltpu.VMEM((4, 2) + rows, BF16),
         pltpu.VMEM((4,) + rows, BF16),
         pltpu.VMEM((4,) + rows, BF16),
@@ -602,7 +891,6 @@
         pltpu.VMEM((tokens, 1024), F32),
         pltpu.VMEM((tokens, 512), F32),
         pltpu.VMEM((tokens, 512), F32),
-        pltpu.VMEM((tokens, 512), F32),
         pltpu.VMEM((tokens, 704), F32),
         pltpu.VMEM((tokens, 704), F32),
         pltpu.VMEM((tokens, 704), F32),
@@ -613,6 +901,7 @@
         pltpu.VMEM((4, LEN, DV), BF16),
         pltpu.VMEM((6, 4, LEN, LEN), F32),
         pltpu.VMEM((4, 2, 1, 1024), F32),
+        pltpu.VMEM((2, 1, 1024), F32),
     ]
     sems = [
         pltpu.SemaphoreType.DMA((4, 2)), pltpu.SemaphoreType.DMA((4, 2)),
@@ -626,239 +915,11 @@
         out_shape=[jax.ShapeDtypeStruct(s, d) for s, d in results],
         in_specs=[pl.BlockSpec(memory_space=pltpu.VMEM)] * len(args),
         out_specs=[pl.BlockSpec(memory_space=pltpu.VMEM)] * len(results),
-        scratch_shapes=buffers + sems,
+        scratch_shapes=buffers + sems + sum_scratch(),
         compiler_params=pltpu.CompilerParams(
-            collective_id=0, has_side_effects=True, vmem_limit_bytes=58 * 1024 * 1024
+            collective_id=0, has_side_effects=True, vmem_limit_bytes=61 * 1024 * 1024
         ),
         name="layer",
-    )(*args)
-
-
-def grad_kernel(
-    a1, dpr, a2, dgu, dho, mix, dyo, act, small,
-    gq, gk, gv, gb, gd, ggo, gout, gfg, gfu, gfd, gsmall,
-    ga, gz, a1p, a1m, a2p, a2m, b1p, b1m, b2p, b2m,
-    ha, hb, c1p, c1m, c2p, c2m, d1p, d1m, d2p, d2m,
-    sx, sz, a1t, a2t, dht, dyt, send, recv, ssend, srecv,
-):
-    place = lax.axis_index("dp")
-    z = place // 4
-    x = place % 4
-
-    def at_x(step):
-        return {"dp": z * 4 + (x + step) % 4}
-
-    def at_z(step):
-        return {"dp": ((z + step) % 4) * 4 + x}
-
-    def remote(src, dst, ssem, rsem, device):
-        return pltpu.make_async_remote_copy(
-            src_ref=src, dst_ref=dst, send_sem=ssem, recv_sem=rsem,
-            device_id=device, device_id_type=MESH,
-        )
-
-    barrier = pltpu.get_barrier_semaphore()
-    for step in range(1, 4):
-        pl.semaphore_signal(barrier, inc=1, device_id=at_x(step), device_id_type=MESH)
-        pl.semaphore_signal(barrier, inc=1, device_id=at_z(step), device_id_type=MESH)
-
-    def turned(source, out):
-        for rows in range(4):
-            flat = source[:, 256 * rows : 256 * (rows + 1)].T
-            for c in range(4):
-                out[rows, c] = flat[ROWS * c : ROWS * (c + 1)]
-
-    def outer(left, right, width, out, offset):
-        for start in range(0, width, 256):
-            size = min(256, width - start)
-            value = jnp.dot(
-                left, right[:, start : start + size], preferred_element_type=F32
-            ).astype(BF16)
-            for c in range(4):
-                out[c, :, offset + start : offset + start + size] = value[
-                    ROWS * c : ROWS * (c + 1)
-                ]
-
-    def chunk_a(c):
-        outer(a1t[:, c].reshape(256, 256), dpr, PEND, ga.at[c], 0)
-        outer(dht[:, c].reshape(256, 256), mix, 512, ga.at[c], PEND)
-
-    def chunk_b(c):
-        outer(a2t[c].reshape(256, 256), dgu, 2 * FPAD, gz.at[c], 0)
-        outer(dyt[c].reshape(256, 256), act, FPAD, gz.at[c], 2 * FPAD)
-
-    turned(a1, a1t)
-    turned(dho, dht)
-    turned(a2, a2t)
-    turned(dyo, dyt)
-    pl.semaphore_wait(barrier, 6)
-
-    class Ring:
-        def __init__(self, g, me, where, bufs, k, half):
-            one_p, one_m, two_p, two_m = bufs
-            self.g, self.me, self.bufs, self.half = g, me, bufs, half
-            self.right = right = (me + 1) % 4
-            self.left = left = (me + 3) % 4
-            far = (me + 2) % 4
-            lo, up = pl.ds(0, half), pl.ds(half, half)
-            self.lo, self.up = lo, up
-            self.p1 = remote(g.at[far, lo], one_p, send.at[k, 0], recv.at[k, 0], where(1))
-            self.m1 = remote(g.at[far, up], one_m, send.at[k, 1], recv.at[k, 1], where(3))
-            self.p2 = remote(g.at[right, up], two_p.at[up], send.at[k, 2], recv.at[k, 2], where(1))
-            self.m2 = remote(g.at[left, lo], two_m.at[lo], send.at[k, 3], recv.at[k, 3], where(3))
-            self.p3 = remote(g.at[right, lo], two_p.at[lo], send.at[k, 4], recv.at[k, 4], where(1))
-            self.m3 = remote(g.at[left, up], two_m.at[up], send.at[k, 5], recv.at[k, 5], where(3))
-
-        def start(self, chunk=None):
-            for at, copies in (
-                ((self.me + 2) % 4, (self.p1, self.m1)),
-                (self.right, (self.p2,)),
-                (self.left, (self.m2,)),
-            ):
-                if chunk is not None:
-                    chunk(at)
-                for copy in copies:
-                    copy.start()
-            if chunk is not None:
-                chunk(self.me)
-
-        def relay(self):
-            one_p, one_m, two_p, two_m = self.bufs
-            g, lo, up = self.g, self.lo, self.up
-            self.p1.wait_recv()
-            add_into(g.at[self.right, lo], one_p)
-            self.p3.start()
-            self.m1.wait_recv()
-            add_into(g.at[self.left, up], one_m)
-            self.m3.start()
-
-        def arrive(self):
-            for copy in (self.p2, self.m2, self.p3, self.m3):
-                copy.wait_recv()
-
-        def sent(self):
-            for copy in (self.p1, self.m1, self.p2, self.m2, self.p3, self.m3):
-                copy.wait_send()
-
-    def add_into(ref, other):
-        if len(other.shape) == 3:
-            @pl.loop(0, other.shape[0])
-            def _(c):
-                ref[c] = (ref[c].astype(F32) + other[c].astype(F32)).astype(BF16)
-        else:
-            ref[...] = (ref[...].astype(F32) + other[...].astype(F32)).astype(BF16)
-
-    sx[0] = small[...]
-    small_x = [
-        remote(sx.at[0], sx.at[step], ssend.at[step - 1], srecv.at[step - 1], at_x(step))
-        for step in range(1, 4)
-    ]
-    small_z = [
-        remote(sz.at[0], sz.at[step], ssend.at[step + 2], srecv.at[step + 2], at_z(step))
-        for step in range(1, 4)
-    ]
-    first_a = Ring(ga, x, at_x, (a1p, a1m, a2p, a2m), 0, 2)
-    first_b = Ring(gz, z, at_z, (b1p, b1m, b2p, b2m), 1, 2)
-    second_a = Ring(ha, z, at_z, (c1p, c1m, c2p, c2m), 2, 32)
-    second_b = Ring(hb, x, at_x, (d1p, d1m, d2p, d2m), 3, 32)
-    first_a.start(chunk_a)
-    first_b.start(chunk_b)
-    for copy in small_x:
-        copy.start()
-    first_a.relay()
-    first_b.relay()
-    for copy in small_x:
-        copy.wait_recv()
-    sz[0] = (sx[0] + sx[2]) + (sx[1] + sx[3])
-    for copy in small_z:
-        copy.start()
-
-    def merge(ring, out):
-        _, _, two_p, two_m = ring.bufs
-
-        @pl.loop(0, 4)
-        def _(c):
-            out[c] = (
-                ring.g[ring.me, c].astype(F32) + two_p[c].astype(F32) + two_m[c].astype(F32)
-            ).astype(BF16)
-
-    first_a.arrive()
-    merge(first_a, ha)
-    second_a.start()
-    first_b.arrive()
-    merge(first_b, hb)
-    second_b.start()
-    second_a.relay()
-    second_b.relay()
-    for copy in small_z:
-        copy.wait_recv()
-    sums = (sz[0] + sz[2]) + (sz[1] + sz[3])
-    gsmall[...] = sums
-
-    def total(ring, start, size):
-        _, _, two_p, two_m = ring.bufs
-        at = slice(start, start + size)
-        return (
-            ring.g[ring.me, :, at].astype(F32)
-            + two_p[:, at].astype(F32)
-            + two_m[:, at].astype(F32)
-        )
-
-    second_a.arrive()
-    gq[...] = total(second_a, PQ, 256)
-    gk[...] = total(second_a, PK, 256)
-    gv[...] = total(second_a, PV, 512)
-    ggo[...] = total(second_a, PG, 512)
-    pair = total(second_a, PB, 128).T
-    gb[...] = pair[0:2]
-    gd[...] = pair[2:4]
-    gout[...] = total(second_a, PEND, 512)
-    second_b.arrive()
-    gfg[...] = total(second_b, 0, FPAD)[:, 0:704]
-    gfu[...] = total(second_b, FPAD, FPAD)[:, 0:704]
-    gfd[...] = total(second_b, 2 * FPAD, FPAD)[:, 0:704]
-    for ring in (first_a, first_b, second_a, second_b):
-        ring.sent()
-    for copy in small_x + small_z:
-        copy.wait_send()
-
-
-def run_grads(args):
-    results = (
-        (ROWS, 256), (ROWS, 256), (ROWS, 512), (2, ROWS), (2, ROWS), (ROWS, 512),
-        (ROWS, 512), (ROWS, 704), (ROWS, 704), (ROWS, 704), (8, 1024),
-    )
-
-    def first(n):
-        return [pltpu.VMEM((2, ROWS, n), BF16)] * 2 + [pltpu.VMEM((4, ROWS, n), BF16)] * 2
-
-    def second(n):
-        return [pltpu.VMEM((ROWS // 2, n), BF16)] * 2 + [pltpu.VMEM((ROWS, n), BF16)] * 2
-
-    buffers = (
-        [pltpu.VMEM((4, 4, ROWS, NA), BF16), pltpu.VMEM((4, 4, ROWS, NB), BF16)]
-        + first(NA)
-        + first(NB)
-        + [pltpu.VMEM((4, ROWS, NA), BF16), pltpu.VMEM((4, ROWS, NB), BF16)]
-        + second(NA)
-        + second(NB)
-        + [pltpu.VMEM((4, 8, 1024), F32)] * 2
-        + [pltpu.VMEM((4, 4, ROWS, 256), BF16)] * 4
-    )
-    sems = [
-        pltpu.SemaphoreType.DMA((4, 6)), pltpu.SemaphoreType.DMA((4, 6)),
-        pltpu.SemaphoreType.DMA((6,)), pltpu.SemaphoreType.DMA((6,)),
-    ]
-    return pl.pallas_call(
-        grad_kernel,
-        out_shape=[jax.ShapeDtypeStruct(s, F32) for s in results],
-        in_specs=[pl.BlockSpec(memory_space=pltpu.VMEM)] * len(args),
-        out_specs=[pl.BlockSpec(memory_space=pltpu.VMEM)] * len(results),
-        scratch_shapes=buffers + sems,
-        compiler_params=pltpu.CompilerParams(
-            collective_id=1, has_side_effects=True, vmem_limit_bytes=58 * 1024 * 1024
-        ),
-        name="grads",
     )(*args)
 
 
@@ -890,7 +951,7 @@
         out_shape=[jax.ShapeDtypeStruct(s, d) for s, d in results],
         in_specs=[pl.BlockSpec(memory_space=pltpu.VMEM)] * len(args),
         out_specs=[pl.BlockSpec(memory_space=pltpu.VMEM)] * len(results),
-        compiler_params=pltpu.CompilerParams(vmem_limit_bytes=32 * 1024 * 1024),
+        compiler_params=pltpu.CompilerParams(vmem_limit_bytes=60 * 1024 * 1024),
         name="results",
     )(*args)
 
@@ -909,11 +970,10 @@
         log_rate, step_bias, out_gain, w_gate_out[0], w_out[0], norm_gain2,
         w_ffn_gate[0].T, w_ffn_up[0].T, w_ffn_down[0],
     ))
-    grads = run_grads(tuple(out[2:]))
     (
         hidden, input_grad, gq, gk, gv, gb, gd, ggo, gout, gfg, gfu, gfd,
         dg1, dcq, dck, dcv, dlr, dsb, dog, dg2,
-    ) = run_results(tuple(out[:2]) + tuple(grads))
+    ) = run_results(tuple(out))
     shape = (1,) + inputs.shape
     return (
         hidden.reshape(shape), input_grad.reshape(shape), dg1, gq[None], gk[None], gv[None],

time: 185 us -> 147 us (0.79)
  Pallas kernels: 175 us -> 146 us
  local copies, waits for them, and re-layouts: 9.17 us -> 0 us
    pallas_call x1 -> x0, Pallas kernels: 63.9 us -> none  [run_grads(): pl.pallas_call(grad_kernel, out_shape=[jax.ShapeDtypeStruct(s, F32) for s...]
    pallas_call x1, Pallas kernels: 109 us -> 143 us  [run_layer(): pl.pallas_call(layer_kernel, out_shape=[jax.ShapeDtypeStruct(s, d) for s,...]
    unnamed x26 -> x0, local copies, waits for them, and re-layouts: 9.17 us -> none
where the time goes in v3:
time: 147 us
  Pallas kernels  146 us (99%)
    pallas_call x1, Pallas kernels, run_layer(): pl.pallas_call(layer_kernel, out_shape=[jax.ShapeDtypeStruct(s, d) for s,...  143 us
    pallas_call x1, Pallas kernels, run_results(): pl.pallas_call(result_kernel, out_shape=[jax.ShapeDtypeStruct(s, d) for s...  2.97 us

profile of v3, /device:TPU:0, one launch (start us, length us, event | category | flops | bytes accessed | tf_op | source)
XLA Modules:
  0.0 146.6 jit_solution(1705759586993341268)
XLA Ops:
  0.7 142.8 %layer.1 = (bf16[256,1024]{1,0:T(8,128)(2,1)}, bf16[256,1024]{1,0:T(8,128)(2,1)}, f32[64,256]{1,0:T(8,128)}, f32[64,256]{1,0:T(8,128)}, f32[64,512]{1,0:T(8,128)...) custom-call(bf16[256,1024]{1,0:T(8,128)(2,1)} %bitcast.56, ...), custom_call_target="tpu_custom_call" | custom-call | tf_op jit(solution)/shard_map/layer/pallas_call | solution.py:913
  143.4 3.0 %results.1 = (bf16[256,1024]{1,0:T(8,128)(2,1)}, bf16[256,1024]{1,0:T(8,128)(2,1)}, f32[64,256]{1,0:T(8,128)}, f32[64,256]{1,0:T(8,128)}, f32[64,512]{1,0:T(8,12...) custom-call(bf16[256,1024]{1,0:T(8,128)(2,1)} %get-tuple-element.53., ...), custom_call_target="tpu_custom_call" | custom-call | tf_op jit(solution)/shard_map/results/pallas_call | solution.py:949

commit v4 on v3

--- a/solution.py
+++ b/solution.py
@@ -16,9 +16,12 @@
 SCALE = DK**-0.5
 PQ, PK, PV, PG, PB, PEND = 0, 256, 512, 1024, 1536, 1664
 FPAD = 768
-NF = FPAD + FPAD // 2
-NQ = PV + (PEND - PB) + 512
-NV = PB - PV
+FF = 704
+PAIR = 2 * FF
+NF = 1152
+NG = PAIR - NF + FPAD
+NQ = PV + 512
+NV = PEND - PV
 
 
 def dot(left, right):
@@ -180,7 +183,7 @@
         )
 
 
-WIDTHS = (NF, NF, NQ, NV)
+WIDTHS = (NF, NG, NQ, NV)
 
 
 def sum_scratch():
@@ -239,15 +242,16 @@
                         ROWS * i : ROWS * (i + 1)
                     ]
 
-        if k < 2:
-            outer(data["a2"], data["pair"], FPAD * k, FPAD, 0)
-            outer(data["dy"], data["act"], FPAD // 2 * k, FPAD // 2, FPAD)
+        if k == 0:
+            outer(data["a2"], data["pair"], 0, NF, 0)
+        elif k == 1:
+            outer(data["a2"], data["pair"], NF, PAIR - NF, 0)
+            outer(data["dy"], data["act"], 0, FPAD, PAIR - NF)
         elif k == 2:
             outer(data["a1"], data["proj"], PQ, PV, 0)
-            outer(data["a1"], data["proj"], PB, PEND - PB, PV)
-            outer(data["dh"], data["mix"], 0, 512, PV + PEND - PB)
+            outer(data["dh"], data["mix"], 0, 512, PV)
         else:
-            outer(data["a1"], data["proj"], PV, PB - PV, 0)
+            outer(data["a1"], data["proj"], PV, PEND - PV, 0)
 
     def begin(self, groups):
         for step in range(3):
@@ -282,11 +286,11 @@
     def ffn_finish(self):
         one, two, outs = self.second[0], self.second[1], self.outs
         one.arrive()
-        outs["fg"][...] = one.total(0, FPAD)[:, 0:704]
-        outs["fd"][:, 0:384] = one.total(FPAD, 384)
+        outs["fg"][...] = one.total(0, FPAD)[:, 0:FF]
+        outs["fu"][:, 0 : NF - FF] = one.total(640, NF - 640)[:, FF - 640 :]
         two.arrive()
-        outs["fu"][...] = two.total(0, FPAD)[:, 0:704]
-        outs["fd"][:, 384:704] = two.total(FPAD, 384)[:, 0:320]
+        outs["fu"][:, NF - FF : FF] = two.total(0, PAIR - NF)
+        outs["fd"][...] = two.total(PAIR - NF, FPAD)[:, 0:FF]
 
     def mix_start(self):
         self.begin((2, 3))
@@ -307,13 +311,13 @@
         one.arrive()
         outs["q"][...] = one.total(0, 256)
         outs["k"][...] = one.total(256, 256)
-        both = one.total(PV, PEND - PB).T
-        outs["b"][...] = both[0:2]
-        outs["d"][...] = both[2:4]
-        outs["out"][...] = one.total(PV + PEND - PB, 512)
+        outs["out"][...] = one.total(PV, 512)
         two.arrive()
         outs["v"][...] = two.total(0, 512)
         outs["go"][...] = two.total(512, 512)
+        both = two.total(1024, PEND - PB).T
+        outs["b"][...] = both[0:2]
+        outs["d"][...] = both[2:4]
 
     def small_start(self, small):
         self.sx[0] = small[...]
@@ -347,7 +351,7 @@
     a1, dpr, a2, dgu, dho, mix, dyo, act, small, a1t, a2t, dht, dyt,
     part, r1, r2, fwd, hopb, gbuf, xrow, hrow, drow,
     proj, zsum, qkv, gpre, onorm, upg, upu, dact,
-    tinv, amat, dmat, emat, umat, cols, gains, dg2s,
+    tinv, amat, dmat, emat, umat, cols, gains, dg1s, dg2s,
     rs_s, rs_r, op_s, op_r, ag_s, ag_r, hop_s, hop_r, ga_s, ga_r,
     *sum_refs,
 ):
@@ -358,7 +362,7 @@
     sib = hi * 2 + (1 - core)
     opp = (1 - hi) * 2 + core
     other = 1 - section
-    pieces = range(2)
+    seqs = range(2)
 
     def remote(src, dst, ssem, rsem, device):
         return pltpu.make_async_remote_copy(
@@ -391,22 +395,29 @@
 
     def pair_sum(ph):
         return [
-            remote(part.at[ph, 1 - core, p], r1.at[ph, p], rs_s.at[ph, p], rs_r.at[ph, p],
+            remote(part.at[ph, s, 1 - core], r1.at[ph, s], rs_s.at[ph, s], rs_r.at[ph, s],
                    {"tensor": sib})
-            for p in pieces
+            for s in seqs
         ]
 
     def chip_swap(ph):
         return [
-            remote(fwd.at[ph, p], r2.at[ph, p], op_s.at[ph, p], op_r.at[ph, p], {"tensor": opp})
-            for p in pieces
+            remote(fwd.at[ph, s], r2.at[ph, s], op_s.at[ph, s], op_r.at[ph, s], {"tensor": opp})
+            for s in seqs
         ]
 
     def pair_share(k):
         return [
-            remote(gbuf.at[k, core, p], gbuf.at[k, core, p], ag_s.at[k, p], ag_r.at[k, p],
+            remote(gbuf.at[k, s, core], gbuf.at[k, s, core], ag_s.at[k, s], ag_r.at[k, s],
                    {"tensor": sib})
-            for p in pieces
+            for s in seqs
+        ]
+
+    def hop_send(ph, k, s):
+        return [
+            remote(fwd.at[ph, s], hopb.at[k, hi, s], hop_s.at[k, y, s], hop_r.at[k, hi, s],
+                   {"section": other, "tensor": 2 * y + core})
+            for y in range(2)
         ]
 
     def started(copies):
@@ -421,68 +432,51 @@
         for copy in copies:
             copy.wait_send()
 
-    def pair_total(ph, p):
-        return part[ph, core, p].astype(F32) + r1[ph, p].astype(F32)
-
-    def chip_total(ph, p):
-        return fwd[ph, p].astype(F32) + r2[ph, p].astype(F32)
-
-    def all_sum(ph, k, finish, between=None):
-        firsts, swaps, shares = pair_sum(ph), chip_swap(ph), pair_share(k)
-        started(firsts)
-        for p in pieces:
-            firsts[p].wait_recv()
-            fwd[ph, p] = pair_total(ph, p).astype(BF16)
-            swaps[p].start()
-        if between is not None:
-            between()
-        for p in pieces:
-            swaps[p].wait_recv()
-            gbuf[k, core, p] = finish(p, chip_total(ph, p)).astype(BF16)
-            shares[p].start()
-        received(shares)
-        sent(firsts + swaps + shares)
-
-    def hop_send(ph, k):
-        return [
-            remote(fwd.at[ph, p], hopb.at[k, hi, p], hop_s.at[k, y, p], hop_r.at[k, hi, p],
-                   {"section": other, "tensor": 2 * y + core})
-            for p in pieces
-            for y in range(2)
-        ]
-
-    def hop_receive(k, share, finish):
-        shares = pair_share(share)
-        for p in pieces:
-            for y in range(2):
-                remote(hopb.at[k, y, p], hopb.at[k, y, p], hop_s.at[k, y, p], hop_r.at[k, y, p],
-                       {"section": other, "tensor": t}).wait_recv()
-            value = (hopb[k, 0, p].astype(F32) + hopb[k, 1, p].astype(F32)).astype(BF16)
-            gbuf[share, core, p] = finish(p, value)
-            shares[p].start()
-        received(shares)
-        sent(shares)
-
-    def put_part(ph, value):
-        for s in range(2):
-            for p in pieces:
-                at = LEN * s + ROWS * p
-                part[ph, s, p] = value[at : at + ROWS].astype(BF16)
-
-    def spread(k, out):
-        for s in range(2):
-            for p in pieces:
-                at = LEN * s + ROWS * p
-                out[at : at + ROWS] = gbuf[k, s, p]
-
-    def piece(p):
-        return slice(ROWS * p, ROWS * (p + 1))
+    def pair_total(ph, s):
+        return part[ph, s, core].astype(F32) + r1[ph, s].astype(F32)
+
+    def chip_total(ph, s):
+        return fwd[ph, s].astype(F32) + r2[ph, s].astype(F32)
+
+    def swap(ph, s):
+        firsts[ph][s].wait_recv()
+        fwd[ph, s] = pair_total(ph, s).astype(BF16)
+        swaps[ph][s].start()
+
+    def hop_receive(k, share, s, finish, out):
+        passes = pair_share(share)[s]
+        for y in range(2):
+            remote(hopb.at[k, y, s], hopb.at[k, y, s], hop_s.at[k, y, s], hop_r.at[k, y, s],
+                   {"section": other, "tensor": t}).wait_recv()
+        value = (hopb[k, 0, s].astype(F32) + hopb[k, 1, s].astype(F32)).astype(BF16)
+        gbuf[share, s, core] = finish(s, value)
+        passes.start()
+        passes.wait_recv()
+        spread(share, s, out)
+        passes.wait_send()
+
+    def put_part(ph, s, value):
+        for p in range(2):
+            part[ph, s, p] = value[ROWS * p : ROWS * (p + 1)].astype(BF16)
+
+    def spread(k, s, out):
+        for p in range(2):
+            at = LEN * s + ROWS * p
+            out[at : at + ROWS] = gbuf[k, s, p]
+
+    def piece(s):
+        return slice(ROWS * s, ROWS * (s + 1))
+
+    def mine(s):
+        return pl.ds(pl.multiple_of(core * ROWS + LEN * s, ROWS), ROWS)
 
     def normed(x, gain):
         inv = lax.rsqrt(jnp.mean(x * x, axis=-1, keepdims=True) + 1e-06)
         return (x * inv * gain).astype(BF16)
 
-    pairs = [(s, h) for s in range(2) for h in range(HEADS)]
+    firsts = [pair_sum(ph) for ph in range(4)]
+    swaps = [chip_swap(ph) for ph in range(4)]
+    middles, backs, hiddens, inners = (pair_share(k) for k in (1, 3, 4, 5))
     row = lax.broadcasted_iota(jnp.int32, (LEN, LEN), 0)
     col = lax.broadcasted_iota(jnp.int32, (LEN, LEN), 1)
     within = row >= col
@@ -509,283 +503,228 @@
     def hv(h):
         return slice(DV * h, DV * (h + 1))
 
-    @pl.when(section == 0)
-    def _():
-        for c in range(4):
-            at = slice(ROWS * c, ROWS * (c + 1))
-            a1[at] = normed(inp[at].astype(F32), gain1)
-        for p in pieces:
-            at = pl.multiple_of(core * LEN + ROWS * p, ROWS)
-            xrow[piece(p)] = inp[pl.ds(at, ROWS)].astype(F32)
-
-    def take_input(p, value):
-        x = value.astype(F32)
-        xrow[piece(p)] = x
-        return normed(x, gain1)
-
-    @pl.when(section == 1)
-    def _():
-        dyo[...] = cot[...]
-        dact[...] = dot_nt(cot[...], wfd[...])
-        turned(dyo, dyt)
-        hop_receive(0, 0, take_input)
-        spread(0, a1)
-
-    source = a1[...]
-    proj[:, PQ:PK] = dot(source, wq[...])
-    proj[:, PK:PV] = dot(source, wk[...])
-    proj[:, PV:PG] = dot(source, wv[...])
+    lane = lax.broadcasted_iota(jnp.int32, (LEN, LEN), 1)
+    lane_row = lax.broadcasted_iota(jnp.int32, (1, LEN), 1)
+    ltri = jnp.where(within, 1.0, 0.0)
+    utri = jnp.where(row <= col, 1.0, 0.0)
     wba = jnp.concatenate(
         [wb[...].astype(F32), wd[...].astype(F32), jnp.zeros((4, 1024), F32)], axis=0
     ).astype(BF16)
-    pba = dot_nt(source, wba)
-    gpre[...] = dot(source, wgo[...])
-
-    lane = lax.broadcasted_iota(jnp.int32, (LEN, LEN), 1)
-    ltri = jnp.where(within, 1.0, 0.0)
-    utri = jnp.where(row <= col, 1.0, 0.0)
-    betas, decays, slopes = [], [], []
-    for s, h in pairs:
-        betas.append(sigmoid(pba[seq(s), h : h + 1]))
-        pre = pba[seq(s), 2 + h : 3 + h] + sbias[0:1, h : h + 1]
-        soft = jnp.maximum(pre, 0.0) + jnp.log1p(jnp.exp(-jnp.abs(pre)))
-        rate = -jnp.exp(lrate[0:1, h : h + 1])
-        decays.append(rate * soft)
-        slopes.append(rate * sigmoid(pre))
-    packed = jnp.zeros((LEN, LEN), F32)
-    for i in range(4):
-        packed = jnp.where(lane == i, decays[i], packed)
-    cums = dot_full(ltri, packed)
-
-    for s, h in pairs:
-        z = conv_sum(proj[seq(s), qc(h)], taps_q[:, DK * h : DK * (h + 1)])
-        zsum[seq(s), qc(h)] = z
-        c = z * sigmoid(z)
-        rq = lax.rsqrt(jnp.sum(c * c, axis=-1, keepdims=True) + 1e-06)
-        qkv[seq(s), qc(h)] = c * (rq * SCALE)
-        z = conv_sum(proj[seq(s), kc(h)], taps_k[:, DK * h : DK * (h + 1)])
-        zsum[seq(s), kc(h)] = z
-        c = z * sigmoid(z)
-        rk = lax.rsqrt(jnp.sum(c * c, axis=-1, keepdims=True) + 1e-06)
-        qkv[seq(s), kc(h)] = c * rk
-        z = conv_sum(proj[seq(s), vc(h)], taps_v[:, hv(h)])
-        zsum[seq(s), vc(h)] = z
-        qkv[seq(s), vc(h)] = z * sigmoid(z)
-        i = 2 * s + h
-        cols[0, i] = jnp.broadcast_to(betas[i], (LEN, LEN))
-        cols[1, i] = jnp.broadcast_to(decays[i], (LEN, LEN))
-        cols[2, i] = jnp.broadcast_to(slopes[i], (LEN, LEN))
-        cols[3, i] = jnp.broadcast_to(rq, (LEN, LEN))
-        cols[4, i] = jnp.broadcast_to(rk, (LEN, LEN))
-
-    systems = []
-    for i, (s, h) in enumerate(pairs):
-        cum = jnp.broadcast_to(cums[:, i : i + 1], (LEN, LEN))
-        gaps = cum - cum.T
-        decay = jnp.where(within, jnp.exp(jnp.where(within, gaps, 0.0)), 0.0)
-        dmat[i] = decay
-        kn = qkv[seq(s), kc(h)]
-        e = jnp.where(strict, dot_nt(kn, kn) * decay, 0.0)
-        emat[i] = e
-        systems.append(cols[0, i] * e)
-        amat[i] = dot_nt(qkv[seq(s), qc(h)], kn) * decay
-    for i, inverse in enumerate(unit_inverses(systems)):
-        tinv[i] = inverse.astype(BF16)
-    for i, (s, h) in enumerate(pairs):
-        w = qkv[seq(s), vc(h)] * cols[0, i][:, 0:1]
-        umat[i] = dot(tinv[i], w).astype(BF16)
-    for i, (s, h) in enumerate(pairs):
-        o = dot(amat[i], umat[i])
-        ro = lax.rsqrt(jnp.mean(o * o, axis=-1, keepdims=True) + 1e-05)
-        cols[5, i] = jnp.broadcast_to(ro, (LEN, LEN))
-        on = o * ro
-        onorm[seq(s), hv(h)] = on
-        gp = gpre[seq(s), hv(h)]
-        mix[seq(s), hv(h)] = (on * ogains[:, hv(h)] * (gp * sigmoid(gp))).astype(BF16)
-
-    put_part(0, dot(mix[...], wo[...]))
-
-    def take_middle(p, total):
-        h = xrow[piece(p)] + total
-        hrow[piece(p)] = h
-        return normed(h, gain2)
-
-    all_sum(0, 1, take_middle)
-    spread(1, a2)
-    source = a2[...]
-    upg[...] = dot_nt(source, wfg[...])
-    upu[...] = dot_nt(source, wfu[...])
-
-    outs = pair_sum(1)
-    out_swaps = chip_swap(1)
-
-    def output_part():
-        ug = upg[...]
-        s_act = (ug * sigmoid(ug) * upu[...]).astype(BF16)
-        act[:, 704:FPAD] = jnp.zeros((2 * LEN, FPAD - 704), BF16)
-        act[:, 0:704] = s_act
-        put_part(1, dot(s_act, wfd[...]))
-        started(outs)
-
-    def output_sum():
-        for p in pieces:
-            outs[p].wait_recv()
-            h = jnp.where(hi == 0, hrow[piece(p)], 0.0)
-            fwd[1, p] = (pair_total(1, p) + h).astype(BF16)
-
-    def take_cotangent(p, value):
-        return value
-
-    @pl.when(section == 0)
-    def _():
-        output_part()
-        output_sum()
-        hops = hop_send(1, 0)
-        started(hops)
-        sent(hops)
-        started(out_swaps)
-        turned(a1, a1t)
-        turned(a2, a2t)
-        hop_receive(1, 2, take_cotangent)
-        spread(2, dyo)
-        dact[...] = dot_nt(dyo[...], wfd[...])
-
-    ds = dact[...]
-    ug = upg[...]
-    uu = upu[...]
-    sg = sigmoid(ug)
-    pad = jnp.zeros((2 * LEN, FPAD - 704), BF16)
-    dgu[:, 704:FPAD] = pad
-    dgu[:, FPAD + 704 :] = pad
-    dgu[:, 0:704] = (ds * uu * (sg * (1.0 + ug * (1.0 - sg)))).astype(BF16)
-    dgu[:, FPAD : FPAD + 704] = (ds * (ug * sg)).astype(BF16)
-    put_part(2, dot(dgu[:, 0:704], wfg[...]) + dot(dgu[:, FPAD : FPAD + 704], wfu[...]))
-
-    def take_gradient(p, total):
-        dz, dgain = rms_back(hrow[piece(p)], gain2, total)
-        at = pl.multiple_of(core * LEN + ROWS * p, ROWS)
-        dh = dyo[pl.ds(at, ROWS)].astype(F32) + dz
-        drow[piece(p)] = dh
-        dg2s[p] = dgain
-        return dh
-
-    def second_output():
-        @pl.when(section == 1)
-        def _():
-            output_part()
-            turned(a1, a1t)
-            turned(a2, a2t)
-
-        @pl.when(section == 0)
-        def _():
-            turned(dyo, dyt)
-
-        grads.ffn_start()
-
-    all_sum(2, 3, take_gradient, second_output)
-
-    @pl.when(section == 1)
-    def _():
-        output_sum()
-        started(out_swaps)
-
-    spread(3, dho)
-    dact[:, 0:512] = dot_nt(dho[...], wo[...])
-    grads.ffn_relay()
-
-    small[...] = jnp.zeros_like(small)
-    douts = [jnp.zeros((1, DV), F32) for _ in range(HEADS)]
-    dos = []
-    for i, (s, h) in enumerate(pairs):
-        dm = dact[seq(s), hv(h)]
-        gp = gpre[seq(s), hv(h)]
-        sg = sigmoid(gp)
-        on = onorm[seq(s), hv(h)]
-        og = ogains[:, hv(h)]
-        dgate = dm * on
-        dpr[seq(s), PG + DV * h : PG + DV * (h + 1)] = (
-            dgate * og * (sg * (1.0 + gp * (1.0 - sg)))
-        ).astype(BF16)
-        silu_g = gp * sg
-        douts[h] = douts[h] + jnp.sum(dgate * silu_g, axis=0, keepdims=True)
-        don = dm * silu_g * og
-        ro = cols[5, i][:, 0:1]
-        do = ro * (don - on * jnp.mean(don * on, axis=-1, keepdims=True))
-        dos.append(do.astype(BF16))
-    for h in range(HEADS):
-        small[6:7, hv(h)] = douts[h]
-    das = [dot_nt(dos[i], umat[i]) for i in range(4)]
-    dus = [dot(amat[i].T, dos[i]) for i in range(4)]
-    dws = [dot(tinv[i].astype(F32).T, dus[i]) for i in range(4)]
-    dms = [jnp.where(strict, -dot_nt(dws[i], umat[i]), 0.0) for i in range(4)]
-    dbetas, dcs, dqs, dks = [], [], [], []
-    for i, (s, h) in enumerate(pairs):
-        beta = cols[0, i]
-        e = emat[i]
-        decay = dmat[i]
-        v = qkv[seq(s), vc(h)]
-        de = dms[i] * e
-        dbetas.append(
-            jnp.sum(dws[i] * v, axis=-1, keepdims=True) + jnp.sum(de, axis=-1, keepdims=True)
-        )
-        dgap = das[i] * amat[i] + de * beta
-        dcs.append(jnp.sum(dgap - dgap.T, axis=-1, keepdims=True))
-        dqk = das[i] * decay
-        dkk = dms[i] * beta * decay
-        kn = qkv[seq(s), kc(h)]
-        qn = qkv[seq(s), qc(h)]
-        dqs.append(dot(dqk, kn))
-        dks.append(dot(dqk.T, qn) + dot(dkk + dkk.T, kn))
-    packed = jnp.zeros((LEN, LEN), F32)
-    for i in range(4):
-        packed = jnp.where(lane == i, dcs[i], packed)
-    dgs = dot_full(utri, packed)
-
-    dcq = [jnp.zeros((1, DK), F32) for _ in range(4 * HEADS)]
-    dck = [jnp.zeros((1, DK), F32) for _ in range(4 * HEADS)]
-    dcv = [jnp.zeros((1, DV), F32) for _ in range(4 * HEADS)]
-
-    def conv_back(dz, at_rows, at_cols, taps, sums, h):
+
+    def pair_of(columns):
+        packed = jnp.zeros((LEN, LEN), F32)
+        for h in range(HEADS):
+            packed = jnp.where(lane == h, columns[h], packed)
+        return packed
+
+    def mixer_systems(s):
+        at = seq(s)
+        source = a1[at]
+        proj[at, PQ:PK] = dot(source, wq[...])
+        proj[at, PK:PV] = dot(source, wk[...])
+        proj[at, PV:PG] = dot(source, wv[...])
+        pba = dot_nt(source, wba)
+        gpre[at] = dot(source, wgo[...])
+        betas, decays, slopes = [], [], []
+        for h in range(HEADS):
+            betas.append(sigmoid(pba[:, h : h + 1]))
+            pre = pba[:, 2 + h : 3 + h] + sbias[0:1, h : h + 1]
+            soft = jnp.maximum(pre, 0.0) + jnp.log1p(jnp.exp(-jnp.abs(pre)))
+            rate = -jnp.exp(lrate[0:1, h : h + 1])
+            decays.append(rate * soft)
+            slopes.append(rate * sigmoid(pre))
+        cums = dot_full(ltri, pair_of(decays))
+        for h in range(HEADS):
+            z = conv_sum(proj[at, qc(h)], taps_q[:, DK * h : DK * (h + 1)])
+            zsum[at, qc(h)] = z
+            c = z * sigmoid(z)
+            rq = lax.rsqrt(jnp.sum(c * c, axis=-1, keepdims=True) + 1e-06)
+            qkv[at, qc(h)] = c * (rq * SCALE)
+            z = conv_sum(proj[at, kc(h)], taps_k[:, DK * h : DK * (h + 1)])
+            zsum[at, kc(h)] = z
+            c = z * sigmoid(z)
+            rk = lax.rsqrt(jnp.sum(c * c, axis=-1, keepdims=True) + 1e-06)
+            qkv[at, kc(h)] = c * rk
+            z = conv_sum(proj[at, vc(h)], taps_v[:, hv(h)])
+            zsum[at, vc(h)] = z
+            qkv[at, vc(h)] = z * sigmoid(z)
+            i = 2 * s + h
+            cols[0, i] = jnp.broadcast_to(betas[h], (LEN, LEN))
+            cols[1, i] = jnp.broadcast_to(decays[h], (LEN, LEN))
+            cols[2, i] = jnp.broadcast_to(slopes[h], (LEN, LEN))
+            cols[3, i] = jnp.broadcast_to(rq, (LEN, LEN))
+            cols[4, i] = jnp.broadcast_to(rk, (LEN, LEN))
+        systems = []
+        for h in range(HEADS):
+            i = 2 * s + h
+            cum = jnp.broadcast_to(cums[:, h : h + 1], (LEN, LEN))
+            gaps = cum - cum.T
+            decay = jnp.where(within, jnp.exp(jnp.where(within, gaps, 0.0)), 0.0)
+            dmat[i] = decay
+            kn = qkv[at, kc(h)]
+            e = jnp.where(strict, dot_nt(kn, kn) * decay, 0.0)
+            emat[i] = e
+            systems.append(cols[0, i] * e)
+            amat[i] = dot_nt(qkv[at, qc(h)], kn) * decay
+        return systems
+
+    def mixer_outputs(s, systems):
+        at = seq(s)
+        for h, inverse in enumerate(unit_inverses(systems)):
+            tinv[2 * s + h] = inverse.astype(BF16)
+        for h in range(HEADS):
+            i = 2 * s + h
+            w = qkv[at, vc(h)] * cols[0, i][:, 0:1]
+            umat[i] = dot(tinv[i], w).astype(BF16)
+        for h in range(HEADS):
+            i = 2 * s + h
+            o = dot(amat[i], umat[i])
+            ro = lax.rsqrt(jnp.mean(o * o, axis=-1, keepdims=True) + 1e-05)
+            cols[5, i] = jnp.broadcast_to(ro, (LEN, LEN))
+            on = o * ro
+            onorm[at, hv(h)] = on
+            gp = gpre[at, hv(h)]
+            mix[at, hv(h)] = (on * ogains[:, hv(h)] * (gp * sigmoid(gp))).astype(BF16)
+        put_part(0, s, dot(mix[at], wo[...]))
+
+    def take_middle(s):
+        swaps[0][s].wait_recv()
+        h = xrow[piece(s)] + chip_total(0, s)
+        hrow[piece(s)] = h
+        gbuf[1, s, core] = normed(h, gain2)
+        middles[s].start()
+
+    def ffn_inputs(s):
+        middles[s].wait_recv()
+        spread(1, s, a2)
+        source = a2[seq(s)]
+        upg[seq(s)] = dot_nt(source, wfg[...])
+        upu[seq(s)] = dot_nt(source, wfu[...])
+
+    def ffn_outputs(s):
+        at = seq(s)
+        ug = upg[at]
+        s_act = (ug * sigmoid(ug) * upu[at]).astype(BF16)
+        act[at, FF:FPAD] = jnp.zeros((LEN, FPAD - FF), BF16)
+        act[at, 0:FF] = s_act
+        put_part(1, s, dot(s_act, wfd[...]))
+        firsts[1][s].start()
+
+    def ffn_output_sum(s):
+        firsts[1][s].wait_recv()
+        h = jnp.where(hi == 0, hrow[piece(s)], 0.0)
+        fwd[1, s] = (pair_total(1, s) + h).astype(BF16)
+
+    def ffn_back(s):
+        at = seq(s)
+        ds = dact[at]
+        ug = upg[at]
+        uu = upu[at]
+        sg = sigmoid(ug)
+        dug = (ds * uu * (sg * (1.0 + ug * (1.0 - sg)))).astype(BF16)
+        duu = (ds * (ug * sg)).astype(BF16)
+        put_part(2, s, dot(dug, wfg[...]) + dot(duu, wfu[...]))
+        firsts[2][s].start()
+        dgu[at, 0:FF] = dug
+        dgu[at, FF:PAIR] = duu
+
+    def take_gradient(s):
+        swaps[2][s].wait_recv()
+        dz, dgain = rms_back(hrow[piece(s)], gain2, chip_total(2, s))
+        dh = dyo[mine(s)].astype(F32) + dz
+        drow[piece(s)] = dh
+        dg2s[s] = dgain
+        gbuf[3, s, core] = dh.astype(BF16)
+        backs[s].start()
+
+    def mixer_back(s):
+        at = seq(s)
+        backs[s].wait_recv()
+        spread(3, s, dho)
+        dmix = dot_nt(dho[at], wo[...])
+        dos = []
+        for h in range(HEADS):
+            i = 2 * s + h
+            dm = dmix[:, hv(h)]
+            gp = gpre[at, hv(h)]
+            sg = sigmoid(gp)
+            on = onorm[at, hv(h)]
+            og = ogains[:, hv(h)]
+            dgate = dm * on
+            dpr[at, PG + DV * h : PG + DV * (h + 1)] = (
+                dgate * og * (sg * (1.0 + gp * (1.0 - sg)))
+            ).astype(BF16)
+            silu_g = gp * sg
+            small[6:7, hv(h)] += jnp.sum(dgate * silu_g, axis=0, keepdims=True)
+            don = dm * silu_g * og
+            ro = cols[5, i][:, 0:1]
+            do = ro * (don - on * jnp.mean(don * on, axis=-1, keepdims=True))
+            dos.append(do.astype(BF16))
+        index = [2 * s + h for h in range(HEADS)]
+        das = [dot_nt(do, umat[i]) for i, do in zip(index, dos)]
+        dus = [dot(amat[i].T, do) for i, do in zip(index, dos)]
+        dws = [dot(tinv[i].astype(F32).T, du) for i, du in zip(index, dus)]
+        dms = [jnp.where(strict, -dot_nt(dw, umat[i]), 0.0) for i, dw in zip(index, dws)]
+        return das, dws, dms
+
+    def conv_back(dz, at_rows, at_cols, taps, place_in_small):
         pre = proj[at_rows, at_cols]
         total = dz * taps[3:4]
         for j in range(3):
             total = total + shift_up(dz, 3 - j) * taps[j : j + 1]
         for j in range(4):
-            sums[4 * h + j] = sums[4 * h + j] + jnp.sum(
+            small[2 + j : 3 + j, place_in_small] += jnp.sum(
                 dz * shift_down(pre, 3 - j), axis=0, keepdims=True
             )
         dpr[at_rows, at_cols] = total.astype(BF16)
 
-    for i, (s, h) in enumerate(pairs):
-        qn = qkv[seq(s), qc(h)]
-        dq = dqs[i]
-        dc = (cols[3, i] * SCALE) * (
-            dq - qn * (jnp.sum(qn * dq, axis=-1, keepdims=True) * (1.0 / (SCALE * SCALE)))
-        )
-        dz = dc * silu_slope(zsum[seq(s), qc(h)])
-        conv_back(dz, seq(s), qc(h), taps_q[:, DK * h : DK * (h + 1)], dcq, h)
-        kn = qkv[seq(s), kc(h)]
-        dk = dks[i]
-        dc = cols[4, i] * (dk - kn * jnp.sum(kn * dk, axis=-1, keepdims=True))
-        dz = dc * silu_slope(zsum[seq(s), kc(h)])
-        conv_back(dz, seq(s), kc(h), taps_k[:, DK * h : DK * (h + 1)], dck, h)
-        dv = dws[i] * cols[0, i][:, 0:1]
-        dz = dv * silu_slope(zsum[seq(s), vc(h)])
-        conv_back(dz, seq(s), vc(h), taps_v[:, hv(h)], dcv, h)
-    for h in range(HEADS):
-        for j in range(4):
-            small[2 + j : 3 + j, DK * h : DK * (h + 1)] = dcq[4 * h + j]
-            small[2 + j : 3 + j, 256 + DK * h : 256 + DK * (h + 1)] = dck[4 * h + j]
-            small[2 + j : 3 + j, 512 + DV * h : 512 + DV * (h + 1)] = dcv[4 * h + j]
-    lane_row = lax.broadcasted_iota(jnp.int32, (1, LEN), 1)
-    scal = jnp.zeros((1, LEN), F32)
-    for s in range(2):
+    def mixer_inputs_back(s, kept):
+        das, dws, dms = kept
+        at = seq(s)
+        dbetas, dcs, dqs, dks = [], [], [], []
+        for h in range(HEADS):
+            i = 2 * s + h
+            beta = cols[0, i]
+            e = emat[i]
+            decay = dmat[i]
+            de = dms[h] * e
+            dbetas.append(
+                jnp.sum(dws[h] * qkv[at, vc(h)], axis=-1, keepdims=True)
+                + jnp.sum(de, axis=-1, keepdims=True)
+            )
+            dgap = das[h] * amat[i] + de * beta
+            dcs.append(jnp.sum(dgap - dgap.T, axis=-1, keepdims=True))
+            dqk = das[h] * decay
+            dkk = dms[h] * beta * decay
+            kn = qkv[at, kc(h)]
+            qn = qkv[at, qc(h)]
+            dqs.append(dot(dqk, kn))
+            dks.append(dot(dqk.T, qn) + dot(dkk + dkk.T, kn))
+        dgs = dot_full(utri, pair_of(dcs))
+        for h in range(HEADS):
+            i = 2 * s + h
+            qn = qkv[at, qc(h)]
+            dq = dqs[h]
+            dc = (cols[3, i] * SCALE) * (
+                dq - qn * (jnp.sum(qn * dq, axis=-1, keepdims=True) * (1.0 / (SCALE * SCALE)))
+            )
+            dz = dc * silu_slope(zsum[at, qc(h)])
+            conv_back(dz, at, qc(h), taps_q[:, DK * h : DK * (h + 1)], qc(h))
+            kn = qkv[at, kc(h)]
+            dk = dks[h]
+            dc = cols[4, i] * (dk - kn * jnp.sum(kn * dk, axis=-1, keepdims=True))
+            dz = dc * silu_slope(zsum[at, kc(h)])
+            conv_back(dz, at, kc(h), taps_k[:, DK * h : DK * (h + 1)], kc(h))
+            dv = dws[h] * cols[0, i][:, 0:1]
+            dz = dv * silu_slope(zsum[at, vc(h)])
+            conv_back(dz, at, vc(h), taps_v[:, hv(h)], vc(h))
+        scal = jnp.zeros((1, LEN), F32)
         block = jnp.zeros((LEN, LEN), F32)
         for h in range(HEADS):
             i = 2 * s + h
             beta = cols[0, i]
-            dg = jnp.broadcast_to(dgs[:, i : i + 1], (LEN, LEN))
-            dpb = dbetas[i] * beta * (1.0 - beta)
+            dg = jnp.broadcast_to(dgs[:, h : h + 1], (LEN, LEN))
+            dpb = dbetas[h] * beta * (1.0 - beta)
             dpa = dg * cols[2, i]
             block = jnp.where(lane == h, dpb, block)
             block = jnp.where(lane == 2 + h, dpa, block)
@@ -793,39 +732,154 @@
                 lane_row == h, jnp.sum(dg * cols[1, i], axis=0, keepdims=True), 0.0
             )
             scal = scal + jnp.where(lane_row == 2 + h, jnp.sum(dpa, axis=0, keepdims=True), 0.0)
-        dpr[seq(s), PB:PEND] = block.astype(BF16)
-    small[6:7, 512:640] = scal
-
-    def mixer_grads():
+        dpr[at, PB:PEND] = block.astype(BF16)
+        small[6:7, 512:640] += scal
+
+    def layer_back(s):
+        at = seq(s)
+        value = dot_nt(dpr[at, PQ:PK], wq[...])
+        value = value + dot_nt(dpr[at, PK:PV], wk[...])
+        value = value + dot_nt(dpr[at, PV:PG], wv[...])
+        value = value + dot_nt(dpr[at, PG:PB], wgo[...])
+        value = value + dot(dpr[at, PB:PEND][:, 0:8], wba)
+        put_part(3, s, value)
+        firsts[3][s].start()
+
+    def layer_back_sum(s):
+        firsts[3][s].wait_recv()
+        dz, dgain = rms_back(xrow[piece(s)], gain1, pair_total(3, s))
+        dg1s[s] = dgain
+        fwd[3, s] = (dz + jnp.where(hi == 0, drow[piece(s)], 0.0)).astype(BF16)
+
+    small[...] = jnp.zeros_like(small)
+
+    @pl.when(section == 0)
+    def _():
+        for c in range(4):
+            at = slice(ROWS * c, ROWS * (c + 1))
+            a1[at] = normed(inp[at].astype(F32), gain1)
+        for s in seqs:
+            xrow[piece(s)] = inp[mine(s)].astype(F32)
+
+    @pl.when(section == 1)
+    def _():
+        dyo[...] = cot[...]
+        dact[...] = dot_nt(cot[...], wfd[...])
+        turned(dyo, dyt)
+
+    def take_input(s, value):
+        x = value.astype(F32)
+        xrow[piece(s)] = x
+        return normed(x, gain1)
+
+    for s in seqs:
+        @pl.when(section == 1)
+        def _():
+            hop_receive(0, 0, s, take_input, a1)
+
+        systems = mixer_systems(s)
+        if s == 1:
+            swap(0, 0)
+        mixer_outputs(s, systems)
+        firsts[0][s].start()
+    swap(0, 1)
+
+    take_middle(0)
+    ffn_inputs(0)
+
+    @pl.when(section == 0)
+    def _():
+        ffn_outputs(0)
+
+    @pl.when(section == 1)
+    def _():
+        ffn_back(0)
+
+    take_middle(1)
+
+    @pl.when(section == 0)
+    def _():
+        ffn_output_sum(0)
+        started(hop_send(1, 0, 0))
+
+    @pl.when(section == 1)
+    def _():
+        swap(2, 0)
+
+    ffn_inputs(1)
+
+    def take_cotangent(s, value):
+        return value
+
+    @pl.when(section == 0)
+    def _():
+        ffn_outputs(1)
+        ffn_output_sum(1)
+        started(hop_send(1, 0, 1))
+        turned(a1, a1t)
+        turned(a2, a2t)
+        for s in seqs:
+            sent(hop_send(1, 0, s))
+        started(swaps[1])
+        for s in seqs:
+            hop_receive(1, 2, s, take_cotangent, dyo)
+            dact[seq(s)] = dot_nt(dyo[seq(s)], wfd[...])
+            ffn_back(s)
+            swap(2, s)
+        turned(dyo, dyt)
+        grads.ffn_start()
+
+    @pl.when(section == 1)
+    def _():
+        ffn_back(1)
+        swap(2, 1)
+
+    take_gradient(0)
+    kept = mixer_back(0)
+    take_gradient(1)
+    mixer_inputs_back(0, kept)
+    layer_back(0)
+    kept = mixer_back(1)
+    layer_back_sum(0)
+
+    @pl.when(section == 0)
+    def _():
+        grads.ffn_relay()
+
+    @pl.when(section == 1)
+    def _():
+        started(hop_send(3, 1, 0))
+
+    mixer_inputs_back(1, kept)
+
+    @pl.when(section == 0)
+    def _():
         turned(dho, dht)
         grads.mix_start()
 
-    pl.when(section == 0)(mixer_grads)
-    value = dot_nt(dpr[:, PQ:PK], wq[...])
-    value = value + dot_nt(dpr[:, PK:PV], wk[...])
-    value = value + dot_nt(dpr[:, PV:PG], wv[...])
-    value = value + dot_nt(dpr[:, PG:PB], wgo[...])
-    value = value + dot(dpr[:, PB:PEND][:, 0:8], wba)
-    put_part(3, value)
-    firsts, swaps = pair_sum(3), chip_swap(3)
-    started(firsts)
-    dgain1 = jnp.zeros((1, 1024), F32)
-    for p in pieces:
-        firsts[p].wait_recv()
-        dz, dgain = rms_back(xrow[piece(p)], gain1, pair_total(3, p))
-        dgain1 = dgain1 + dgain
-        fwd[3, p] = (dz + jnp.where(hi == 0, drow[piece(p)], 0.0)).astype(BF16)
-    gains[0, 0] = dgain1
+    layer_back(1)
+    layer_back_sum(1)
+
+    @pl.when(section == 1)
+    def _():
+        started(hop_send(3, 1, 1))
+        for s in seqs:
+            ffn_outputs(s)
+        turned(a2, a2t)
+        grads.ffn_start()
+        for s in seqs:
+            ffn_output_sum(s)
+        turned(a1, a1t)
+        turned(dho, dht)
+        grads.ffn_relay()
+        grads.mix_start()
+        for s in seqs:
+            sent(hop_send(3, 1, s))
+        started(swaps[1])
+
+    started(swaps[3])
+    gains[0, 0] = dg1s[0] + dg1s[1]
     gains[0, 1] = jnp.where(hi == 0, dg2s[0] + dg2s[1], 0.0)
-
-    @pl.when(section == 1)
-    def _():
-        hops = hop_send(3, 1)
-        started(hops)
-        mixer_grads()
-        sent(hops)
-
-    started(swaps)
     sums = [
         remote(
             gains.at[0], gains.at[step], ga_s.at[step - 1], ga_r.at[step - 1],
@@ -834,33 +888,35 @@
         for step in range(1, 4)
     ]
     started(sums)
-    hidden, back = pair_share(4), pair_share(5)
-    for p in pieces:
-        out_swaps[p].wait_recv()
-        gbuf[4, core, p] = chip_total(1, p).astype(BF16)
-        hidden[p].start()
     grads.ffn_merge()
-    grads.mix_relay()
-    for p in pieces:
-        swaps[p].wait_recv()
-        gbuf[5, core, p] = chip_total(3, p).astype(BF16)
-        back[p].start()
+    for s in seqs:
+        swaps[1][s].wait_recv()
+        gbuf[4, s, core] = chip_total(1, s).astype(BF16)
+        hiddens[s].start()
     received(sums)
     small[0:1] = (gains[0, 0] + gains[2, 0]) + (gains[1, 0] + gains[3, 0])
     small[1:2] = (gains[0, 1] + gains[2, 1]) + (gains[1, 1] + gains[3, 1])
     grads.small_start(small)
+    for s in seqs:
+        swaps[3][s].wait_recv()
+        gbuf[5, s, core] = chip_total(3, s).astype(BF16)
+        inners[s].start()
+    grads.mix_relay()
     grads.ffn_relay_second()
-    received(hidden)
-    spread(4, hid)
-    received(back)
-    spread(5, ing)
+    for s in seqs:
+        hiddens[s].wait_recv()
+        spread(4, s, hid)
+        inners[s].wait_recv()
+        spread(5, s, ing)
+    grads.small_relay()
     grads.mix_merge()
-    grads.small_relay()
     grads.ffn_finish()
+    grads.small_finish()
     grads.mix_relay_second()
-    grads.small_finish()
     grads.mix_finish()
-    sent(outs + out_swaps + firsts + swaps + sums + hidden + back)
+    for ph in range(4):
+        sent(firsts[ph] + swaps[ph])
+    sent(sums + middles + backs + hiddens + inners)
     grads.sent()
 
 
@@ -875,7 +931,7 @@
     ]
     rows = (2, ROWS, 1024)
     buffers = [
-        pltpu.VMEM((tokens, n), BF16) for n in (1024, PEND, 1024, 2 * FPAD, 1024, 512, 1024, FPAD)
+        pltpu.VMEM((tokens, n), BF16) for n in (1024, PEND, 1024, PAIR, 1024, 512, 1024, FPAD)
     ] + [pltpu.VMEM((8, 1024), F32)] + [pltpu.VMEM((4, 4, ROWS, 256), BF16)] * 4 + [
         pltpu.VMEM((4, 2) + rows, BF16),
         pltpu.VMEM((4,) + rows, BF16),
@@ -902,6 +958,7 @@
         pltpu.VMEM((6, 4, LEN, LEN), F32),
         pltpu.VMEM((4, 2, 1, 1024), F32),
         pltpu.VMEM((2, 1, 1024), F32),
+        pltpu.VMEM((2, 1, 1024), F32),
     ]
     sems = [
         pltpu.SemaphoreType.DMA((4, 2)), pltpu.SemaphoreType.DMA((4, 2)),

time: 147 us -> 134 us (0.912)
  Pallas kernels: 146 us -> 133 us
    pallas_call x1, Pallas kernels: 143 us -> 130 us  [run_layer(): pl.pallas_call(layer_kernel, out_shape=[jax.ShapeDtypeStruct(s, d) for s,...]
where the time goes in v4:
time: 134 us
  Pallas kernels  133 us (99%)
    pallas_call x1, Pallas kernels, run_layer(): pl.pallas_call(layer_kernel, out_shape=[jax.ShapeDtypeStruct(s, d) for s,...  130 us
    pallas_call x1, Pallas kernels, run_results(): pl.pallas_call(result_kernel, out_shape=[jax.ShapeDtypeStruct(s, d) for s...  2.97 us

profile of v4, /device:TPU:0, one launch (start us, length us, event | category | flops | bytes accessed | tf_op | source)
XLA Modules:
  0.0 134.0 jit_solution(3118164798524313304)
XLA Ops:
  0.7 130.2 %layer.1 = (bf16[256,1024]{1,0:T(8,128)(2,1)}, bf16[256,1024]{1,0:T(8,128)(2,1)}, f32[64,256]{1,0:T(8,128)}, f32[64,256]{1,0:T(8,128)}, f32[64,512]{1,0:T(8,128)...) custom-call(bf16[256,1024]{1,0:T(8,128)(2,1)} %bitcast.56, ...), custom_call_target="tpu_custom_call" | custom-call | tf_op jit(solution)/shard_map/layer/pallas_call | solution.py:970
  130.9 3.0 %results.1 = (bf16[256,1024]{1,0:T(8,128)(2,1)}, bf16[256,1024]{1,0:T(8,128)(2,1)}, f32[64,256]{1,0:T(8,128)}, f32[64,256]{1,0:T(8,128)}, f32[64,512]{1,0:T(8,12...) custom-call(bf16[256,1024]{1,0:T(8,128)(2,1)} %get-tuple-element.53., ...), custom_call_target="tpu_custom_call" | custom-call | tf_op jit(solution)/shard_map/results/pallas_call | solution.py:1006

commit v5 on v4

--- a/solution.py
+++ b/solution.py
@@ -20,8 +20,8 @@
 PAIR = 2 * FF
 NF = 1152
 NG = PAIR - NF + FPAD
-NQ = PV + 512
-NV = PEND - PV
+NO = 512
+NV = 512 + PEND - PB
 
 
 def dot(left, right):
@@ -183,7 +183,8 @@
         )
 
 
-WIDTHS = (NF, NG, NQ, NV)
+FFN, GATE, MIX = (0, 1), (2, 3), (4, 5)
+WIDTHS = (NF, NG, NO, NO, PV, NV)
 
 
 def sum_scratch():
@@ -193,7 +194,7 @@
         scratch += [pltpu.VMEM((2, ROWS, n), BF16)] * 2 + [pltpu.VMEM((4, ROWS, n), BF16)] * 3
         scratch += [pltpu.VMEM((ROWS // 2, n), BF16)] * 2 + [pltpu.VMEM((ROWS, n), BF16)] * 2
     scratch += [pltpu.VMEM((4, 8, 1024), F32)] * 2
-    scratch += [pltpu.SemaphoreType.DMA((8, 6))] * 2 + [pltpu.SemaphoreType.DMA((6,))] * 2
+    scratch += [pltpu.SemaphoreType.DMA((12, 6))] * 2 + [pltpu.SemaphoreType.DMA((6,))] * 2
     return scratch
 
 
@@ -205,7 +206,7 @@
         ways = ((x, steps[:3]), (z, steps[3:]))
         self.sx, self.sz, send, recv, ssend, srecv = refs[-6:]
         self.first, self.second, self.half = [], [], []
-        for k in range(4):
+        for k in range(6):
             g, one_p, one_m, two_p, two_m, h, a, b, c, d = refs[10 * k : 10 * k + 10]
             me, way = ways[k % 2]
             self.first.append(
@@ -213,7 +214,7 @@
             )
             me, way = ways[1 - k % 2]
             self.second.append(
-                Ring(remote, h, me, way, (a, b, c, d), send.at[4 + k], recv.at[4 + k], ROWS // 2)
+                Ring(remote, h, me, way, (a, b, c, d), send.at[6 + k], recv.at[6 + k], ROWS // 2)
             )
         self.small_x = [
             remote(self.sx.at[0], self.sx.at[i + 1], ssend.at[i], srecv.at[i], steps[i])
@@ -248,10 +249,14 @@
             outer(data["a2"], data["pair"], NF, PAIR - NF, 0)
             outer(data["dy"], data["act"], 0, FPAD, PAIR - NF)
         elif k == 2:
+            outer(data["dh"], data["mix"], 0, NO, 0)
+        elif k == 3:
+            outer(data["a1"], data["proj"], PG, NO, 0)
+        elif k == 4:
             outer(data["a1"], data["proj"], PQ, PV, 0)
-            outer(data["dh"], data["mix"], 0, 512, PV)
         else:
-            outer(data["a1"], data["proj"], PV, PEND - PV, 0)
+            outer(data["a1"], data["proj"], PV, PG - PV, 0)
+            outer(data["a1"], data["proj"], PB, PEND - PB, PG - PV)
 
     def begin(self, groups):
         for step in range(3):
@@ -269,19 +274,13 @@
             self.first[k].merge(self.second[k].g)
             self.second[k].start()
 
-    def ffn_start(self):
-        self.begin((0, 1))
-
-    def ffn_relay(self):
-        self.first[0].relay()
-        self.first[1].relay()
-
-    def ffn_merge(self):
-        self.merge((0, 1))
-
-    def ffn_relay_second(self):
-        self.second[0].relay()
-        self.second[1].relay()
+    def relay(self, groups):
+        for k in groups:
+            self.first[k].relay()
+
+    def relay_second(self, groups):
+        for k in groups:
+            self.second[k].relay()
 
     def ffn_finish(self):
         one, two, outs = self.second[0], self.second[1], self.outs
@@ -292,30 +291,21 @@
         outs["fu"][:, NF - FF : FF] = two.total(0, PAIR - NF)
         outs["fd"][...] = two.total(PAIR - NF, FPAD)[:, 0:FF]
 
-    def mix_start(self):
-        self.begin((2, 3))
-
-    def mix_relay(self):
-        self.first[2].relay()
-        self.first[3].relay()
-
-    def mix_merge(self):
-        self.merge((2, 3))
-
-    def mix_relay_second(self):
-        self.second[2].relay()
-        self.second[3].relay()
+    def gate_finish(self):
+        one, two, outs = self.second[2], self.second[3], self.outs
+        one.arrive()
+        outs["out"][...] = one.total(0, NO)
+        two.arrive()
+        outs["go"][...] = two.total(0, NO)
 
     def mix_finish(self):
-        one, two, outs = self.second[2], self.second[3], self.outs
+        one, two, outs = self.second[4], self.second[5], self.outs
         one.arrive()
         outs["q"][...] = one.total(0, 256)
         outs["k"][...] = one.total(256, 256)
-        outs["out"][...] = one.total(PV, 512)
         two.arrive()
         outs["v"][...] = two.total(0, 512)
-        outs["go"][...] = two.total(512, 512)
-        both = two.total(1024, PEND - PB).T
+        both = two.total(512, PEND - PB).T
         outs["b"][...] = both[0:2]
         outs["d"][...] = both[2:4]
 
@@ -346,8 +336,10 @@
 
 
 def layer_kernel(
-    inp, cot, g1, wq, wk, wv, cvq, cvk, cvv, wb, wd, lrate, sbias, ogain, wgo, wo, g2, wfg, wfu, wfd,
+    inp, cot, g1, cvq, cvk, cvv, wb, wd, lrate, sbias, ogain, g2,
+    hq, hk, hval, hgo, ho, hfg, hfu, hfd,
     hid, ing, gq, gk, gv, gb, gd, ggo, gout, gfg, gfu, gfd, gsmall,
+    wq, wk, wv, wgo, wo, wfg, wfu, wfd, w_s,
     a1, dpr, a2, dgu, dho, mix, dyo, act, small, a1t, a2t, dht, dyt,
     part, r1, r2, fwd, hopb, gbuf, xrow, hrow, drow,
     proj, zsum, qkv, gpre, onorm, upg, upu, dact,
@@ -370,6 +362,12 @@
             device_id=device, device_id_type=MESH,
         )
 
+    stored = (hq, hk, hval, hgo, ho, hfg, hfu, hfd)
+    held = (wq, wk, wv, wgo, wo, wfg, wfu, wfd)
+    loads = [pltpu.make_async_copy(a, b, w_s.at[i]) for i, (a, b) in enumerate(zip(stored, held))]
+    for i in (0, 1, 2, 3, 4, 7, 5, 6):
+        loads[i].start()
+
     barrier = pltpu.get_barrier_semaphore()
     for step in range(1, 4):
         pl.semaphore_signal(
@@ -384,7 +382,9 @@
     links = torus_steps(place)
     for device in links:
         pl.semaphore_signal(barrier, inc=1, device_id=device, device_id_type=MESH)
-    pl.semaphore_wait(barrier, 7 + len(links))
+
+    def all_entered():
+        pl.semaphore_wait(barrier, 7 + len(links))
 
     grads = Sums(
         place, remote,
@@ -764,14 +764,18 @@
     @pl.when(section == 1)
     def _():
         dyo[...] = cot[...]
+        turned(dyo, dyt)
+        loads[7].wait()
         dact[...] = dot_nt(cot[...], wfd[...])
-        turned(dyo, dyt)
+        all_entered()
 
     def take_input(s, value):
         x = value.astype(F32)
         xrow[piece(s)] = x
         return normed(x, gain1)
 
+    for load in loads[:5]:
+        load.wait()
     for s in seqs:
         @pl.when(section == 1)
         def _():
@@ -781,9 +785,14 @@
         if s == 1:
             swap(0, 0)
         mixer_outputs(s, systems)
+        if s == 0:
+            pl.when(section == 0)(all_entered)
         firsts[0][s].start()
     swap(0, 1)
 
+    for load in loads[5:7]:
+        load.wait()
+    pl.when(section == 0)(loads[7].wait)
     take_middle(0)
     ffn_inputs(0)
 
@@ -827,7 +836,7 @@
             ffn_back(s)
             swap(2, s)
         turned(dyo, dyt)
-        grads.ffn_start()
+        grads.begin(FFN)
 
     @pl.when(section == 1)
     def _():
@@ -844,7 +853,9 @@
 
     @pl.when(section == 0)
     def _():
-        grads.ffn_relay()
+        grads.relay(FFN)
+        turned(dho, dht)
+        grads.begin(GATE)
 
     @pl.when(section == 1)
     def _():
@@ -854,8 +865,7 @@
 
     @pl.when(section == 0)
     def _():
-        turned(dho, dht)
-        grads.mix_start()
+        grads.begin(MIX)
 
     layer_back(1)
     layer_back_sum(1)
@@ -866,13 +876,14 @@
         for s in seqs:
             ffn_outputs(s)
         turned(a2, a2t)
-        grads.ffn_start()
+        grads.begin(FFN)
         for s in seqs:
             ffn_output_sum(s)
         turned(a1, a1t)
         turned(dho, dht)
-        grads.ffn_relay()
-        grads.mix_start()
+        grads.begin(GATE)
+        grads.relay(FFN)
+        grads.begin(MIX)
         for s in seqs:
             sent(hop_send(3, 1, s))
         started(swaps[1])
@@ -888,11 +899,12 @@
         for step in range(1, 4)
     ]
     started(sums)
-    grads.ffn_merge()
     for s in seqs:
         swaps[1][s].wait_recv()
         gbuf[4, s, core] = chip_total(1, s).astype(BF16)
         hiddens[s].start()
+    grads.relay(GATE)
+    grads.merge(FFN)
     received(sums)
     small[0:1] = (gains[0, 0] + gains[2, 0]) + (gains[1, 0] + gains[3, 0])
     small[1:2] = (gains[0, 1] + gains[2, 1]) + (gains[1, 1] + gains[3, 1])
@@ -901,18 +913,21 @@
         swaps[3][s].wait_recv()
         gbuf[5, s, core] = chip_total(3, s).astype(BF16)
         inners[s].start()
-    grads.mix_relay()
-    grads.ffn_relay_second()
+    grads.relay(MIX)
+    grads.merge(GATE)
+    grads.relay_second(FFN)
     for s in seqs:
         hiddens[s].wait_recv()
         spread(4, s, hid)
         inners[s].wait_recv()
         spread(5, s, ing)
     grads.small_relay()
-    grads.mix_merge()
+    grads.merge(MIX)
+    grads.relay_second(GATE)
     grads.ffn_finish()
     grads.small_finish()
-    grads.mix_relay_second()
+    grads.relay_second(MIX)
+    grads.gate_finish()
     grads.mix_finish()
     for ph in range(4):
         sent(firsts[ph] + swaps[ph])
@@ -930,7 +945,8 @@
         )
     ]
     rows = (2, ROWS, 1024)
-    buffers = [
+    weights = args[12:]
+    buffers = [pltpu.VMEM(w.shape, w.dtype) for w in weights] + [pltpu.SemaphoreType.DMA((8,))] + [
         pltpu.VMEM((tokens, n), BF16) for n in (1024, PEND, 1024, PAIR, 1024, 512, 1024, FPAD)
     ] + [pltpu.VMEM((8, 1024), F32)] + [pltpu.VMEM((4, 4, ROWS, 256), BF16)] * 4 + [
         pltpu.VMEM((4, 2) + rows, BF16),
@@ -970,7 +986,8 @@
     return pl.pallas_call(
         layer_kernel,
         out_shape=[jax.ShapeDtypeStruct(s, d) for s, d in results],
-        in_specs=[pl.BlockSpec(memory_space=pltpu.VMEM)] * len(args),
+        in_specs=[pl.BlockSpec(memory_space=pltpu.VMEM)] * 12
+        + [pl.BlockSpec(memory_space=pl.ANY)] * len(weights),
         out_specs=[pl.BlockSpec(memory_space=pltpu.VMEM)] * len(results),
         scratch_shapes=buffers + sems + sum_scratch(),
         compiler_params=pltpu.CompilerParams(
@@ -1022,9 +1039,9 @@
     width = inputs.shape[-1]
     out = run_layer((
         inputs.reshape(tokens, width), cotangent.reshape(tokens, width),
-        norm_gain1, w_query[0], w_key[0], w_value[0],
-        conv_query[0], conv_key[0], conv_value[0], w_beta[0].T, w_decay[0].T,
-        log_rate, step_bias, out_gain, w_gate_out[0], w_out[0], norm_gain2,
+        norm_gain1, conv_query[0], conv_key[0], conv_value[0], w_beta[0].T, w_decay[0].T,
+        log_rate, step_bias, out_gain, norm_gain2,
+        w_query[0], w_key[0], w_value[0], w_gate_out[0], w_out[0],
         w_ffn_gate[0].T, w_ffn_up[0].T, w_ffn_down[0],
     ))
     (

time: 134 us -> 132 us (0.985)
  Pallas kernels: 133 us -> 131 us
    pallas_call x1, Pallas kernels: 130 us -> 128 us  [run_layer(): pl.pallas_call(layer_kernel, out_shape=[jax.ShapeDtypeStruct(s, d) for s,...]
where the time goes in v5:
time: 132 us
  Pallas kernels  131 us (99%)
    pallas_call x1, Pallas kernels, run_layer(): pl.pallas_call(layer_kernel, out_shape=[jax.ShapeDtypeStruct(s, d) for s,...  128 us
    pallas_call x1, Pallas kernels, run_results(): pl.pallas_call(result_kernel, out_shape=[jax.ShapeDtypeStruct(s, d) for s...  2.97 us

profile of v5, /device:TPU:0, one launch (start us, length us, event | category | flops | bytes accessed | tf_op | source)
XLA Modules:
  0.0 131.7 jit_solution(13851313279780884190)
XLA Ops:
  0.7 127.9 %layer.1 = (bf16[256,1024]{1,0:T(8,128)(2,1)}, bf16[256,1024]{1,0:T(8,128)(2,1)}, f32[64,256]{1,0:T(8,128)}, f32[64,256]{1,0:T(8,128)}, f32[64,512]{1,0:T(8,128)...) custom-call(bf16[256,1024]{1,0:T(8,128)(2,1)} %bitcast.56, ...), custom_call_target="tpu_custom_call" | custom-call | tf_op jit(solution)/shard_map/layer/pallas_call | solution.py:986
  128.6 3.0 %results.1 = (bf16[256,1024]{1,0:T(8,128)(2,1)}, bf16[256,1024]{1,0:T(8,128)(2,1)}, f32[64,256]{1,0:T(8,128)}, f32[64,256]{1,0:T(8,128)}, f32[64,512]{1,0:T(8,12...) custom-call(bf16[256,1024]{1,0:T(8,128)(2,1)} %get-tuple-element.53., ...), custom_call_target="tpu_custom_call" | custom-call | tf_op jit(solution)/shard_map/results/pallas_call | solution.py:1023

commit v6 on v5

--- a/solution.py
+++ b/solution.py
@@ -258,13 +258,15 @@
             outer(data["a1"], data["proj"], PV, PG - PV, 0)
             outer(data["a1"], data["proj"], PB, PEND - PB, PG - PV)
 
-    def begin(self, groups):
+    def begin(self, groups, after_first=None):
         for step in range(3):
             for k in groups:
                 at, copies = self.first[k].steps[step]
                 self.chunk(k, at)
                 for copy in copies:
                     copy.start()
+            if step == 0 and after_first is not None:
+                after_first()
         for k in groups:
             self.chunk(k, self.first[k].me)
 
@@ -834,9 +836,10 @@
             hop_receive(1, 2, s, take_cotangent, dyo)
             dact[seq(s)] = dot_nt(dyo[seq(s)], wfd[...])
             ffn_back(s)
-            swap(2, s)
+            if s == 0:
+                swap(2, 0)
         turned(dyo, dyt)
-        grads.begin(FFN)
+        grads.begin(FFN, lambda: swap(2, 1))
 
     @pl.when(section == 1)
     def _():
@@ -853,9 +856,9 @@
 
     @pl.when(section == 0)
     def _():
-        grads.relay(FFN)
         turned(dho, dht)
         grads.begin(GATE)
+        grads.relay(FFN)
 
     @pl.when(section == 1)
     def _():
@@ -998,11 +1001,16 @@
 
 
 def result_kernel(*refs):
-    hid, ing, gq, gk, gv, gb, gd, ggo, gout, gfg, gfu, gfd, sums = refs[:13]
-    outs = refs[13:]
-    dg1, dcq, dck, dcv, dlr, dsb, dog, dg2 = outs[12:]
-    for source, out in zip((hid, ing, gq, gk, gv, gb, gd, ggo, gout, gfg, gfu, gfd), outs):
-        out[...] = source[...]
+    gb, gd, sums = refs[10:13]
+    large = refs[13:23]
+    ogb, ogd, dg1, dcq, dck, dcv, dlr, dsb, dog, dg2, sems = refs[23:]
+    copies = [
+        pltpu.make_async_copy(a, b, sems.at[i]) for i, (a, b) in enumerate(zip(refs[:10], large))
+    ]
+    for copy in copies:
+        copy.start()
+    ogb[...] = gb[...]
+    ogd[...] = gd[...]
     dg1[...] = sums[0:1]
     dg2[...] = sums[1:2]
     dcq[...] = sums[2:6, 0:256]
@@ -1011,23 +1019,27 @@
     dog[...] = sums[6:7, 0:512]
     dlr[...] = sums[6:7, 512:514]
     dsb[...] = sums[6:7, 514:516]
-
-
-def run_results(args):
-    results = [(v.shape, v.dtype) for v in args[:12]] + [
+    for copy in copies:
+        copy.wait()
+
+
+def run_results(large, small):
+    results = [(v.shape, v.dtype) for v in large + small[:2]] + [
         (shape, F32)
         for shape in (
             (1, 1024), (4, 256), (4, 256), (4, 512), (1, 2), (1, 2), (1, 512), (1, 1024)
         )
     ]
+    far = [pl.BlockSpec(memory_space=pl.ANY)] * len(large)
     return pl.pallas_call(
         result_kernel,
         out_shape=[jax.ShapeDtypeStruct(s, d) for s, d in results],
-        in_specs=[pl.BlockSpec(memory_space=pltpu.VMEM)] * len(args),
-        out_specs=[pl.BlockSpec(memory_space=pltpu.VMEM)] * len(results),
+        in_specs=far + [pl.BlockSpec(memory_space=pltpu.VMEM)] * len(small),
+        out_specs=far + [pl.BlockSpec(memory_space=pltpu.VMEM)] * (len(results) - len(large)),
+        scratch_shapes=[pltpu.SemaphoreType.DMA((len(large),))],
         compiler_params=pltpu.CompilerParams(vmem_limit_bytes=60 * 1024 * 1024),
         name="results",
-    )(*args)
+    )(*large, *small)
 
 
 def per_device(
@@ -1044,10 +1056,13 @@
         w_query[0], w_key[0], w_value[0], w_gate_out[0], w_out[0],
         w_ffn_gate[0].T, w_ffn_up[0].T, w_ffn_down[0],
     ))
+    hidden, input_grad, gq, gk, gv, gb, gd, ggo, gout, gfg, gfu, gfd, sums = out
     (
-        hidden, input_grad, gq, gk, gv, gb, gd, ggo, gout, gfg, gfu, gfd,
+        hidden, input_grad, gq, gk, gv, ggo, gout, gfg, gfu, gfd, gb, gd,
         dg1, dcq, dck, dcv, dlr, dsb, dog, dg2,
-    ) = run_results(tuple(out))
+    ) = run_results(
+        (hidden, input_grad, gq, gk, gv, ggo, gout, gfg, gfu, gfd), (gb, gd, sums)
+    )
     shape = (1,) + inputs.shape
     return (
         hidden.reshape(shape), input_grad.reshape(shape), dg1, gq[None], gk[None], gv[None],

time: 132 us -> 196 us (1.48)
  Pallas kernels: 131 us -> 195 us
    pallas_call x1, Pallas kernels: 2.97 us -> 68.2 us  [run_results(): pl.pallas_call(result_kernel, out_shape=[jax.ShapeDtypeStruct(s, d) for s...]
where the time goes in v6:
time: 196 us
  Pallas kernels  195 us (99%)
    pallas_call x1, Pallas kernels, run_layer(): pl.pallas_call(layer_kernel, out_shape=[jax.ShapeDtypeStruct(s, d) for s,...  127 us
    pallas_call x1, Pallas kernels, run_results(): pl.pallas_call(result_kernel, out_shape=[jax.ShapeDtypeStruct(s, d) for s...  68.2 us

profile of v6, /device:TPU:0, one launch (start us, length us, event | category | flops | bytes accessed | tf_op | source)
XLA Modules:
  0.0 195.7 jit_solution(14501611514182459578)
XLA Ops:
  0.7 126.7 %layer.1 = (bf16[256,1024]{1,0:T(8,128)(2,1)}, bf16[256,1024]{1,0:T(8,128)(2,1)}, f32[64,256]{1,0:T(8,128)}, f32[64,256]{1,0:T(8,128)}, f32[64,512]{1,0:T(8,128)...) custom-call(bf16[256,1024]{1,0:T(8,128)(2,1)} %bitcast.56, ...), custom_call_target="tpu_custom_call" | custom-call | tf_op jit(solution)/shard_map/layer/pallas_call | solution.py:989
  127.4 68.2 %results.1 = (bf16[256,1024]{1,0:T(8,128)(2,1)}, bf16[256,1024]{1,0:T(8,128)(2,1)}, f32[64,256]{1,0:T(8,128)}, f32[64,256]{1,0:T(8,128)}, f32[64,512]{1,0:T(8,12...) custom-call(bf16[256,1024]{1,0:T(8,128)(2,1)} %get-tuple-element.53., ...), custom_call_target="tpu_custom_call" | custom-call | tf_op jit(solution)/shard_map/results/pallas_call | solution.py:1034
